TPU v7x, 32 devices: a whole 2x2x4 slice. The times are simulated.
32 devices in a mesh: prow: 4 (over y, x), pcol: 8 (over z, core).
Axes of the slice: x: 2, y: 2, z: 4, core: 2. Of those that a mesh axis runs over, the one named last changes fastest.
Arguments:
- top_inverse: bfloat16 [8, 8, 256, 256], P('pcol'), may hold values from -3 to 3
- upper_structure: int32 [4, 8], replicated, may hold values from 0 to 1, as said below
- upper_panels: bfloat16 [4, 8, 256, 256], P('prow', 'pcol'), may hold values from -0.375 to 0.375
- upper_diag_inverse: float32 [4, 256, 256], P('prow'), may hold values from -6 to 6
- child_order: int32 [8], replicated, may hold values from 0 to 7, each once
- child_keep: int32 [8, 8], P('prow'), may hold values 0 or 1
- lower_panels: bfloat16 [8, 8, 256, 256], P('prow', 'pcol'), may hold values from -0.25 to 0.25
- parent_panels: bfloat16 [8, 256, 256], P('prow'), may hold values from -0.1875 to 0.1875
- lower_diag_inverse: float32 [8, 256, 256], P('prow'), may hold values from -6 to 6
Outputs:
- upper_blocks: bfloat16 [4, 8, 256, 256], P('prow', 'pcol')
- upper_diag: float32 [4, 256, 256], P('prow')
- lower_blocks: bfloat16 [8, 8, 256, 256], P('prow', 'pcol')
- lower_parent: bfloat16 [8, 256, 256], P('prow')
- lower_diag: float32 [8, 256, 256], P('prow')
Inputs may be any that keep to these rules, and one draw needn't show every extreme that they name: `upper_structure`: 1 where top-separator supernode I lies in the block structure of upper-level supernode K, else 0. `child_order`: each number once; lower-level supernode k is a child of upper-level supernode child_order[k] // 2, so every upper-level supernode has exactly 2 children. `child_keep`: 1 where a lower-level supernode keeps a block of its parent's structure.
All inputs are finite; a program needn't handle non-finite values.
Results may differ from a plain program's by a relative error of at most 0.0049.
Values may be sent and summed in bfloat16 or wider, within the bound.
No kernel may reach another device: no remote copies, remote signals or barrier semaphores. Data moves between devices by JAX's collectives and lax.ppermute only.
A program may use at most 128 MiB of HBM per device.

v0:
```python
import jax
import jax.numpy as jnp
from jax import lax
from jax.sharding import PartitionSpec as P

CH = 2


def dense_sum(top_rows, piece):
    return jnp.einsum("isd,kide->kse", top_rows, piece, preferred_element_type=jnp.float32)


def shards(
    top_inverse,
    upper_structure,
    upper_panels,
    upper_diag_inverse,
    child_order,
    child_keep,
    lower_panels,
    parent_panels,
    lower_diag_inverse,
):
    row_index = lax.axis_index("prow")
    col_index = lax.axis_index("pcol")
    upper_count = upper_panels.shape[0]
    lower_count = lower_panels.shape[0]
    top_rows = top_inverse[0]
    upper_rows = lax.dynamic_slice_in_dim(upper_structure, row_index * upper_count, upper_count, 0)
    upper_flags = lax.dynamic_index_in_dim(upper_rows, col_index, 1, keepdims=False)
    upper_own = upper_panels[:, 0] * upper_flags[:, None, None].astype(jnp.bfloat16)
    order_rows = lax.dynamic_slice_in_dim(child_order, row_index * lower_count, lower_count, 0)
    parent = order_rows // CH
    lower_structure = jnp.take(upper_structure, parent, axis=0) * child_keep
    lower_flags = lax.dynamic_index_in_dim(lower_structure, col_index, 1, keepdims=False)
    lower_own = lower_panels[:, 0] * lower_flags[:, None, None].astype(jnp.bfloat16)
    upper_sum = dense_sum(top_rows, lax.all_gather(upper_own[:, None], "pcol", axis=1, tiled=True))
    upper_local = (-(upper_flags[:, None, None].astype(jnp.float32) * upper_sum)).astype(
        jnp.bfloat16
    )
    diag_term = jnp.einsum(
        "kds,kde->kse", upper_panels[:, 0], upper_local, preferred_element_type=jnp.float32
    )
    own_share = (
        jnp.where(col_index == 0, upper_diag_inverse, jnp.zeros_like(upper_diag_inverse))
        - diag_term
    )
    upper_diag = lax.psum(own_share, "pcol")
    diag_every = lax.all_gather(upper_diag, "prow", axis=0, tiled=True)
    upper_every = lax.all_gather(upper_local, "prow", axis=0, tiled=True)
    lower_sum = dense_sum(top_rows, lax.all_gather(lower_own[:, None], "pcol", axis=1, tiled=True))
    parent_rows = jnp.take(upper_every, parent, axis=0)
    parent_diag = jnp.take(diag_every, parent, axis=0)
    through_parent = jnp.einsum(
        "ksd,kde->kse", parent_rows, parent_panels, preferred_element_type=jnp.float32
    )
    lower_local = (
        -(lower_flags[:, None, None].astype(jnp.float32) * (through_parent + lower_sum))
    ).astype(jnp.bfloat16)
    cross_term = jnp.einsum(
        "kds,kde->kse", parent_rows, lower_own, preferred_element_type=jnp.float32
    )
    lower_term = jnp.einsum(
        "kds,kde->kse", lower_panels[:, 0], lower_local, preferred_element_type=jnp.float32
    )
    cross, lower_total = lax.psum((cross_term, lower_term), "pcol")
    parent_part = jnp.einsum(
        "ksd,kde->kse",
        parent_diag,
        parent_panels.astype(jnp.float32),
        precision=lax.Precision.HIGHEST,
    )
    lower_parent = (-(parent_part + cross)).astype(jnp.bfloat16)
    lower_diag = (
        lower_diag_inverse
        - jnp.einsum(
            "kds,kde->kse", parent_panels, lower_parent, preferred_element_type=jnp.float32
        )
        - lower_total
    )
    return (upper_local[:, None], upper_diag, lower_local[:, None], lower_parent, lower_diag)


def solution(mesh):
    in_specs = (
        P("pcol", None, None, None),
        P(),
        P("prow", "pcol", None, None),
        P("prow", None, None),
        P(),
        P("prow", None),
        P("prow", "pcol", None, None),
        P("prow", None, None),
        P("prow", None, None),
    )
    out_specs = (
        P("prow", "pcol", None, None),
        P("prow", None, None),
        P("prow", "pcol", None, None),
        P("prow", None, None),
        P("prow", None, None),
    )
    return jax.shard_map(shards, mesh=mesh, in_specs=in_specs, out_specs=out_specs, check_vma=False)
```

profile of v0, /device:TPU:0, one launch (start us, length us, event | category | flops | bytes accessed | tf_op | source)
XLA Modules:
  0.0 169.6 jit_solution(16752283277493487608)
XLA Ops:
  7.2 1.3 dynamic_slice.12
  9.2 1.6 bitcast_multiply_fusion.2
  10.8 0.0 all-gather.6.cloned.1.call-start
  10.9 0.7 compare_and_fusion
  11.7 1.2 gather_fusion
  12.9 0.8 select_multiply_fusion
  13.7 0.2 fusion.22
  13.8 1.1 copy.44
  14.9 0.8 broadcast_multiply_fusion
  15.7 0.0 all-reduce.3.cloned.1.call-start
  16.4 0.2 convert_reduce_fusion
  16.6 1.1 copy.42
  17.8 18.0 %all-gather.4.cloned.1.call-done = bf16[1,8,256,256]{3,2,0,1:T(8,128)(2,1)} async-done(((bf16[1,1,256,256]{3,2,0,1:T(8,128)(2,1)}), bf16[1,8,256,256]{3,2,0,1:T(8,128)(2,1)}) %all-gather.4.cloned.1.call-update) | async-done | bytes 1048592 | tf_op jit(solution)/shard_map/all_gather | solution.py:37
  35.8 1.8 %fusion.10 = bf16[256,256]{1,0:T(8,128)(2,1)S(1)} fusion(bf16[1,8,256,256]{3,2,0,1:T(8,128)(2,1)} %all-gather.4.cloned.1.call-done, bf16[1,8,256,256]{3,2,1,0:T(8,128)(2,1)S(1)} %copy-done, f32[]{:T(128)} %bitcast), kind=kOutput, calls=%fused_computation.20 | convolution fusion | flops 268632064 | bytes 2228228 | tf_op jit(solution)/shard_map/isd,kide->kse/dot_general | solution.py:10
  37.6 0.1 copy.43
  37.7 10.0 %all_gather.13 = bf16[4,256,256]{2,1,0:T(8,128)(2,1)S(1)} all-gather(bf16[1,256,256]{2,1,0:T(8,128)(2,1)S(1)} %copy.43), channel_id=1, replica_groups=mesh['prow'=4,'pcol'=8] {'prow'}, dimensions={0}, use_global_device_ids=true | all-gather | bytes 655360 | tf_op jit(solution)/shard_map/all_gather | solution.py:50
  47.7 0.6 gather_fusion.1
  48.2 0.9 fusion.9
  49.1 1.1 fusion.16
  50.3 16.4 %all-gather.6.cloned.1.call-done = bf16[2,8,256,256]{2,3,1,0:T(8,128)(2,1)} async-done(((bf16[2,1,256,256]{2,3,1,0:T(8,128)(2,1)}), bf16[2,8,256,256]{2,3,1,0:T(8,128)(2,1)}) %all-gather.6.cloned.1.call-update) | async-done | bytes 2097168 | tf_op jit(solution)/shard_map/all_gather | solution.py:51
  66.7 2.3 %convolution_bitcast_fusion.2 = f32[2,256,256]{2,1,0:T(8,128)S(1)} fusion(bf16[2,8,256,256]{2,3,1,0:T(8,128)(2,1)} %all-gather.6.cloned.1.call-done, bf16[1,8,256,256]{3,2,1,0:T(8,128)(2,1)S(1)} %copy-done), kind=kOutput, calls=%fused_computation.5 | convolution fusion | flops 536870912 | bytes 3670016 | tf_op jit(solution)/shard_map/isd,kide->kse/dot_general | solution.py:10
  69.1 0.3 fusion.6
  69.4 1.1 convolution_bitcast_fusion
  70.5 59.9 %all-reduce.3.cloned.1.call-done = (f32[1,256,256]{1,2,0:T(8,128)}, f32[2,256,256]{2,1,0:T(8,128)}, f32[2,256,256]{1,2,0:T(8,128)}) async-done(((f32[1,256,256]{1,2,0:T(8,128)}, f32[2,256,256]{2,1,0:T(8,128)}, f32[2,256,256]{1,2,0:T(8,128)}), (f32[1,256,256]{1,2,0:T(8,128)}, f32[2,256,256]{2,1,0:T(8,128)}, f32[2,256,256]{1,2,0:T(8,128)})) %all-reduce.3.cloned.1.call-update) | async-done | bytes 1310736 | tf_op jit(solution)/shard_map/psum | solution.py:48
  130.5 1.8 %copy.52 = f32[1,256,256]{2,1,0:T(8,128)} copy(f32[1,256,256]{1,2,0:T(8,128)} %get-tuple-element.20) | data formatting | bytes 524288
  132.3 0.2 copy.49
  132.6 0.8 copy.51
  133.3 25.0 %all-gather.8.cloned.1.call-done = f32[4,256,256]{2,1,0:T(8,128)} async-done(((f32[1,256,256]{2,1,0:T(8,128)}), f32[4,256,256]{2,1,0:T(8,128)}) %all-gather.8.cloned.1.call-update) | async-done | bytes 1048592 | tf_op jit(solution)/shard_map/all_gather | solution.py:49
  158.4 1.8 %gather_fusion.2 = f32[2,256,256]{2,1,0:T(8,128)S(1)} fusion(f32[4,256,256]{2,1,0:T(8,128)} %all-gather.8.cloned.1.call-done, s32[1024]{0:T(1024)S(1)} %pad_clamp_fusion), kind=kCustom, calls=%fused_computation.2 | custom fusion | bytes 1048584 | tf_op jit(solution)/shard_map/jit(_take)/gather | solution.py:53
  160.2 0.5 fusion.5
  160.7 1.4 fusion.1
  162.1 1.0 copy.54
  (23 shorter events, 0.2 us)
Async XLA Ops:
  7.2 28.6 %copy-start = (bf16[1,8,256,256]{3,2,1,0:T(8,128)(2,1)S(1)}, bf16[1,8,256,256]{3,2,1,0:T(8,128)(2,1)}, u32[]{:S(2)}) copy-start(bf16[1,8,256,256]{3,2,1,0:T(8,128)(2,1)} %param.9) | copy-start | bytes 3145732
  7.2 28.6 %all-gather.4.cloned.1.call-start = ((), (), s32[]{:S(2)}) async-start(), calls=%async_computation | async-start | bytes 1179648 | tf_op jit(solution)/shard_map/all_gather | solution.py:37
  10.8 55.9 %all-gather.6.cloned.1.call-start = ((), (), s32[]{:S(2)}) async-start(), calls=%async_computation.1 | async-start | bytes 2359296 | tf_op jit(solution)/shard_map/all_gather | solution.py:51
  15.7 114.7 %all-reduce.3.cloned.1.call-start = ((), (), s32[]{:S(2)}) async-start(), calls=%async_computation.3 | async-start | bytes 2621440 | tf_op jit(solution)/shard_map/psum | solution.py:48
  16.6 31.6 %copy-start.7 = (bf16[1,1,256,256]{3,2,1,0:T(8,128)(2,1)S(1)}, bf16[1,1,256,256]{3,2,1,0:T(8,128)(2,1)}, u32[]{:S(2)}) copy-start(bf16[1,1,256,256]{3,2,1,0:T(8,128)(2,1)} %param.11) | copy-start | bytes 393220
  35.8 13.3 %copy-start.1 = (bf16[2,1,256,256]{3,2,1,0:T(8,128)(2,1)S(1)}, bf16[2,1,256,256]{3,2,1,0:T(8,128)(2,1)}, u32[]{:S(2)}) copy-start(bf16[2,1,256,256]{3,2,1,0:T(8,128)(2,1)} %param.15) | copy-start | bytes 786436
  50.3 18.8 %copy-start.2 = (bf16[2,256,256]{2,1,0:T(8,128)(2,1)S(1)}, bf16[2,256,256]{2,1,0:T(8,128)(2,1)}, u32[]{:S(2)}) copy-start(bf16[2,256,256]{2,1,0:T(8,128)(2,1)} %param.16) | copy-start | bytes 786436
  69.1 63.3 %copy-start.5 = (f32[2,256,256]{2,1,0:T(8,128)S(1)}, f32[2,256,256]{2,1,0:T(8,128)}, u32[]{:S(2)}) copy-start(f32[2,256,256]{2,1,0:T(8,128)} %param.17) | copy-start | bytes 1572868
  69.4 63.2 %copy-start.3 = (bf16[2,256,256]{2,1,0:T(8,128)(2,1)}, bf16[2,256,256]{2,1,0:T(8,128)(2,1)S(1)}, u32[]{:S(2)}) copy-start(bf16[2,256,256]{2,1,0:T(8,128)(2,1)S(1)} %fusion.6) | copy-start | bytes 786436
  70.5 87.9 %all-gather.8.cloned.1.call-start = ((), (), s32[]{:S(2)}) async-start(), calls=%async_computation.2 | async-start | bytes 1310720 | tf_op jit(solution)/shard_map/all_gather | solution.py:49
  130.5 29.7 %copy-start.6 = (f32[2,256,256]{2,1,0:T(8,128)S(1)}, f32[2,256,256]{2,1,0:T(8,128)}, u32[]{:S(2)}) copy-start(f32[2,256,256]{2,1,0:T(8,128)} %get-tuple-element.21) | copy-start | bytes 1572868
  160.6 2.4 %copy-start.4 = (bf16[2,256,256]{2,1,0:T(8,128)(2,1)}, bf16[2,256,256]{2,1,0:T(8,128)(2,1)S(1)}, u32[]{:S(2)}) copy-start(bf16[2,256,256]{2,1,0:T(8,128)(2,1)S(1)} %fusion.5) | copy-start | bytes 786436
Sparse Core Ops, SparseCore 0:
  11.0 24.7 all-gather.3
  38.0 28.7 all-gather.5
  70.6 59.8 all-reduce.2
  132.7 25.5 all-gather.7
where the time goes:
time: 170 us
  waiting for transfers between devices  120 us (71%)
  between operations  15.3 us (9%)
  local copies, waits for them, and re-layouts  11.1 us (7%)
  blocking collectives  10 us (6%)
  matrix products  9.34 us (5%)
  other arithmetic  4.24 us (2%)
    psum x1, waiting for transfers between devices, shards(): upper_diag = lax.psum(own_share, 'pcol')  59.9 us
    all_gather x1, waiting for transfers between devices, shards(): diag_every = lax.all_gather(upper_diag, 'prow', axis=0, tiled=True)  25 us
    all_gather x1, waiting for transfers between devices, shards(): lax.all_gather(upper_own[:, None], 'pcol', axis=1, tiled=True)  18 us
    all_gather x1, waiting for transfers between devices, shards(): lax.all_gather(lower_own[:, None], 'pcol', axis=1, tiled=True)  16.4 us
    all_gather x1, blocking collectives, shards(): upper_every = lax.all_gather(upper_local, 'prow', axis=0, tiled=True)  10 us
    unnamed x22, local copies, waits for them, and re-layouts  6.04 us
    dot_general x2, matrix products, dense_sum(): jnp.einsum('isd,kide->kse', top_rows, piece, preferred_element_type=jnp.f...  4.07 us
  transfers between devices with their start and end apart: 4, of which 4 were waited for; matrix products, arithmetic and copies ran while one was open for 7% of the time, Pallas kernels for 0%

commit v1 on v0

--- a/solution.py
+++ b/solution.py
@@ -1,16 +1,23 @@
+import functools
+
 import jax
 import jax.numpy as jnp
 from jax import lax
+from jax.experimental import pallas as pl
+from jax.experimental.pallas import tpu as pltpu
 from jax.sharding import PartitionSpec as P
 
 CH = 2
+CORES = 2
+BF = jnp.bfloat16
+F32 = jnp.float32
 
 
 def dense_sum(top_rows, piece):
     return jnp.einsum("isd,kide->kse", top_rows, piece, preferred_element_type=jnp.float32)
 
 
-def shards(
+def wide_shards(
     top_inverse,
     upper_structure,
     upper_panels,
@@ -81,6 +88,273 @@
     return (upper_local[:, None], upper_diag, lower_local[:, None], lower_parent, lower_diag)
 
 
+def dot(a, b):
+    return lax.dot_general(a, b, (((1,), (0,)), ((), ())), preferred_element_type=F32)
+
+
+def dot_t(a, b):
+    return lax.dot_general(a, b, (((0,), (0,)), ((), ())), preferred_element_type=F32)
+
+
+def place():
+    col = lax.axis_index("pcol")
+    return lax.axis_index("prow"), col // CORES, col % CORES
+
+
+def upper_body(nz, us_ref, to_ref, ts_ref, uo_ref, us_full_ref, d_ref, *refs):
+    stacks, (rx_ref, ud_ref, xs) = refs[:nz], refs[nz:]
+    row, z, c = place()
+    half = xs.shape[1]
+    quarter = xs.shape[0] // nz
+    acc = [None, None]
+    for s in range(nz):
+        for q in range(CORES):
+            i = CORES * (z ^ s) + (c if q == 0 else 1 - c)
+            flag = us_ref[row, i].astype(F32).astype(BF)
+            piece = stacks[s][q] * flag
+            for p, t_ref in enumerate((to_ref, ts_ref)):
+                prod = dot(t_ref[i], piece)
+                acc[p] = prod if acc[p] is None else acc[p] + prod
+    x = None
+    for p, u_ref in enumerate((uo_ref, us_full_ref)):
+        j = CORES * z + (c if p == 0 else 1 - c)
+        flag = us_ref[row, j].astype(F32)
+        block = (-(flag * acc[p])).astype(BF)
+        rx_ref[p] = block
+        prod = dot_t(u_ref[...], block)
+        x = prod if x is None else x + prod
+    xs[...] = -x
+    for s in range(nz):
+        ud_ref[s] = xs[pl.ds(pl.multiple_of((z ^ s) * quarter, quarter), quarter), :].astype(BF)
+    own = pl.ds(pl.multiple_of(z * quarter, quarter), quarter)
+    rows = d_ref[own, :]
+    xs[own, :] = xs[own, :] + jnp.where(c == 0, rows[:, :half], rows[:, half:])
+    rx_ref[CORES] = xs[...].astype(BF)
+
+
+def parent_body(nz, us_ref, co_ref, ck_ref, keep_ref, got_ref, pp_ref, lm_ref, lg_ref, ud_ref,
+                w_ref, rs_ref, a_ref):
+    row, z, c = place()
+    half = keep_ref.shape[2]
+    size = pp_ref.shape[1]
+    quarter = size // nz
+    mine = pl.ds(pl.multiple_of(c * half, half), half)
+    other = pl.ds(pl.multiple_of((1 - c) * half, half), half)
+    parent = co_ref[CORES * row + c] // CH
+    p_mine, p_other = pp_ref[c, mine, :], pp_ref[c, other, :]
+    a_ref[...] = dot(keep_ref[CORES], p_mine) + dot(got_ref[CORES], p_other)
+    for p, l_ref in enumerate((lm_ref, lg_ref)):
+        j = CORES * z + (c if p == 0 else 1 - c)
+        flag = (us_ref[parent, j] * ck_ref[c, j]).astype(F32).astype(BF)
+        k_half, g_half = keep_ref[p], got_ref[1 - p]
+        w_ref[p] = dot(k_half, p_mine) + dot(g_half, p_other)
+        masked = l_ref[...] * flag
+        a_ref[mine, :] = a_ref[mine, :] + dot_t(k_half, masked)
+        a_ref[other, :] = a_ref[other, :] + dot_t(g_half, masked)
+    for s in range(nz):
+        block = pl.ds(pl.multiple_of((z ^ s) * quarter, quarter), quarter)
+        rs_ref[s, :, :size] = a_ref[block, :].astype(BF)
+        rs_ref[s, :, size:] = ud_ref[s]
+
+
+def lower_body(nz, us_ref, co_ref, ck_ref, to_ref, ts_ref, w_ref, *refs):
+    stacks, (lo_ref, lg_ref, rs_ref, r_ref) = refs[:nz], refs[nz:]
+    row, z, c = place()
+    quarter = r_ref.shape[0] // nz
+    parent = co_ref[CORES * row + c] // CH
+    acc = [w_ref[0], w_ref[1]]
+    for s in range(nz):
+        for q in range(CORES):
+            i = CORES * (z ^ s) + (c if q == 0 else 1 - c)
+            flag = (us_ref[parent, i] * ck_ref[c, i]).astype(F32).astype(BF)
+            piece = stacks[s][q] * flag
+            for p, t_ref in enumerate((to_ref, ts_ref)):
+                acc[p] = acc[p] + dot(t_ref[i], piece)
+    total = None
+    for p, o_ref in enumerate((lo_ref, lg_ref)):
+        j = CORES * z + (c if p == 0 else 1 - c)
+        flag = (us_ref[parent, j] * ck_ref[c, j]).astype(F32)
+        block = (-(flag * acc[p])).astype(BF)
+        o_ref[...] = block
+        prod = dot_t(stacks[0][p], block)
+        total = prod if total is None else total + prod
+    r_ref[...] = total
+    for s in range(nz):
+        rs_ref[s] = r_ref[
+            pl.ds(pl.multiple_of((z ^ s) * quarter, quarter), quarter), :
+        ].astype(BF)
+
+
+def add_body(negate, *refs):
+    *parts, out_ref = refs
+    total = parts[0][0].astype(F32)
+    for part in parts[1:]:
+        total = total + part[...].astype(F32)
+    if negate:
+        out_ref[:, :negate] = (-total[:, :negate]).astype(BF)
+        out_ref[:, negate:] = total[:, negate:].astype(BF)
+    else:
+        out_ref[...] = total.astype(BF)
+
+
+def join_body(*refs):
+    *parts, out_ref = refs
+    _, z, _ = place()
+    for s, part in enumerate(parts):
+        quarter = part.shape[0]
+        out_ref[pl.ds(pl.multiple_of((z ^ s) * quarter, quarter), quarter), :] = part[...]
+
+
+def parent_out_body(own_ref, got_ref, d_ref, ld_ref, pp_ref, ud_ref, lp_ref, base_ref):
+    _, _, c = place()
+    size = pp_ref.shape[1]
+    half = size // CORES
+    first, second = own_ref[:, size:].astype(F32), got_ref[:, size:].astype(F32)
+    ud_ref[0, :, :half] = d_ref[0, :, :half] + jnp.where(c == 0, first, second)
+    ud_ref[0, :, half:] = d_ref[0, :, half:] + jnp.where(c == 0, second, first)
+    for k, ref in ((c, own_ref), (1 - c, got_ref)):
+        block = ref[:, :size]
+        lp_ref[k] = block
+        base_ref[k] = ld_ref[k] - dot_t(pp_ref[k], block)
+
+
+def lower_out_body(base_ref, own_ref, got_ref, ld_ref):
+    _, _, c = place()
+    ld_ref[c] = base_ref[c] - own_ref[...].astype(F32)
+    ld_ref[1 - c] = base_ref[1 - c] - got_ref[...].astype(F32)
+
+
+def near_shards(
+    rows,
+    cols,
+    top_inverse,
+    upper_structure,
+    upper_panels,
+    upper_diag_inverse,
+    child_order,
+    child_keep,
+    lower_panels,
+    parent_panels,
+    lower_diag_inverse,
+):
+    nz = cols // CORES
+    size = upper_panels.shape[-1]
+    half, quarter = size // CORES, size // nz
+    row, z, c = place()
+    first = c == 0
+
+    def over_core(x):
+        return lax.ppermute(x, "pcol", [(i, i ^ 1) for i in range(cols)])
+
+    def over_z(x, s):
+        return lax.ppermute(x, "pcol", [(i, i ^ (CORES * s)) for i in range(cols)])
+
+    def over_row(x, s):
+        return lax.ppermute(x, "prow", [(i, i ^ s) for i in range(rows)])
+
+    shape = jax.ShapeDtypeStruct
+    t_own = top_inverse[0]
+    u_own = upper_panels[0, 0]
+    l_all = lower_panels[:, 0]
+    d_own = upper_diag_inverse[0]
+    u_sib = over_core(u_own)
+    l_own = jnp.where(first, l_all[0], l_all[1])
+    l_sib = over_core(jnp.where(first, l_all[1], l_all[0]))
+    t_sib = over_core(t_own)
+    u_both = jnp.stack([u_own, u_sib])
+    u_stack = jnp.where(first, u_both[:, :, :half], u_both[:, :, half:])
+    l_stack = jnp.stack([l_own, l_sib])
+    u_all = [u_stack] + [over_z(u_stack, s) for s in range(1, nz)]
+    l_all = [l_stack] + [over_z(l_stack, s) for s in range(1, nz)]
+
+    vm = pl.BlockSpec(memory_space=pltpu.VMEM)
+    sm = pl.BlockSpec(memory_space=pltpu.SMEM)
+
+    def kernel(body, out, args, smem=0, scratch=()):
+        return pl.pallas_call(
+            body,
+            out_shape=out,
+            in_specs=[sm] * smem + [vm] * (len(args) - smem),
+            out_specs=jax.tree.map(lambda _: vm, out),
+            scratch_shapes=list(scratch),
+            compiler_params=pltpu.CompilerParams(vmem_limit_bytes=24 * 1024 * 1024),
+        )(*args)
+
+    rx, ud_part = kernel(
+        functools.partial(upper_body, nz),
+        (shape((CORES + 1, size, half), BF), shape((nz, quarter, half), BF)),
+        (upper_structure, t_own, t_sib, u_own, u_sib, d_own, *u_all),
+        smem=1,
+        scratch=[pltpu.VMEM((size, half), F32)],
+    )
+    ub_got = over_core(rx[1])
+    ub_own = rx[0]
+    upper_blocks = jnp.where(
+        first,
+        jnp.concatenate([ub_own, ub_got], axis=1),
+        jnp.concatenate([ub_got, ub_own], axis=1),
+    )[None, None]
+
+    rx_all = [rx] + [over_row(rx, s) for s in range(1, rows)]
+    parents = lax.dynamic_slice_in_dim(child_order, CORES * row, CORES) // CH
+
+    def pick(k):
+        index = jnp.where(k == 0, parents[0], parents[1]) ^ row
+        out = rx_all[0]
+        for s in range(1, rows):
+            out = jnp.where(index == s, rx_all[s], out)
+        return out
+
+    keep = pick(c)
+    got = over_core(pick(1 - c))
+    scalars = (upper_structure, child_order, child_keep)
+    w, rs1 = kernel(
+        functools.partial(parent_body, nz),
+        (shape((CORES, size, size), F32), shape((nz, quarter, size + half), BF)),
+        (*scalars, keep, got, parent_panels, l_own, l_sib, ud_part),
+        smem=3,
+        scratch=[pltpu.VMEM((size, size), F32)],
+    )
+    lb_own, lb_give, rs2 = kernel(
+        functools.partial(lower_body, nz),
+        (shape((size, size), BF), shape((size, size), BF), shape((nz, quarter, size), BF)),
+        (*scalars, t_own, t_sib, w, *l_all),
+        smem=3,
+        scratch=[pltpu.VMEM((size, size), F32)],
+    )
+    lb_got = over_core(lb_give)
+    lower_blocks = jnp.where(
+        first, jnp.stack([lb_own, lb_got]), jnp.stack([lb_got, lb_own])
+    )[:, None]
+
+    def reduce(parts, negate):
+        got = [over_z(parts[s], s) for s in range(1, nz)]
+        part = kernel(
+            functools.partial(add_body, negate), shape(parts.shape[1:], BF), (parts, *got)
+        )
+        every = [part] + [over_z(part, s) for s in range(1, nz)]
+        return kernel(join_body, shape((size, parts.shape[2]), BF), tuple(every))
+
+    total1 = reduce(rs1, size)
+    total1_got = over_core(total1)
+    upper_diag, lower_parent, base = kernel(
+        parent_out_body,
+        (
+            shape((1, size, size), F32),
+            shape((CORES, size, size), BF),
+            shape((CORES, size, size), F32),
+        ),
+        (total1, total1_got, upper_diag_inverse, lower_diag_inverse, parent_panels),
+    )
+    total2 = reduce(rs2, 0)
+    lower_diag = kernel(
+        lower_out_body,
+        shape((CORES, size, size), F32),
+        (base, total2, over_core(total2)),
+    )
+    return upper_blocks, upper_diag, lower_blocks, lower_parent, lower_diag
+
+
 def solution(mesh):
     in_specs = (
         P("pcol", None, None, None),
@@ -100,4 +374,6 @@
         P("prow", None, None),
         P("prow", None, None),
     )
-    return jax.shard_map(shards, mesh=mesh, in_specs=in_specs, out_specs=out_specs, check_vma=False)
+    rows, cols = mesh.shape["prow"], mesh.shape["pcol"]
+    body = functools.partial(near_shards, rows, cols) if cols <= 8 else wide_shards
+    return jax.shard_map(body, mesh=mesh, in_specs=in_specs, out_specs=out_specs, check_vma=False)

time: 170 us -> 86 us (0.51)
  waiting for transfers between devices: 120 us -> 33.8 us
  starting transfers between devices: 0.16 us -> 34.6 us
  between operations: 15.3 us -> 3.48 us
  blocking collectives: 10 us -> 0 us
  matrix products: 9.34 us -> 0 us
  local copies, waits for them, and re-layouts: 11.1 us -> 4.09 us
  Pallas kernels: 0 us -> 6.2 us
    psum x1 -> x0, waiting for transfers between devices: 59.9 us -> none  [shards(): upper_diag = lax.psum(own_share, 'pcol')]
    all_gather x3 -> x0, waiting for transfers between devices: 59.5 us -> none  [the longest x1 25 us: shards(): diag_every = lax.all_gather(upper_diag, 'prow', axis=0, tiled=True)]
    ppermute x0 -> x29, starting transfers between devices: none -> 34.6 us  [the longest x18 29.6 us: over_z(): return lax.ppermute(x, 'pcol', [(i, i ^ CORES * s) for i in range(cols)])]
    ppermute x0 -> x29, waiting for transfers between devices: none -> 33.8 us  [the longest x18 29.7 us: over_z(): return lax.ppermute(x, 'pcol', [(i, i ^ CORES * s) for i in range(cols)])]
    all_gather x1 -> x0, blocking collectives: 10 us -> none  [shards(): upper_every = lax.all_gather(upper_local, 'prow', axis=0, tiled=True)]
    dot_general x8 -> x0, matrix products: 9.34 us -> none  [the longest x2 4.07 us: dense_sum(): jnp.einsum('isd,kide->kse', top_rows, piece, preferred_element_type=jnp.f...]
    pallas_call x0 -> x9, Pallas kernels: none -> 6.2 us  [kernel(): pl.pallas_call(body, out_shape=out, in_specs=[sm] * smem + [vm] * (len(ar...]
    gather x3 -> x0, local copies, waits for them, and re-layouts: 3.61 us -> none  [the longest x1 1.8 us: shards(): parent_diag = jnp.take(diag_every, parent, axis=0)]
  transfers between devices with their start and end apart: 4 -> 29, of which waited for: 4 -> 9; matrix products, arithmetic and copies ran while one was open for 7% -> 5% of each run, Pallas kernels for 0% -> 4%
where the time goes in v1:
time: 86 us; the launch traced here: 85.6 us
  starting transfers between devices  34.6 us (40%)
  waiting for transfers between devices  33.8 us (39%)
  Pallas kernels  6.2 us (7%)
  local copies, waits for them, and re-layouts  4.09 us (5%)
  other arithmetic  3.49 us (4%)
  between operations  3.48 us (4%)
    ppermute x18, waiting for transfers between devices, over_z(): return lax.ppermute(x, 'pcol', [(i, i ^ CORES * s) for i in range(cols)])  29.7 us
    ppermute x18, starting transfers between devices, over_z(): return lax.ppermute(x, 'pcol', [(i, i ^ CORES * s) for i in range(cols)])  29.6 us
    pallas_call x9, Pallas kernels, kernel(): pl.pallas_call(body, out_shape=out, in_specs=[sm] * smem + [vm] * (len(ar...  6.2 us
    ppermute x8, waiting for transfers between devices, over_core(): return lax.ppermute(x, 'pcol', [(i, i ^ 1) for i in range(cols)])  4.05 us
    ppermute x3, starting transfers between devices, over_row(): return lax.ppermute(x, 'prow', [(i, i ^ s) for i in range(rows)])  3.55 us
    unnamed x18, local copies, waits for them, and re-layouts  3.48 us
  transfers between devices with their start and end apart: 29, of which 9 were waited for; matrix products, arithmetic and copies ran while one was open for 5% of the time, Pallas kernels for 4%

profile of v1, /device:TPU:0, one launch (start us, length us, event | category | flops | bytes accessed | tf_op | source)
XLA Modules:
  0.0 85.6 jit_solution(11756089045262476787)
XLA Ops:
  1.2 2.6 %collective-permute-done.1.us_full_ref = bf16[256,256]{1,0:T(8,128)(2,1)S(1)} collective-permute-done((bf16[256,256]{1,0:T(8,128)(2,1)}, bf16[256,256]{1,0:T(8,128)(2,1)S(1)}, u32[]{:S(2)}, u32[]{:S(2)}) %collective-permute-start.1) | collective-permute-done | bytes 131104 | tf_op jit(solution)/shard_map/ppermute | solution.py:247
  3.8 0.9 %fusion.1.refs_0_ = bf16[2,256,128]{2,1,0:T(8,128)(2,1)S(1)} fusion(bf16[1,256,256]{2,1,0:T(8,128)(2,1)} %bitcast.39, bf16[1,256,256]{2,1,0:T(8,128)(2,1)S(1)} %bitcast.41, pred[]{:T(512)S(6)} %eq.27), kind=kLoop, calls=%fused_computation.7 | loop fusion | flops 589824 | bytes 393217 | tf_op jit(solution)/shard_map/jit(_where)/select_n | solution.py:265
  4.8 3.0 %collective-permute-start.2 = (bf16[2,256,128]{2,1,0:T(8,128)(2,1)S(1)}, bf16[2,256,128]{2,1,0:T(8,128)(2,1)S(1)}, u32[]{:S(2)}, u32[]{:S(2)}) collective-permute-start(bf16[2,256,128]{2,1,0:T(8,128)(2,1)S(1)} %fusion.1.refs_0_), channel_id=1, source_target_pairs={{0,2},{1,3},{2,0},{3,1},{4,6},{5,7},{6,4},{7,5},{8,10},{9,11},{10,... | collective-permute-start | bytes 393224 | tf_op jit(solution)/shard_map/ppermute | solution.py:250
  7.8 2.6 %collective-permute-start.3 = (bf16[2,256,128]{2,1,0:T(8,128)(2,1)S(1)}, bf16[2,256,128]{2,1,0:T(8,128)(2,1)S(1)}, u32[]{:S(2)}, u32[]{:S(2)}) collective-permute-start(bf16[2,256,128]{2,1,0:T(8,128)(2,1)S(1)} %fusion.1.refs_0_), channel_id=1, source_target_pairs={{0,4},{1,5},{2,6},{3,7},{4,0},{5,1},{6,2},{7,3},{8,12},{9,13},{10,... | collective-permute-start | bytes 393224 | tf_op jit(solution)/shard_map/ppermute | solution.py:250
  10.4 1.0 %fusion.2 = (bf16[1,256,256]{2,1,0:T(8,128)(2,1)S(1)}, bf16[256,256]{1,0:T(8,128)(2,1)S(1)}, bf16[256,256]{1,0:T(8,128)(2,1)S(1)}) fusion(bf16[2,1,256,256]{3,2,1,0:T(8,128)(2,1)} %param.15, pred[]{:T(512)S(6)} %eq.27), kind=kLoop, calls=%fused_computation.20 | loop fusion | flops 131072 | bytes 655361 | tf_op jit(solution)/shard_map/jit(_where)/select_n | solution.py:261
  12.2 1.3 %collective-permute-done.2.refs_1_ = bf16[2,256,128]{2,1,0:T(8,128)(2,1)S(1)} collective-permute-done((bf16[2,256,128]{2,1,0:T(8,128)(2,1)S(1)}, bf16[2,256,128]{2,1,0:T(8,128)(2,1)S(1)}, u32[]{:S(2)}, u32[]{:S(2)}) %collective-permute-start.2) | collective-permute-done | bytes 131104 | tf_op jit(solution)/shard_map/ppermute | solution.py:250
  13.4 7.2 %collective-permute-done.3.refs_2_ = bf16[2,256,128]{2,1,0:T(8,128)(2,1)S(1)} collective-permute-done((bf16[2,256,128]{2,1,0:T(8,128)(2,1)S(1)}, bf16[2,256,128]{2,1,0:T(8,128)(2,1)S(1)}, u32[]{:S(2)}, u32[]{:S(2)}) %collective-permute-start.3) | collective-permute-done | bytes 131104 | tf_op jit(solution)/shard_map/ppermute | solution.py:250
  20.7 0.9 %copy-done.2 = f32[1,256,256]{2,1,0:T(8,128)S(1)} copy-done((f32[1,256,256]{2,1,0:T(8,128)S(1)}, f32[1,256,256]{2,1,0:T(8,128)}, u32[]{:S(2)}) %copy-start.2) | copy-done | bytes 262168
  22.5 1.5 %shard_map.128 = (bf16[3,256,128]{2,1,0:T(8,128)(2,1)S(1)}, bf16[4,64,128]{2,1,0:T(8,128)(2,1)S(1)}) custom-call(s32[4,8]{1,0:T(4,128)S(1)} %copy-done.6, bf16[8,256,256]{2,1,0:T(8,128)(2,1)S(1)} %bitcast.34, bf16[8,256,256]{2,1,0:T(8,128)(2,1)S(1)} %collective-permute-done.ts_ref, bf16[256,256]{1,0:T(8,128)(2,1)S(1)} %bitcast.40, ...), custom_call_target="tpu_custom_call" | custom-call | tf_op jit(solution)/shard_map/pallas_call | solution.py:274
  24.1 2.5 %collective-permute-start.6 = (bf16[3,256,128]{2,1,0:T(8,128)(2,1)S(1)}, bf16[3,256,128]{2,1,0:T(8,128)(2,1)S(1)}, u32[]{:S(2)}, u32[]{:S(2)}) collective-permute-start(bf16[3,256,128]{2,1,0:T(8,128)(2,1)S(1)} %get-tuple-element.15), channel_id=1, source_target_pairs={{0,24},{8,16},{16,8},{24,0},{1,25},{9,17},{17,9},{25,1},{2,26},{10... | collective-permute-start | bytes 589832 | tf_op jit(solution)/shard_map/ppermute | solution.py:253
  30.9 2.4 %collective-permute-start.18 = (bf16[2,256,256]{2,1,0:T(8,128)(2,1)S(1)}, bf16[2,256,256]{2,1,0:T(8,128)(2,1)S(1)}, u32[]{:S(2)}, u32[]{:S(2)}) collective-permute-start(bf16[2,256,256]{2,1,0:T(8,128)(2,1)S(1)} %pad_maximum_fusion.refs_0_), channel_id=1, source_target_pairs={{0,2},{1,3},{2,0},{3,1},{4,6},{5,7},{6,4},{7,5},{8,10},{9,11},{10,... | collective-permute-start | bytes 786440 | tf_op jit(solution)/shard_map/ppermute | solution.py:250
  33.2 1.1 %collective-permute-start.19 = (bf16[2,256,256]{2,1,0:T(8,128)(2,1)S(1)}, bf16[2,256,256]{2,1,0:T(8,128)(2,1)S(1)}, u32[]{:S(2)}, u32[]{:S(2)}) collective-permute-start(bf16[2,256,256]{2,1,0:T(8,128)(2,1)S(1)} %pad_maximum_fusion.refs_0_), channel_id=1, source_target_pairs={{0,4},{1,5},{2,6},{3,7},{4,0},{5,1},{6,2},{7,3},{8,12},{9,13},{10,... | collective-permute-start | bytes 786440 | tf_op jit(solution)/shard_map/ppermute | solution.py:250
  34.3 1.4 %collective-permute-start.20 = (bf16[2,256,256]{2,1,0:T(8,128)(2,1)S(1)}, bf16[2,256,256]{2,1,0:T(8,128)(2,1)S(1)}, u32[]{:S(2)}, u32[]{:S(2)}) collective-permute-start(bf16[2,256,256]{2,1,0:T(8,128)(2,1)S(1)} %pad_maximum_fusion.refs_0_), channel_id=1, source_target_pairs={{0,6},{1,7},{2,4},{3,5},{4,2},{5,3},{6,0},{7,1},{8,14},{9,15},{10,... | collective-permute-start | bytes 786440 | tf_op jit(solution)/shard_map/ppermute | solution.py:250
  35.8 1.4 %collective-permute-done.9.got_ref = bf16[3,256,128]{2,1,0:T(8,128)(2,1)S(1)} collective-permute-done((bf16[3,256,128]{2,1,0:T(8,128)(2,1)S(1)}, bf16[3,256,128]{2,1,0:T(8,128)(2,1)S(1)}, u32[]{:S(2)}, u32[]{:S(2)}) %collective-permute-start.9) | collective-permute-done | bytes 196640 | tf_op jit(solution)/shard_map/ppermute | solution.py:247
  38.0 1.0 %shard_map.129 = (f32[2,256,256]{2,1,0:T(8,128)S(1)}, bf16[4,64,384]{2,1,0:T(8,128)(2,1)S(1)}) custom-call(s32[4,8]{1,0:T(4,128)S(1)} %copy-done.6, s32[8]{0:T(128)S(1)} %copy-done.8, s32[2,8]{1,0:T(2,128)S(1)} %copy-done.7, bf16[3,256,128]{2,1,0:T(8,128)(2,1)S(1)} %get-tuple-element.26.keep_ref, bf16[3,256,128]{2,1,0:T(8,128)(2,1)S(1)} %collective-permute-done.9.got_ref, ...), custom_call_target="tpu_custom_call" | custom-call | tf_op jit(solution)/shard_map/pallas_call | solution.py:274
  39.0 2.7 %collective-permute-done.18.refs_1_ = bf16[2,256,256]{2,1,0:T(8,128)(2,1)S(1)} collective-permute-done((bf16[2,256,256]{2,1,0:T(8,128)(2,1)S(1)}, bf16[2,256,256]{2,1,0:T(8,128)(2,1)S(1)}, u32[]{:S(2)}, u32[]{:S(2)}) %collective-permute-start.18) | collective-permute-done | bytes 262176 | tf_op jit(solution)/shard_map/ppermute | solution.py:250
  41.7 12.7 %collective-permute-done.19.refs_2_ = bf16[2,256,256]{2,1,0:T(8,128)(2,1)S(1)} collective-permute-done((bf16[2,256,256]{2,1,0:T(8,128)(2,1)S(1)}, bf16[2,256,256]{2,1,0:T(8,128)(2,1)S(1)}, u32[]{:S(2)}, u32[]{:S(2)}) %collective-permute-start.19) | collective-permute-done | bytes 262176 | tf_op jit(solution)/shard_map/ppermute | solution.py:250
  54.4 1.7 %shard_map.133 = (bf16[256,256]{1,0:T(8,128)(2,1)S(1)}, bf16[256,256]{1,0:T(8,128)(2,1)S(1)}, bf16[4,64,256]{2,1,0:T(8,128)(2,1)S(1)}) custom-call(s32[4,8]{1,0:T(4,128)S(1)} %copy-done.6, s32[8]{0:T(128)S(1)} %copy-done.8, s32[2,8]{1,0:T(2,128)S(1)} %copy-done.7, bf16[8,256,256]{2,1,0:T(8,128)(2,1)S(1)} %bitcast.35, ...), custom_call_target="tpu_custom_call" | custom-call | tf_op jit(solution)/shard_map/pallas_call | solution.py:274
  56.1 3.4 %collective-permute-start.22 = (bf16[64,256]{1,0:T(8,128)(2,1)S(1)}, bf16[64,256]{1,0:T(8,128)(2,1)S(1)}, u32[]{:S(2)}, u32[]{:S(2)}) collective-permute-start(bf16[64,256]{1,0:T(8,128)(2,1)S(1)} %get-tuple-element.37), channel_id=1, source_target_pairs={{0,2},{1,3},{2,0},{3,1},{4,6},{5,7},{6,4},{7,5},{8,10},{9,11},{10,... | collective-permute-start | bytes 98312 | tf_op jit(solution)/shard_map/ppermute | solution.py:250
  59.5 1.1 %collective-permute-start.23 = (bf16[64,256]{1,0:T(8,128)(2,1)S(1)}, bf16[64,256]{1,0:T(8,128)(2,1)S(1)}, u32[]{:S(2)}, u32[]{:S(2)}) collective-permute-start(bf16[64,256]{1,0:T(8,128)(2,1)S(1)} %get-tuple-element.36), channel_id=1, source_target_pairs={{0,4},{1,5},{2,6},{3,7},{4,0},{5,1},{6,2},{7,3},{8,12},{9,13},{10,... | collective-permute-start | bytes 98312 | tf_op jit(solution)/shard_map/ppermute | solution.py:250
  60.6 1.4 %collective-permute-start.24 = (bf16[64,256]{1,0:T(8,128)(2,1)S(1)}, bf16[64,256]{1,0:T(8,128)(2,1)S(1)}, u32[]{:S(2)}, u32[]{:S(2)}) collective-permute-start(bf16[64,256]{1,0:T(8,128)(2,1)S(1)} %get-tuple-element.35), channel_id=1, source_target_pairs={{0,6},{1,7},{2,4},{3,5},{4,2},{5,3},{6,0},{7,1},{8,14},{9,15},{10,... | collective-permute-start | bytes 98312 | tf_op jit(solution)/shard_map/ppermute | solution.py:250
  62.0 1.1 %collective-permute-start.11 = (bf16[64,384]{1,0:T(8,128)(2,1)S(1)}, bf16[64,384]{1,0:T(8,128)(2,1)S(1)}, u32[]{:S(2)}, u32[]{:S(2)}) collective-permute-start(bf16[64,384]{1,0:T(8,128)(2,1)S(1)} %get-tuple-element.32), channel_id=1, source_target_pairs={{0,2},{1,3},{2,0},{3,1},{4,6},{5,7},{6,4},{7,5},{8,10},{9,11},{10,... | collective-permute-start | bytes 147464 | tf_op jit(solution)/shard_map/ppermute | solution.py:250
  63.1 2.0 %collective-permute-start.12 = (bf16[64,384]{1,0:T(8,128)(2,1)S(1)}, bf16[64,384]{1,0:T(8,128)(2,1)S(1)}, u32[]{:S(2)}, u32[]{:S(2)}) collective-permute-start(bf16[64,384]{1,0:T(8,128)(2,1)S(1)} %get-tuple-element.31), channel_id=1, source_target_pairs={{0,4},{1,5},{2,6},{3,7},{4,0},{5,1},{6,2},{7,3},{8,12},{9,13},{10,... | collective-permute-start | bytes 147464 | tf_op jit(solution)/shard_map/ppermute | solution.py:250
  65.1 1.4 %collective-permute-start.13 = (bf16[64,384]{1,0:T(8,128)(2,1)S(1)}, bf16[64,384]{1,0:T(8,128)(2,1)S(1)}, u32[]{:S(2)}, u32[]{:S(2)}) collective-permute-start(bf16[64,384]{1,0:T(8,128)(2,1)S(1)} %get-tuple-element.30), channel_id=1, source_target_pairs={{0,6},{1,7},{2,4},{3,5},{4,2},{5,3},{6,0},{7,1},{8,14},{9,15},{10,... | collective-permute-start | bytes 147464 | tf_op jit(solution)/shard_map/ppermute | solution.py:250
  66.6 1.0 %collective-permute-start.25 = (bf16[64,256]{1,0:T(8,128)(2,1)S(1)}, bf16[64,256]{1,0:T(8,128)(2,1)S(1)}, u32[]{:S(2)}, u32[]{:S(2)}) collective-permute-start(bf16[64,256]{1,0:T(8,128)(2,1)S(1)} %shard_map.134.refs_0_), channel_id=1, source_target_pairs={{0,2},{1,3},{2,0},{3,1},{4,6},{5,7},{6,4},{7,5},{8,10},{9,11},{10,... | collective-permute-start | bytes 98312 | tf_op jit(solution)/shard_map/ppermute | solution.py:250
  67.6 2.0 %collective-permute-start.26 = (bf16[64,256]{1,0:T(8,128)(2,1)S(1)}, bf16[64,256]{1,0:T(8,128)(2,1)S(1)}, u32[]{:S(2)}, u32[]{:S(2)}) collective-permute-start(bf16[64,256]{1,0:T(8,128)(2,1)S(1)} %shard_map.134.refs_0_), channel_id=1, source_target_pairs={{0,4},{1,5},{2,6},{3,7},{4,0},{5,1},{6,2},{7,3},{8,12},{9,13},{10,... | collective-permute-start | bytes 98312 | tf_op jit(solution)/shard_map/ppermute | solution.py:250
  69.7 1.4 %collective-permute-done.13.refs_3_ = bf16[64,384]{1,0:T(8,128)(2,1)S(1)} collective-permute-done((bf16[64,384]{1,0:T(8,128)(2,1)S(1)}, bf16[64,384]{1,0:T(8,128)(2,1)S(1)}, u32[]{:S(2)}, u32[]{:S(2)}) %collective-permute-start.13) | collective-permute-done | bytes 49184 | tf_op jit(solution)/shard_map/ppermute | solution.py:250
  71.2 1.9 %collective-permute-start.15 = (bf16[64,384]{1,0:T(8,128)(2,1)S(1)}, bf16[64,384]{1,0:T(8,128)(2,1)S(1)}, u32[]{:S(2)}, u32[]{:S(2)}) collective-permute-start(bf16[64,384]{1,0:T(8,128)(2,1)S(1)} %shard_map.130.refs_0_), channel_id=1, source_target_pairs={{0,4},{1,5},{2,6},{3,7},{4,0},{5,1},{6,2},{7,3},{8,12},{9,13},{10,... | collective-permute-start | bytes 147464 | tf_op jit(solution)/shard_map/ppermute | solution.py:250
  73.1 2.4 %collective-permute-start.16 = (bf16[64,384]{1,0:T(8,128)(2,1)S(1)}, bf16[64,384]{1,0:T(8,128)(2,1)S(1)}, u32[]{:S(2)}, u32[]{:S(2)}) collective-permute-start(bf16[64,384]{1,0:T(8,128)(2,1)S(1)} %shard_map.130.refs_0_), channel_id=1, source_target_pairs={{0,6},{1,7},{2,4},{3,5},{4,2},{5,3},{6,0},{7,1},{8,14},{9,15},{10,... | collective-permute-start | bytes 147464 | tf_op jit(solution)/shard_map/ppermute | solution.py:250
  75.6 1.4 %collective-permute-start.27 = (bf16[64,256]{1,0:T(8,128)(2,1)S(1)}, bf16[64,256]{1,0:T(8,128)(2,1)S(1)}, u32[]{:S(2)}, u32[]{:S(2)}) collective-permute-start(bf16[64,256]{1,0:T(8,128)(2,1)S(1)} %shard_map.134.refs_0_), channel_id=1, source_target_pairs={{0,6},{1,7},{2,4},{3,5},{4,2},{5,3},{6,0},{7,1},{8,14},{9,15},{10,... | collective-permute-start | bytes 98312 | tf_op jit(solution)/shard_map/ppermute | solution.py:250
  77.0 4.3 %collective-permute-done.27.refs_3_ = bf16[64,256]{1,0:T(8,128)(2,1)S(1)} collective-permute-done((bf16[64,256]{1,0:T(8,128)(2,1)S(1)}, bf16[64,256]{1,0:T(8,128)(2,1)S(1)}, u32[]{:S(2)}, u32[]{:S(2)}) %collective-permute-start.27) | collective-permute-done | bytes 32800 | tf_op jit(solution)/shard_map/ppermute | solution.py:250
  83.8 1.0 %shard_map.132 = (f32[1,256,256]{2,1,0:T(8,128)}, bf16[2,256,256]{2,1,0:T(8,128)(2,1)}, f32[2,256,256]{2,1,0:T(8,128)S(1)}) custom-call(bf16[256,384]{1,0:T(8,128)(2,1)S(1)} %shard_map.131.own_ref, bf16[256,384]{1,0:T(8,128)(2,1)S(1)} %collective-permute-done.17.got_ref, f32[1,256,256]{2,1,0:T(8,128)S(1)} %copy-done.3, f32[2,256,256]{2,1,0:T(8,128)S(1)} %copy-done.4, ...), custom_call_target="tpu_custom_call" | custom-call | tf_op jit(solution)/shard_map/pallas_call | solution.py:274
  (64 shorter events, 8.4 us)
Async XLA Ops:
  0.6 20.0 %copy-start = (bf16[1,8,256,256]{3,2,1,0:T(8,128)(2,1)S(1)}, bf16[1,8,256,256]{3,2,1,0:T(8,128)(2,1)}, u32[]{:S(2)}) copy-start(bf16[1,8,256,256]{3,2,1,0:T(8,128)(2,1)} %param.9) | copy-start | bytes 3145732
  0.6 20.0 %collective-permute-start = (bf16[8,256,256]{2,1,0:T(8,128)(2,1)}, bf16[8,256,256]{2,1,0:T(8,128)(2,1)S(1)}, u32[]{:S(2)}, u32[]{:S(2)}) collective-permute-start(bf16[8,256,256]{2,1,0:T(8,128)(2,1)} %bitcast.33), channel_id=1, source_target_pairs={{0,1},{1,0},{2,3},{3,2},{4,5},{5,4},{6,7},{7,6},{8,9},{9,8},{10,11... | collective-permute-start | bytes 3145736 | tf_op jit(solution)/shard_map/ppermute | solution.py:247
  1.2 2.7 %collective-permute-start.1 = (bf16[256,256]{1,0:T(8,128)(2,1)}, bf16[256,256]{1,0:T(8,128)(2,1)S(1)}, u32[]{:S(2)}, u32[]{:S(2)}) collective-permute-start(bf16[256,256]{1,0:T(8,128)(2,1)} %bitcast.38), channel_id=1, source_target_pairs={{0,1},{1,0},{2,3},{3,2},{4,5},{5,4},{6,7},{7,6},{8,9},{9,8},{10,11... | collective-permute-start | bytes 393224 | tf_op jit(solution)/shard_map/ppermute | solution.py:247
  4.8 8.7 %collective-permute-start.2 = (bf16[2,256,128]{2,1,0:T(8,128)(2,1)S(1)}, bf16[2,256,128]{2,1,0:T(8,128)(2,1)S(1)}, u32[]{:S(2)}, u32[]{:S(2)}) collective-permute-start(bf16[2,256,128]{2,1,0:T(8,128)(2,1)S(1)} %fusion.1.refs_0_), channel_id=1, source_target_pairs={{0,2},{1,3},{2,0},{3,1},{4,6},{5,7},{6,4},{7,5},{8,10},{9,11},{10,... | collective-permute-start | bytes 393224 | tf_op jit(solution)/shard_map/ppermute | solution.py:250
  7.8 12.9 %collective-permute-start.3 = (bf16[2,256,128]{2,1,0:T(8,128)(2,1)S(1)}, bf16[2,256,128]{2,1,0:T(8,128)(2,1)S(1)}, u32[]{:S(2)}, u32[]{:S(2)}) collective-permute-start(bf16[2,256,128]{2,1,0:T(8,128)(2,1)S(1)} %fusion.1.refs_0_), channel_id=1, source_target_pairs={{0,4},{1,5},{2,6},{3,7},{4,0},{5,1},{6,2},{7,3},{8,12},{9,13},{10,... | collective-permute-start | bytes 393224 | tf_op jit(solution)/shard_map/ppermute | solution.py:250
  10.4 10.3 %collective-permute-start.4 = (bf16[2,256,128]{2,1,0:T(8,128)(2,1)S(1)}, bf16[2,256,128]{2,1,0:T(8,128)(2,1)S(1)}, u32[]{:S(2)}, u32[]{:S(2)}) collective-permute-start(bf16[2,256,128]{2,1,0:T(8,128)(2,1)S(1)} %fusion.1.refs_0_), channel_id=1, source_target_pairs={{0,6},{1,7},{2,4},{3,5},{4,2},{5,3},{6,0},{7,1},{8,14},{9,15},{10,... | collective-permute-start | bytes 393224 | tf_op jit(solution)/shard_map/ppermute | solution.py:250
  11.4 19.5 %collective-permute-start.10 = (bf16[256,256]{1,0:T(8,128)(2,1)S(1)}, bf16[256,256]{1,0:T(8,128)(2,1)S(1)}, u32[]{:S(2)}, u32[]{:S(2)}) collective-permute-start(bf16[256,256]{1,0:T(8,128)(2,1)S(1)} %get-tuple-element.29), channel_id=1, source_target_pairs={{0,1},{1,0},{2,3},{3,2},{4,5},{5,4},{6,7},{7,6},{8,9},{9,8},{10,11... | collective-permute-start | bytes 393224 | tf_op jit(solution)/shard_map/ppermute | solution.py:247
  12.1 8.6 %copy-start.6 = (s32[4,8]{1,0:T(4,128)S(1)}, s32[4,8]{1,0:T(4,128)}, u32[]{:S(2)}) copy-start(s32[4,8]{1,0:T(4,128)} %us_ref.5) | copy-start | bytes 388
  24.1 10.3 %collective-permute-start.6 = (bf16[3,256,128]{2,1,0:T(8,128)(2,1)S(1)}, bf16[3,256,128]{2,1,0:T(8,128)(2,1)S(1)}, u32[]{:S(2)}, u32[]{:S(2)}) collective-permute-start(bf16[3,256,128]{2,1,0:T(8,128)(2,1)S(1)} %get-tuple-element.15), channel_id=1, source_target_pairs={{0,24},{8,16},{16,8},{24,0},{1,25},{9,17},{17,9},{25,1},{2,26},{10... | collective-permute-start | bytes 589832 | tf_op jit(solution)/shard_map/ppermute | solution.py:253
  26.6 9.1 %collective-permute-start.7 = (bf16[3,256,128]{2,1,0:T(8,128)(2,1)S(1)}, bf16[3,256,128]{2,1,0:T(8,128)(2,1)S(1)}, u32[]{:S(2)}, u32[]{:S(2)}) collective-permute-start(bf16[3,256,128]{2,1,0:T(8,128)(2,1)S(1)} %get-tuple-element.15), channel_id=1, source_target_pairs={{0,16},{8,24},{16,0},{24,8},{1,17},{9,25},{17,1},{25,9},{2,18},{10... | collective-permute-start | bytes 589832 | tf_op jit(solution)/shard_map/ppermute | solution.py:253
  27.1 8.6 %collective-permute-start.8 = (bf16[3,256,128]{2,1,0:T(8,128)(2,1)S(1)}, bf16[3,256,128]{2,1,0:T(8,128)(2,1)S(1)}, u32[]{:S(2)}, u32[]{:S(2)}) collective-permute-start(bf16[3,256,128]{2,1,0:T(8,128)(2,1)S(1)} %get-tuple-element.15), channel_id=1, source_target_pairs={{0,8},{8,0},{16,24},{24,16},{1,9},{9,1},{17,25},{25,17},{2,10},{10... | collective-permute-start | bytes 589832 | tf_op jit(solution)/shard_map/ppermute | solution.py:253
  30.9 6.4 %copy-start.1 = (bf16[2,256,256]{2,1,0:T(8,128)(2,1)S(1)}, bf16[2,256,256]{2,1,0:T(8,128)(2,1)}, u32[]{:S(2)}) copy-start(bf16[2,256,256]{2,1,0:T(8,128)(2,1)} %pp_ref.3) | copy-start | bytes 786436
  30.9 10.8 %collective-permute-start.18 = (bf16[2,256,256]{2,1,0:T(8,128)(2,1)S(1)}, bf16[2,256,256]{2,1,0:T(8,128)(2,1)S(1)}, u32[]{:S(2)}, u32[]{:S(2)}) collective-permute-start(bf16[2,256,256]{2,1,0:T(8,128)(2,1)S(1)} %pad_maximum_fusion.refs_0_), channel_id=1, source_target_pairs={{0,2},{1,3},{2,0},{3,1},{4,6},{5,7},{6,4},{7,5},{8,10},{9,11},{10,... | collective-permute-start | bytes 786440 | tf_op jit(solution)/shard_map/ppermute | solution.py:250
  33.2 21.1 %collective-permute-start.19 = (bf16[2,256,256]{2,1,0:T(8,128)(2,1)S(1)}, bf16[2,256,256]{2,1,0:T(8,128)(2,1)S(1)}, u32[]{:S(2)}, u32[]{:S(2)}) collective-permute-start(bf16[2,256,256]{2,1,0:T(8,128)(2,1)S(1)} %pad_maximum_fusion.refs_0_), channel_id=1, source_target_pairs={{0,4},{1,5},{2,6},{3,7},{4,0},{5,1},{6,2},{7,3},{8,12},{9,13},{10,... | collective-permute-start | bytes 786440 | tf_op jit(solution)/shard_map/ppermute | solution.py:250
  34.3 20.0 %collective-permute-start.20 = (bf16[2,256,256]{2,1,0:T(8,128)(2,1)S(1)}, bf16[2,256,256]{2,1,0:T(8,128)(2,1)S(1)}, u32[]{:S(2)}, u32[]{:S(2)}) collective-permute-start(bf16[2,256,256]{2,1,0:T(8,128)(2,1)S(1)} %pad_maximum_fusion.refs_0_), channel_id=1, source_target_pairs={{0,6},{1,7},{2,4},{3,5},{4,2},{5,3},{6,0},{7,1},{8,14},{9,15},{10,... | collective-permute-start | bytes 786440 | tf_op jit(solution)/shard_map/ppermute | solution.py:250
  35.8 1.5 %collective-permute-start.9 = (bf16[3,256,128]{2,1,0:T(8,128)(2,1)S(1)}, bf16[3,256,128]{2,1,0:T(8,128)(2,1)S(1)}, u32[]{:S(2)}, u32[]{:S(2)}) collective-permute-start(bf16[3,256,128]{2,1,0:T(8,128)(2,1)S(1)} %get-tuple-element.25), channel_id=1, source_target_pairs={{0,1},{1,0},{2,3},{3,2},{4,5},{5,4},{6,7},{7,6},{8,9},{9,8},{10,11... | collective-permute-start | bytes 589832 | tf_op jit(solution)/shard_map/ppermute | solution.py:247
  56.1 9.0 %collective-permute-start.22 = (bf16[64,256]{1,0:T(8,128)(2,1)S(1)}, bf16[64,256]{1,0:T(8,128)(2,1)S(1)}, u32[]{:S(2)}, u32[]{:S(2)}) collective-permute-start(bf16[64,256]{1,0:T(8,128)(2,1)S(1)} %get-tuple-element.37), channel_id=1, source_target_pairs={{0,2},{1,3},{2,0},{3,1},{4,6},{5,7},{6,4},{7,5},{8,10},{9,11},{10,... | collective-permute-start | bytes 98312 | tf_op jit(solution)/shard_map/ppermute | solution.py:250
  59.5 7.0 %collective-permute-start.23 = (bf16[64,256]{1,0:T(8,128)(2,1)S(1)}, bf16[64,256]{1,0:T(8,128)(2,1)S(1)}, u32[]{:S(2)}, u32[]{:S(2)}) collective-permute-start(bf16[64,256]{1,0:T(8,128)(2,1)S(1)} %get-tuple-element.36), channel_id=1, source_target_pairs={{0,4},{1,5},{2,6},{3,7},{4,0},{5,1},{6,2},{7,3},{8,12},{9,13},{10,... | collective-permute-start | bytes 98312 | tf_op jit(solution)/shard_map/ppermute | solution.py:250
  60.6 6.0 %collective-permute-start.24 = (bf16[64,256]{1,0:T(8,128)(2,1)S(1)}, bf16[64,256]{1,0:T(8,128)(2,1)S(1)}, u32[]{:S(2)}, u32[]{:S(2)}) collective-permute-start(bf16[64,256]{1,0:T(8,128)(2,1)S(1)} %get-tuple-element.35), channel_id=1, source_target_pairs={{0,6},{1,7},{2,4},{3,5},{4,2},{5,3},{6,0},{7,1},{8,14},{9,15},{10,... | collective-permute-start | bytes 98312 | tf_op jit(solution)/shard_map/ppermute | solution.py:250
  62.0 7.6 %collective-permute-start.11 = (bf16[64,384]{1,0:T(8,128)(2,1)S(1)}, bf16[64,384]{1,0:T(8,128)(2,1)S(1)}, u32[]{:S(2)}, u32[]{:S(2)}) collective-permute-start(bf16[64,384]{1,0:T(8,128)(2,1)S(1)} %get-tuple-element.32), channel_id=1, source_target_pairs={{0,2},{1,3},{2,0},{3,1},{4,6},{5,7},{6,4},{7,5},{8,10},{9,11},{10,... | collective-permute-start | bytes 147464 | tf_op jit(solution)/shard_map/ppermute | solution.py:250
  63.1 6.6 %collective-permute-start.12 = (bf16[64,384]{1,0:T(8,128)(2,1)S(1)}, bf16[64,384]{1,0:T(8,128)(2,1)S(1)}, u32[]{:S(2)}, u32[]{:S(2)}) collective-permute-start(bf16[64,384]{1,0:T(8,128)(2,1)S(1)} %get-tuple-element.31), channel_id=1, source_target_pairs={{0,4},{1,5},{2,6},{3,7},{4,0},{5,1},{6,2},{7,3},{8,12},{9,13},{10,... | collective-permute-start | bytes 147464 | tf_op jit(solution)/shard_map/ppermute | solution.py:250
  65.1 6.0 %collective-permute-start.13 = (bf16[64,384]{1,0:T(8,128)(2,1)S(1)}, bf16[64,384]{1,0:T(8,128)(2,1)S(1)}, u32[]{:S(2)}, u32[]{:S(2)}) collective-permute-start(bf16[64,384]{1,0:T(8,128)(2,1)S(1)} %get-tuple-element.30), channel_id=1, source_target_pairs={{0,6},{1,7},{2,4},{3,5},{4,2},{5,3},{6,0},{7,1},{8,14},{9,15},{10,... | collective-permute-start | bytes 147464 | tf_op jit(solution)/shard_map/ppermute | solution.py:250
  66.6 6.5 %collective-permute-start.25 = (bf16[64,256]{1,0:T(8,128)(2,1)S(1)}, bf16[64,256]{1,0:T(8,128)(2,1)S(1)}, u32[]{:S(2)}, u32[]{:S(2)}) collective-permute-start(bf16[64,256]{1,0:T(8,128)(2,1)S(1)} %shard_map.134.refs_0_), channel_id=1, source_target_pairs={{0,2},{1,3},{2,0},{3,1},{4,6},{5,7},{6,4},{7,5},{8,10},{9,11},{10,... | collective-permute-start | bytes 98312 | tf_op jit(solution)/shard_map/ppermute | solution.py:250
  67.6 8.0 %collective-permute-start.26 = (bf16[64,256]{1,0:T(8,128)(2,1)S(1)}, bf16[64,256]{1,0:T(8,128)(2,1)S(1)}, u32[]{:S(2)}, u32[]{:S(2)}) collective-permute-start(bf16[64,256]{1,0:T(8,128)(2,1)S(1)} %shard_map.134.refs_0_), channel_id=1, source_target_pairs={{0,4},{1,5},{2,6},{3,7},{4,0},{5,1},{6,2},{7,3},{8,12},{9,13},{10,... | collective-permute-start | bytes 98312 | tf_op jit(solution)/shard_map/ppermute | solution.py:250
  69.6 12.5 %collective-permute-start.5 = (bf16[256,128]{1,0:T(8,128)(2,1)S(1)}, bf16[256,128]{1,0:T(8,128)(2,1)S(1)}, u32[]{:S(2)}, u32[]{:S(2)}) collective-permute-start(bf16[256,128]{1,0:T(8,128)(2,1)S(1)} %get-tuple-element.34), channel_id=1, source_target_pairs={{0,1},{1,0},{2,3},{3,2},{4,5},{5,4},{6,7},{7,6},{8,9},{9,8},{10,11... | collective-permute-start | bytes 196616 | tf_op jit(solution)/shard_map/ppermute | solution.py:247
  71.1 10.2 %collective-permute-start.14 = (bf16[64,384]{1,0:T(8,128)(2,1)S(1)}, bf16[64,384]{1,0:T(8,128)(2,1)S(1)}, u32[]{:S(2)}, u32[]{:S(2)}) collective-permute-start(bf16[64,384]{1,0:T(8,128)(2,1)S(1)} %shard_map.130.refs_0_), channel_id=1, source_target_pairs={{0,2},{1,3},{2,0},{3,1},{4,6},{5,7},{6,4},{7,5},{8,10},{9,11},{10,... | collective-permute-start | bytes 147464 | tf_op jit(solution)/shard_map/ppermute | solution.py:250
  71.2 10.7 %collective-permute-start.15 = (bf16[64,384]{1,0:T(8,128)(2,1)S(1)}, bf16[64,384]{1,0:T(8,128)(2,1)S(1)}, u32[]{:S(2)}, u32[]{:S(2)}) collective-permute-start(bf16[64,384]{1,0:T(8,128)(2,1)S(1)} %shard_map.130.refs_0_), channel_id=1, source_target_pairs={{0,4},{1,5},{2,6},{3,7},{4,0},{5,1},{6,2},{7,3},{8,12},{9,13},{10,... | collective-permute-start | bytes 147464 | tf_op jit(solution)/shard_map/ppermute | solution.py:250
  73.1 8.8 %collective-permute-start.16 = (bf16[64,384]{1,0:T(8,128)(2,1)S(1)}, bf16[64,384]{1,0:T(8,128)(2,1)S(1)}, u32[]{:S(2)}, u32[]{:S(2)}) collective-permute-start(bf16[64,384]{1,0:T(8,128)(2,1)S(1)} %shard_map.130.refs_0_), channel_id=1, source_target_pairs={{0,6},{1,7},{2,4},{3,5},{4,2},{5,3},{6,0},{7,1},{8,14},{9,15},{10,... | collective-permute-start | bytes 147464 | tf_op jit(solution)/shard_map/ppermute | solution.py:250
  75.6 5.7 %collective-permute-start.27 = (bf16[64,256]{1,0:T(8,128)(2,1)S(1)}, bf16[64,256]{1,0:T(8,128)(2,1)S(1)}, u32[]{:S(2)}, u32[]{:S(2)}) collective-permute-start(bf16[64,256]{1,0:T(8,128)(2,1)S(1)} %shard_map.134.refs_0_), channel_id=1, source_target_pairs={{0,6},{1,7},{2,4},{3,5},{4,2},{5,3},{6,0},{7,1},{8,14},{9,15},{10,... | collective-permute-start | bytes 98312 | tf_op jit(solution)/shard_map/ppermute | solution.py:250
  81.3 1.5 %collective-permute-start.21 = (bf16[256,256]{1,0:T(8,128)(2,1)S(1)}, bf16[256,256]{1,0:T(8,128)(2,1)S(1)}, u32[]{:S(2)}, u32[]{:S(2)}) collective-permute-start(bf16[256,256]{1,0:T(8,128)(2,1)S(1)} %get-tuple-element.21), channel_id=1, source_target_pairs={{0,1},{1,0},{2,3},{3,2},{4,5},{5,4},{6,7},{7,6},{8,9},{9,8},{10,11... | collective-permute-start | bytes 393224 | tf_op jit(solution)/shard_map/ppermute | solution.py:247
  81.3 3.5 %collective-permute-start.28 = (bf16[256,256]{1,0:T(8,128)(2,1)S(1)}, bf16[256,256]{1,0:T(8,128)(2,1)S(1)}, u32[]{:S(2)}, u32[]{:S(2)}) collective-permute-start(bf16[256,256]{1,0:T(8,128)(2,1)S(1)} %shard_map.135.own_ref), channel_id=1, source_target_pairs={{0,1},{1,0},{2,3},{3,2},{4,5},{5,4},{6,7},{7,6},{8,9},{9,8},{10,11... | collective-permute-start | bytes 393224 | tf_op jit(solution)/shard_map/ppermute | solution.py:247
  81.9 1.5 %collective-permute-start.17 = (bf16[256,384]{1,0:T(8,128)(2,1)S(1)}, bf16[256,384]{1,0:T(8,128)(2,1)S(1)}, u32[]{:S(2)}, u32[]{:S(2)}) collective-permute-start(bf16[256,384]{1,0:T(8,128)(2,1)S(1)} %shard_map.131.own_ref), channel_id=1, source_target_pairs={{0,1},{1,0},{2,3},{3,2},{4,5},{5,4},{6,7},{7,6},{8,9},{9,8},{10,11... | collective-permute-start | bytes 589832 | tf_op jit(solution)/shard_map/ppermute | solution.py:247
  (6 other events, 6.4 us)

commit v2 on v1

--- a/solution.py
+++ b/solution.py
@@ -101,9 +101,15 @@
     return lax.axis_index("prow"), col // CORES, col % CORES
 
 
-def upper_body(nz, us_ref, to_ref, ts_ref, uo_ref, us_full_ref, d_ref, *refs):
-    stacks, (rx_ref, ud_ref, xs) = refs[:nz], refs[nz:]
+def upper_body(nz, us_ref, to_ref, ts_ref, us_full_ref, uo_hbm, d_hbm, *refs):
+    stacks, (rx_ref, ud_ref, xs, uo_ref, d_ref, sems) = refs[:nz], refs[-6:]
     row, z, c = place()
+    copies = [
+        pltpu.make_async_copy(uo_hbm, uo_ref, sems.at[0]),
+        pltpu.make_async_copy(d_hbm, d_ref, sems.at[1]),
+    ]
+    for copy in copies:
+        copy.start()
     half = xs.shape[1]
     quarter = xs.shape[0] // nz
     acc = [None, None]
@@ -115,6 +121,8 @@
             for p, t_ref in enumerate((to_ref, ts_ref)):
                 prod = dot(t_ref[i], piece)
                 acc[p] = prod if acc[p] is None else acc[p] + prod
+    for copy in copies:
+        copy.wait()
     x = None
     for p, u_ref in enumerate((uo_ref, us_full_ref)):
         j = CORES * z + (c if p == 0 else 1 - c)
@@ -130,6 +138,18 @@
     rows = d_ref[own, :]
     xs[own, :] = xs[own, :] + jnp.where(c == 0, rows[:, :half], rows[:, half:])
     rx_ref[CORES] = xs[...].astype(BF)
+
+
+def pick_body(rows, co_ref, *refs):
+    blocks, (keep_ref, give_ref) = refs[:rows], refs[-2:]
+    row, _, c = place()
+    for k, out_ref in ((c, keep_ref), (1 - c, give_ref)):
+        index = (co_ref[CORES * row + k] // CH) ^ row
+        for s, block in enumerate(blocks):
+
+            @pl.when(index == s)
+            def _(out_ref=out_ref, block=block):
+                out_ref[...] = block[...]
 
 
 def parent_body(nz, us_ref, co_ref, ck_ref, keep_ref, got_ref, pp_ref, lm_ref, lg_ref, ud_ref,
@@ -157,8 +177,8 @@
         rs_ref[s, :, size:] = ud_ref[s]
 
 
-def lower_body(nz, us_ref, co_ref, ck_ref, to_ref, ts_ref, w_ref, *refs):
-    stacks, (lo_ref, lg_ref, rs_ref, r_ref) = refs[:nz], refs[nz:]
+def lower_body(nz, us_ref, co_ref, ck_ref, to_ref, ts_ref, w_ref, rs1_ref, *refs):
+    stacks, (lo_ref, lg_ref, rs_ref, r_ref) = refs[:nz], refs[-4:]
     row, z, c = place()
     quarter = r_ref.shape[0] // nz
     parent = co_ref[CORES * row + c] // CH
@@ -179,49 +199,60 @@
         prod = dot_t(stacks[0][p], block)
         total = prod if total is None else total + prod
     r_ref[...] = total
+    size = r_ref.shape[1]
     for s in range(nz):
-        rs_ref[s] = r_ref[
-            pl.ds(pl.multiple_of((z ^ s) * quarter, quarter), quarter), :
-        ].astype(BF)
-
-
-def add_body(negate, *refs):
+        block = pl.ds(pl.multiple_of((z ^ s) * quarter, quarter), quarter)
+        rs_ref[s, :, :size] = r_ref[block, :].astype(BF)
+        rs_ref[s, :, size:] = rs1_ref[s]
+
+
+def pair_body(count, *refs):
+    for i, ref in enumerate(refs[:count]):
+        refs[-1][i] = ref[...]
+
+
+def halves_body(own_ref, got_ref, out_ref):
+    _, _, c = place()
+    half = own_ref.shape[1]
+    own, got = own_ref[...], got_ref[...]
+    out_ref[0, 0, :, :half] = jnp.where(c == 0, own, got)
+    out_ref[0, 0, :, half:] = jnp.where(c == 0, got, own)
+
+
+def order_body(own_ref, got_ref, out_ref):
+    _, _, c = place()
+    out_ref[c, 0] = own_ref[...]
+    out_ref[1 - c, 0] = got_ref[...]
+
+
+def add_body(own_ref, *refs):
     *parts, out_ref = refs
-    total = parts[0][0].astype(F32)
-    for part in parts[1:]:
+    total = own_ref[0].astype(F32)
+    for part in parts:
         total = total + part[...].astype(F32)
-    if negate:
-        out_ref[:, :negate] = (-total[:, :negate]).astype(BF)
-        out_ref[:, negate:] = total[:, negate:].astype(BF)
-    else:
-        out_ref[...] = total.astype(BF)
-
-
-def join_body(*refs):
-    *parts, out_ref = refs
+    out_ref[...] = total.astype(BF)
+
+
+def join_body(nz, *refs):
+    parts, out_ref = refs[:nz], refs[-1]
     _, z, _ = place()
     for s, part in enumerate(parts):
         quarter = part.shape[0]
         out_ref[pl.ds(pl.multiple_of((z ^ s) * quarter, quarter), quarter), :] = part[...]
 
 
-def parent_out_body(own_ref, got_ref, d_ref, ld_ref, pp_ref, ud_ref, lp_ref, base_ref):
+def out_body(own_ref, got_ref, d_ref, pp_ref, ld_ref, ud_ref, lp_ref, out_ref):
     _, _, c = place()
     size = pp_ref.shape[1]
     half = size // CORES
-    first, second = own_ref[:, size:].astype(F32), got_ref[:, size:].astype(F32)
+    first = own_ref[:, 2 * size :].astype(F32)
+    second = got_ref[:, 2 * size :].astype(F32)
     ud_ref[0, :, :half] = d_ref[0, :, :half] + jnp.where(c == 0, first, second)
     ud_ref[0, :, half:] = d_ref[0, :, half:] + jnp.where(c == 0, second, first)
     for k, ref in ((c, own_ref), (1 - c, got_ref)):
-        block = ref[:, :size]
+        block = -ref[:, size : 2 * size]
         lp_ref[k] = block
-        base_ref[k] = ld_ref[k] - dot_t(pp_ref[k], block)
-
-
-def lower_out_body(base_ref, own_ref, got_ref, ld_ref):
-    _, _, c = place()
-    ld_ref[c] = base_ref[c] - own_ref[...].astype(F32)
-    ld_ref[1 - c] = base_ref[1 - c] - got_ref[...].astype(F32)
+        out_ref[k] = ld_ref[k] - dot_t(pp_ref[k], block) - ref[:, :size].astype(F32)
 
 
 def near_shards(
@@ -263,94 +294,102 @@
     t_sib = over_core(t_own)
     u_both = jnp.stack([u_own, u_sib])
     u_stack = jnp.where(first, u_both[:, :, :half], u_both[:, :, half:])
-    l_stack = jnp.stack([l_own, l_sib])
     u_all = [u_stack] + [over_z(u_stack, s) for s in range(1, nz)]
-    l_all = [l_stack] + [over_z(l_stack, s) for s in range(1, nz)]
 
     vm = pl.BlockSpec(memory_space=pltpu.VMEM)
     sm = pl.BlockSpec(memory_space=pltpu.SMEM)
 
-    def kernel(body, out, args, smem=0, scratch=()):
+    anywhere = pl.BlockSpec(memory_space=pl.ANY)
+
+    def kernel(body, out, args, smem=0, scratch=(), rest=()):
         return pl.pallas_call(
             body,
             out_shape=out,
-            in_specs=[sm] * smem + [vm] * (len(args) - smem),
+            in_specs=[sm] * smem + [vm] * (len(args) - smem) + [anywhere] * len(rest),
             out_specs=jax.tree.map(lambda _: vm, out),
             scratch_shapes=list(scratch),
             compiler_params=pltpu.CompilerParams(vmem_limit_bytes=24 * 1024 * 1024),
-        )(*args)
-
-    rx, ud_part = kernel(
-        functools.partial(upper_body, nz),
-        (shape((CORES + 1, size, half), BF), shape((nz, quarter, half), BF)),
-        (upper_structure, t_own, t_sib, u_own, u_sib, d_own, *u_all),
-        smem=1,
-        scratch=[pltpu.VMEM((size, half), F32)],
-    )
-    ub_got = over_core(rx[1])
-    ub_own = rx[0]
-    upper_blocks = jnp.where(
-        first,
-        jnp.concatenate([ub_own, ub_got], axis=1),
-        jnp.concatenate([ub_got, ub_own], axis=1),
-    )[None, None]
-
-    rx_all = [rx] + [over_row(rx, s) for s in range(1, rows)]
-    parents = lax.dynamic_slice_in_dim(child_order, CORES * row, CORES) // CH
-
-    def pick(k):
-        index = jnp.where(k == 0, parents[0], parents[1]) ^ row
-        out = rx_all[0]
-        for s in range(1, rows):
-            out = jnp.where(index == s, rx_all[s], out)
-        return out
-
-    keep = pick(c)
-    got = over_core(pick(1 - c))
+        )(*args, *rest)
+
+    def upper(us, to, ts, usib, *refs):
+        stacks, uo, d = refs[:nz], refs[nz], refs[nz + 1]
+        upper_body(nz, us, to, ts, usib, uo, d, *stacks, *refs[-6:])
+
+    l_stack = kernel(
+        functools.partial(pair_body, 2), shape((CORES, size, size), BF), (l_own, l_sib), rest=(u_stack,)
+    )
+    l_later = lax.optimization_barrier((l_stack, *u_all[1:]))[0]
+    l_stacks = [l_stack, over_z(l_stack, 1)] + [over_z(l_later, s) for s in range(2, nz)]
     scalars = (upper_structure, child_order, child_keep)
-    w, rs1 = kernel(
-        functools.partial(parent_body, nz),
-        (shape((CORES, size, size), F32), shape((nz, quarter, size + half), BF)),
-        (*scalars, keep, got, parent_panels, l_own, l_sib, ud_part),
+
+    def upper_part(_):
+        rx, ud_part = kernel(
+            upper,
+            (shape((CORES + 1, size, half), BF), shape((nz, quarter, half), BF)),
+            (upper_structure, t_own, t_sib, u_sib, *u_all),
+            smem=1,
+            scratch=[
+                pltpu.VMEM((size, half), F32),
+                pltpu.VMEM((size, size), BF),
+                pltpu.VMEM((size, size), F32),
+                pltpu.SemaphoreType.DMA((2,)),
+            ],
+            rest=(u_own, d_own, l_stacks[1]),
+        )
+        rx_all = [rx] + [over_row(rx, s) for s in range(1, rows)]
+        keep, give = kernel(
+            functools.partial(pick_body, rows),
+            (shape(rx.shape, BF), shape(rx.shape, BF)),
+            (child_order, *rx_all),
+            smem=1,
+        )
+        got = over_core(give)
+        w, rs1 = kernel(
+            functools.partial(parent_body, nz),
+            (shape((CORES, size, size), F32), shape((nz, quarter, size + half), BF)),
+            (*scalars, keep, got, parent_panels, l_own, l_sib, ud_part),
+            smem=3,
+            scratch=[pltpu.VMEM((size, size), F32)],
+        )
+        return rx[:CORES], w, rs1
+
+    def no_part(_):
+        return (
+            jnp.zeros((CORES, size, half), BF),
+            jnp.zeros((CORES, size, size), F32),
+            jnp.zeros((nz, quarter, size + half), BF),
+        )
+
+    ub, w, rs1 = lax.cond(child_order[0] >= 0, upper_part, no_part, None)
+    ub_got = over_core(ub[1])
+    upper_blocks = kernel(halves_body, shape((1, 1, size, size), BF), (ub[0], ub_got))
+    lb_own, lb_give, sums = kernel(
+        functools.partial(lower_body, nz),
+        (shape((size, size), BF), shape((size, size), BF), shape((nz, quarter, 2 * size + half), BF)),
+        (*scalars, t_own, t_sib, w, rs1, *l_stacks),
         smem=3,
         scratch=[pltpu.VMEM((size, size), F32)],
-    )
-    lb_own, lb_give, rs2 = kernel(
-        functools.partial(lower_body, nz),
-        (shape((size, size), BF), shape((size, size), BF), shape((nz, quarter, size), BF)),
-        (*scalars, t_own, t_sib, w, *l_all),
-        smem=3,
-        scratch=[pltpu.VMEM((size, size), F32)],
+        rest=(upper_blocks,),
     )
     lb_got = over_core(lb_give)
-    lower_blocks = jnp.where(
-        first, jnp.stack([lb_own, lb_got]), jnp.stack([lb_got, lb_own])
-    )[:, None]
-
-    def reduce(parts, negate):
-        got = [over_z(parts[s], s) for s in range(1, nz)]
-        part = kernel(
-            functools.partial(add_body, negate), shape(parts.shape[1:], BF), (parts, *got)
-        )
-        every = [part] + [over_z(part, s) for s in range(1, nz)]
-        return kernel(join_body, shape((size, parts.shape[2]), BF), tuple(every))
-
-    total1 = reduce(rs1, size)
-    total1_got = over_core(total1)
-    upper_diag, lower_parent, base = kernel(
-        parent_out_body,
+    lower_blocks = kernel(order_body, shape((CORES, 1, size, size), BF), (lb_own, lb_got))
+    got_sums = [over_z(sums[s], s) for s in range(1, nz)]
+    part = kernel(add_body, shape(sums.shape[1:], BF), (sums, *got_sums))
+    every = [part] + [over_z(part, s) for s in range(1, nz)]
+    total = kernel(
+        functools.partial(join_body, nz),
+        shape((size, part.shape[1]), BF),
+        tuple(every),
+        rest=(lower_blocks,),
+    )
+    upper_diag, lower_parent, lower_diag = kernel(
+        out_body,
         (
             shape((1, size, size), F32),
             shape((CORES, size, size), BF),
             shape((CORES, size, size), F32),
         ),
-        (total1, total1_got, upper_diag_inverse, lower_diag_inverse, parent_panels),
-    )
-    total2 = reduce(rs2, 0)
-    lower_diag = kernel(
-        lower_out_body,
-        shape((CORES, size, size), F32),
-        (base, total2, over_core(total2)),
+        (total, over_core(total), upper_diag_inverse, parent_panels, lower_diag_inverse),
     )
     return upper_blocks, upper_diag, lower_blocks, lower_parent, lower_diag
 

time: 86 us -> 76 us (0.88)
  starting transfers between devices: 34.6 us -> 24.3 us
  waiting for transfers between devices: 33.8 us -> 37 us
  between operations: 3.48 us -> 0.87 us
  Pallas kernels: 6.2 us -> 8.49 us
  other arithmetic: 3.49 us -> 1.9 us
    ppermute x18 -> x12, starting transfers between devices: 29.6 us -> 19.3 us  [over_z(): return lax.ppermute(x, 'pcol', [(i, i ^ CORES * s) for i in range(cols)])]
    ppermute x3, waiting for transfers between devices: 0.01 us -> 7.7 us  [over_row(): return lax.ppermute(x, 'prow', [(i, i ^ s) for i in range(rows)])]
    ppermute x18 -> x12, waiting for transfers between devices: 29.7 us -> 24 us  [over_z(): return lax.ppermute(x, 'pcol', [(i, i ^ CORES * s) for i in range(cols)])]
    pallas_call x9 -> x10, Pallas kernels: 6.2 us -> 8.49 us  [kernel(): pl.pallas_call(body, out_shape=out, in_specs=[sm] * smem + [vm] * (len(ar...]
    select_n x5 -> x1, other arithmetic: 2.56 us -> 0.99 us  [near_shards(): l_sib = over_core(jnp.where(first, l_all[1], l_all[0]))]
    ppermute x8 -> x7, waiting for transfers between devices: 4.05 us -> 5.27 us  [over_core(): return lax.ppermute(x, 'pcol', [(i, i ^ 1) for i in range(cols)])]
    unnamed x18 -> x28, local copies, waits for them, and re-layouts: 3.48 us -> 3.2 us
  transfers between devices with their start and end apart: 29 -> 22, of which waited for: 9 -> 13; matrix products, arithmetic and copies ran while one was open for 5% -> 3% of each run, Pallas kernels for 4% -> 7%
where the time goes in v2:
time: 76 us; the launch traced here: 75.8 us
  waiting for transfers between devices  37 us (49%)
  starting transfers between devices  24.3 us (32%)
  Pallas kernels  8.49 us (11%)
  local copies, waits for them, and re-layouts  3.25 us (4%)
  other arithmetic  1.9 us (2%)
  between operations  0.87 us (1%)
    ppermute x12, waiting for transfers between devices, over_z(): return lax.ppermute(x, 'pcol', [(i, i ^ CORES * s) for i in range(cols)])  24 us
    ppermute x12, starting transfers between devices, over_z(): return lax.ppermute(x, 'pcol', [(i, i ^ CORES * s) for i in range(cols)])  19.3 us
    pallas_call x10, Pallas kernels, kernel(): pl.pallas_call(body, out_shape=out, in_specs=[sm] * smem + [vm] * (len(ar...  8.49 us
    ppermute x3, waiting for transfers between devices, over_row(): return lax.ppermute(x, 'prow', [(i, i ^ s) for i in range(rows)])  7.7 us
    ppermute x7, waiting for transfers between devices, over_core(): return lax.ppermute(x, 'pcol', [(i, i ^ 1) for i in range(cols)])  5.27 us
    ppermute x3, starting transfers between devices, over_row(): return lax.ppermute(x, 'prow', [(i, i ^ s) for i in range(rows)])  3.55 us
    unnamed x28, local copies, waits for them, and re-layouts  3.2 us
  transfers between devices with their start and end apart: 22, of which 13 were waited for; matrix products, arithmetic and copies ran while one was open for 3% of the time, Pallas kernels for 7%

profile of v2, /device:TPU:0, one launch (start us, length us, event | category | flops | bytes accessed | tf_op | source)
XLA Modules:
  0.0 75.8 jit_solution(12482590790279939073)
XLA Ops:
  1.2 1.0 %select_bitcast_fusion = (bf16[256,256]{1,0:T(8,128)(2,1)S(1)}, bf16[256,256]{1,0:T(8,128)(2,1)S(1)}) fusion(pred[]{:T(512)S(6)} %eq.5, bf16[2,1,256,256]{3,2,1,0:T(8,128)(2,1)} %param.17), kind=kLoop, calls=%fused_computation.5 | loop fusion | flops 131072 | bytes 524289 | tf_op jit(solution)/shard_map/jit(_where)/select_n | solution.py:293
  2.7 1.1 %collective-permute-done.5 = bf16[256,256]{1,0:T(8,128)(2,1)S(1)} collective-permute-done((bf16[256,256]{1,0:T(8,128)(2,1)}, bf16[256,256]{1,0:T(8,128)(2,1)S(1)}, u32[]{:S(2)}, u32[]{:S(2)}) %collective-permute-start.5) | collective-permute-done | bytes 131104 | tf_op jit(solution)/shard_map/ppermute | solution.py:278
  3.8 0.9 %fusion.1.refs_2_ = bf16[2,256,128]{2,1,0:T(8,128)(2,1)S(1)} fusion(bf16[1,256,256]{2,1,0:T(8,128)(2,1)} %bitcast.26, bf16[1,256,256]{2,1,0:T(8,128)(2,1)S(1)} %bitcast.28, pred[]{:T(512)S(6)} %eq.5), kind=kLoop, calls=%fused_computation.3 | loop fusion | flops 589824 | bytes 393217 | tf_op jit(solution)/shard_map/jit(_where)/select_n | solution.py:296
  4.8 3.0 %collective-permute-start.10 = (bf16[2,256,256]{2,1,0:T(8,128)(2,1)S(1)}, bf16[2,256,256]{2,1,0:T(8,128)(2,1)S(1)}, u32[]{:S(2)}, u32[]{:S(2)}) collective-permute-start(bf16[2,256,256]{2,1,0:T(8,128)(2,1)S(1)} %shard_map.128.refs_0_), channel_id=1, source_target_pairs={{0,2},{1,3},{2,0},{3,1},{4,6},{5,7},{6,4},{7,5},{8,10},{9,11},{10,... | collective-permute-start | bytes 786440 | tf_op jit(solution)/shard_map/ppermute | solution.py:281
  7.9 3.0 %collective-permute-start.7 = (bf16[2,256,128]{2,1,0:T(8,128)(2,1)S(1)}, bf16[2,256,128]{2,1,0:T(8,128)(2,1)S(1)}, u32[]{:S(2)}, u32[]{:S(2)}) collective-permute-start(bf16[2,256,128]{2,1,0:T(8,128)(2,1)S(1)} %fusion.1.refs_2_), channel_id=1, source_target_pairs={{0,4},{1,5},{2,6},{3,7},{4,0},{5,1},{6,2},{7,3},{8,12},{9,13},{10,... | collective-permute-start | bytes 393224 | tf_op jit(solution)/shard_map/ppermute | solution.py:281
  10.9 1.3 %collective-permute-start.8 = (bf16[2,256,128]{2,1,0:T(8,128)(2,1)S(1)}, bf16[2,256,128]{2,1,0:T(8,128)(2,1)S(1)}, u32[]{:S(2)}, u32[]{:S(2)}) collective-permute-start(bf16[2,256,128]{2,1,0:T(8,128)(2,1)S(1)} %fusion.1.refs_2_), channel_id=1, source_target_pairs={{0,6},{1,7},{2,4},{3,5},{4,2},{5,3},{6,0},{7,1},{8,14},{9,15},{10,... | collective-permute-start | bytes 393224 | tf_op jit(solution)/shard_map/ppermute | solution.py:281
  12.9 7.1 %collective-permute-done.6 = bf16[2,256,128]{2,1,0:T(8,128)(2,1)S(1)} collective-permute-done((bf16[2,256,128]{2,1,0:T(8,128)(2,1)S(1)}, bf16[2,256,128]{2,1,0:T(8,128)(2,1)S(1)}, u32[]{:S(2)}, u32[]{:S(2)}) %collective-permute-start.6) | collective-permute-done | bytes 131104 | tf_op jit(solution)/shard_map/ppermute | solution.py:281
  20.1 4.9 %collective-permute-done.8 = bf16[2,256,128]{2,1,0:T(8,128)(2,1)S(1)} collective-permute-done((bf16[2,256,128]{2,1,0:T(8,128)(2,1)S(1)}, bf16[2,256,128]{2,1,0:T(8,128)(2,1)S(1)}, u32[]{:S(2)}, u32[]{:S(2)}) %collective-permute-start.8) | collective-permute-done | bytes 131104 | tf_op jit(solution)/shard_map/ppermute | solution.py:281
  25.1 1.7 %collective-permute-start.13 = (bf16[2,256,256]{2,1,0:T(8,128)(2,1)S(1)}, bf16[2,256,256]{2,1,0:T(8,128)(2,1)S(1)}, u32[]{:S(2)}, u32[]{:S(2)}) collective-permute-start(bf16[2,256,256]{2,1,0:T(8,128)(2,1)S(1)} %shard_map.128.refs_0_), channel_id=1, source_target_pairs={{0,6},{1,7},{2,4},{3,5},{4,2},{5,3},{6,0},{7,1},{8,14},{9,15},{10,... | collective-permute-start | bytes 786440 | tf_op jit(solution)/shard_map/ppermute | solution.py:281
  27.4 16.9 %conditional.1 = (bf16[2,256,128]{2,1,0:T(8,128)(2,1)S(1)}, f32[2,256,256]{2,1,0:T(8,128)S(1)}, bf16[4,64,384]{2,1,0:T(8,128)(2,1)}) conditional(s32[]{:T(128)} %bitcast.1, () %tuple.17, (s32[4,8]{1,0:T(4,128)S(1)}, bf16[8,256,256]{2,1,0:T(8,128)(2,1)S(1)}, bf16[8,256,256]{2,1,0:T(8,128)(2,1)S(1)}, bf16[256,256]{1,0:T(8,128)(2,1)S(1)}, ...), branch_computations={%region_0.1_spmd, %region_1.2_spmd} | conditional | bytes 3408056 | solution.py:363
  27.4 1.8 %branch_1_fun.3 = (bf16[3,256,128]{2,1,0:T(8,128)(2,1)S(1)}, bf16[4,64,128]{2,1,0:T(8,128)(2,1)S(1)}) custom-call(s32[4,8]{1,0:T(4,128)S(1)} %get-tuple-element.32.us.us_ref, bf16[8,256,256]{2,1,0:T(8,128)(2,1)S(1)} %get-tuple-element.33.to, bf16[8,256,256]{2,1,0:T(8,128)(2,1)S(1)} %get-tuple-element.34.ts, bf16[256,256]{1,0:T(8,128)(2,1)S(1)} %get-tuple-element.35.usib, ...), custom_call_target="tpu_custom_call" | custom-call | tf_op jit(solution)/shard_map/cond/branch_1_fun/pallas_call | solution.py:305
  29.2 1.6 %collective-permute-start = (bf16[3,256,128]{2,1,0:T(8,128)(2,1)S(1)}, bf16[3,256,128]{2,1,0:T(8,128)(2,1)S(1)}, u32[]{:S(2)}, u32[]{:S(2)}) collective-permute-start(bf16[3,256,128]{2,1,0:T(8,128)(2,1)S(1)} %get-tuple-element.43.refs_0_), channel_id=1, source_target_pairs={{0,8},{8,0},{16,24},{24,16},{1,9},{9,1},{17,25},{25,17},{2,10},{10... | collective-permute-start | bytes 589832 | tf_op jit(solution)/shard_map/cond/branch_1_fun/ppermute | solution.py:284
  30.8 1.5 %collective-permute-start.1 = (bf16[3,256,128]{2,1,0:T(8,128)(2,1)S(1)}, bf16[3,256,128]{2,1,0:T(8,128)(2,1)S(1)}, u32[]{:S(2)}, u32[]{:S(2)}) collective-permute-start(bf16[3,256,128]{2,1,0:T(8,128)(2,1)S(1)} %get-tuple-element.43.refs_0_), channel_id=1, source_target_pairs={{0,16},{8,24},{16,0},{24,8},{1,17},{9,25},{17,1},{25,9},{2,18},{10... | collective-permute-start | bytes 589832 | tf_op jit(solution)/shard_map/cond/branch_1_fun/ppermute | solution.py:284
  32.8 4.1 %collective-permute-done.refs_1_ = bf16[3,256,128]{2,1,0:T(8,128)(2,1)S(1)} collective-permute-done((bf16[3,256,128]{2,1,0:T(8,128)(2,1)S(1)}, bf16[3,256,128]{2,1,0:T(8,128)(2,1)S(1)}, u32[]{:S(2)}, u32[]{:S(2)}) %collective-permute-start) | collective-permute-done | bytes 196640 | tf_op jit(solution)/shard_map/cond/branch_1_fun/ppermute | solution.py:284
  36.9 3.6 %collective-permute-done.1.refs_2_ = bf16[3,256,128]{2,1,0:T(8,128)(2,1)S(1)} collective-permute-done((bf16[3,256,128]{2,1,0:T(8,128)(2,1)S(1)}, bf16[3,256,128]{2,1,0:T(8,128)(2,1)S(1)}, u32[]{:S(2)}, u32[]{:S(2)}) %collective-permute-start.1) | collective-permute-done | bytes 196640 | tf_op jit(solution)/shard_map/cond/branch_1_fun/ppermute | solution.py:284
  41.2 1.4 %collective-permute-done.3.got_ref = bf16[3,256,128]{2,1,0:T(8,128)(2,1)S(1)} collective-permute-done((bf16[3,256,128]{2,1,0:T(8,128)(2,1)S(1)}, bf16[3,256,128]{2,1,0:T(8,128)(2,1)S(1)}, u32[]{:S(2)}, u32[]{:S(2)}) %collective-permute-start.3) | collective-permute-done | bytes 196640 | tf_op jit(solution)/shard_map/cond/branch_1_fun/ppermute | solution.py:278
  42.6 1.7 %branch_1_fun.5 = (f32[2,256,256]{2,1,0:T(8,128)S(1)}, bf16[4,64,384]{2,1,0:T(8,128)(2,1)}) custom-call(s32[4,8]{1,0:T(4,128)S(1)} %get-tuple-element.32.us.us_ref, s32[8]{0:T(128)S(1)} %get-tuple-element.44.co_ref, s32[2,8]{1,0:T(2,128)S(1)} %get-tuple-element.45.ck_ref, bf16[3,256,128]{2,1,0:T(8,128)(2,1)S(1)} %get-tuple-element.46.keep_ref, ...), custom_call_target="tpu_custom_call" | custom-call | tf_op jit(solution)/shard_map/cond/branch_1_fun/pallas_call | solution.py:305
  44.6 1.1 %collective-permute-done.11.got_ref = bf16[256,128]{1,0:T(8,128)(2,1)S(1)} collective-permute-done((bf16[256,128]{1,0:T(8,128)(2,1)S(1)}, bf16[256,128]{1,0:T(8,128)(2,1)S(1)}, u32[]{:S(2)}, u32[]{:S(2)}) %collective-permute-start.11) | collective-permute-done | bytes 65568 | tf_op jit(solution)/shard_map/ppermute | solution.py:278
  46.4 0.9 %copy-done.1 = bf16[1,1,256,256]{3,2,1,0:T(8,128)(2,1)S(1)} copy-done((bf16[1,1,256,256]{3,2,1,0:T(8,128)(2,1)S(1)}, bf16[1,1,256,256]{3,2,1,0:T(8,128)(2,1)}, u32[]{:S(2)}) %copy-start.1) | copy-done | bytes 131096
  47.3 1.7 %shard_map.130 = (bf16[256,256]{1,0:T(8,128)(2,1)S(1)}, bf16[256,256]{1,0:T(8,128)(2,1)S(1)}, bf16[4,64,640]{2,1,0:T(8,128)(2,1)S(1)}) custom-call(s32[4,8]{1,0:T(4,128)S(1)} %copy-done.11, s32[8]{0:T(128)S(1)} %copy-done.12, s32[2,8]{1,0:T(2,128)S(1)} %copy-done.13, bf16[8,256,256]{2,1,0:T(8,128)(2,1)S(1)} %bitcast.23, ...), custom_call_target="tpu_custom_call" | custom-call | tf_op jit(solution)/shard_map/pallas_call | solution.py:305
  49.0 3.3 %collective-permute-start.14 = (bf16[64,640]{1,0:T(8,128)(2,1)S(1)}, bf16[64,640]{1,0:T(8,128)(2,1)S(1)}, u32[]{:S(2)}, u32[]{:S(2)}) collective-permute-start(bf16[64,640]{1,0:T(8,128)(2,1)S(1)} %get-tuple-element.82), channel_id=1, source_target_pairs={{0,2},{1,3},{2,0},{3,1},{4,6},{5,7},{6,4},{7,5},{8,10},{9,11},{10,... | collective-permute-start | bytes 245768 | tf_op jit(solution)/shard_map/ppermute | solution.py:281
  52.3 1.1 %collective-permute-start.15 = (bf16[64,640]{1,0:T(8,128)(2,1)S(1)}, bf16[64,640]{1,0:T(8,128)(2,1)S(1)}, u32[]{:S(2)}, u32[]{:S(2)}) collective-permute-start(bf16[64,640]{1,0:T(8,128)(2,1)S(1)} %get-tuple-element.81), channel_id=1, source_target_pairs={{0,4},{1,5},{2,6},{3,7},{4,0},{5,1},{6,2},{7,3},{8,12},{9,13},{10,... | collective-permute-start | bytes 245768 | tf_op jit(solution)/shard_map/ppermute | solution.py:281
  53.4 1.4 %collective-permute-start.16 = (bf16[64,640]{1,0:T(8,128)(2,1)S(1)}, bf16[64,640]{1,0:T(8,128)(2,1)S(1)}, u32[]{:S(2)}, u32[]{:S(2)}) collective-permute-start(bf16[64,640]{1,0:T(8,128)(2,1)S(1)} %get-tuple-element.80), channel_id=1, source_target_pairs={{0,6},{1,7},{2,4},{3,5},{4,2},{5,3},{6,0},{7,1},{8,14},{9,15},{10,... | collective-permute-start | bytes 245768 | tf_op jit(solution)/shard_map/ppermute | solution.py:281
  55.0 6.7 %collective-permute-done.15.refs_1_ = bf16[64,640]{1,0:T(8,128)(2,1)S(1)} collective-permute-done((bf16[64,640]{1,0:T(8,128)(2,1)S(1)}, bf16[64,640]{1,0:T(8,128)(2,1)S(1)}, u32[]{:S(2)}, u32[]{:S(2)}) %collective-permute-start.15) | collective-permute-done | bytes 81952 | tf_op jit(solution)/shard_map/ppermute | solution.py:281
  61.7 1.5 %collective-permute-start.17 = (bf16[64,640]{1,0:T(8,128)(2,1)S(1)}, bf16[64,640]{1,0:T(8,128)(2,1)S(1)}, u32[]{:S(2)}, u32[]{:S(2)}) collective-permute-start(bf16[64,640]{1,0:T(8,128)(2,1)S(1)} %shard_map.131.refs_0_), channel_id=1, source_target_pairs={{0,2},{1,3},{2,0},{3,1},{4,6},{5,7},{6,4},{7,5},{8,10},{9,11},{10,... | collective-permute-start | bytes 245768 | tf_op jit(solution)/shard_map/ppermute | solution.py:281
  63.3 1.2 %collective-permute-start.18 = (bf16[64,640]{1,0:T(8,128)(2,1)S(1)}, bf16[64,640]{1,0:T(8,128)(2,1)S(1)}, u32[]{:S(2)}, u32[]{:S(2)}) collective-permute-start(bf16[64,640]{1,0:T(8,128)(2,1)S(1)} %shard_map.131.refs_0_), channel_id=1, source_target_pairs={{0,4},{1,5},{2,6},{3,7},{4,0},{5,1},{6,2},{7,3},{8,12},{9,13},{10,... | collective-permute-start | bytes 245768 | tf_op jit(solution)/shard_map/ppermute | solution.py:281
  64.5 1.7 %collective-permute-start.19 = (bf16[64,640]{1,0:T(8,128)(2,1)S(1)}, bf16[64,640]{1,0:T(8,128)(2,1)S(1)}, u32[]{:S(2)}, u32[]{:S(2)}) collective-permute-start(bf16[64,640]{1,0:T(8,128)(2,1)S(1)} %shard_map.131.refs_0_), channel_id=1, source_target_pairs={{0,6},{1,7},{2,4},{3,5},{4,2},{5,3},{6,0},{7,1},{8,14},{9,15},{10,... | collective-permute-start | bytes 245768 | tf_op jit(solution)/shard_map/ppermute | solution.py:281
  66.2 0.7 shard_map.132.refs_4_
  67.1 4.8 %collective-permute-done.18.refs_2_ = bf16[64,640]{1,0:T(8,128)(2,1)S(1)} collective-permute-done((bf16[64,640]{1,0:T(8,128)(2,1)S(1)}, bf16[64,640]{1,0:T(8,128)(2,1)S(1)}, u32[]{:S(2)}, u32[]{:S(2)}) %collective-permute-start.18) | collective-permute-done | bytes 81952 | tf_op jit(solution)/shard_map/ppermute | solution.py:281
  71.9 0.9 %copy-done = bf16[2,1,256,256]{3,2,1,0:T(8,128)(2,1)S(1)} copy-done((bf16[2,1,256,256]{3,2,1,0:T(8,128)(2,1)S(1)}, bf16[2,1,256,256]{3,2,1,0:T(8,128)(2,1)}, u32[]{:S(2)}) %copy-start) | copy-done | bytes 262168
  73.0 1.6 %collective-permute-done.21.got_ref = bf16[256,640]{1,0:T(8,128)(2,1)S(1)} collective-permute-done((bf16[256,640]{1,0:T(8,128)(2,1)S(1)}, bf16[256,640]{1,0:T(8,128)(2,1)S(1)}, u32[]{:S(2)}, u32[]{:S(2)}) %collective-permute-start.21) | collective-permute-done | bytes 327712 | tf_op jit(solution)/shard_map/ppermute | solution.py:278
  74.6 1.2 %shard_map.134 = (f32[1,256,256]{2,1,0:T(8,128)}, bf16[2,256,256]{2,1,0:T(8,128)(2,1)}, f32[2,256,256]{2,1,0:T(8,128)}) custom-call(bf16[256,640]{1,0:T(8,128)(2,1)S(1)} %shard_map.133.own_ref, bf16[256,640]{1,0:T(8,128)(2,1)S(1)} %collective-permute-done.21.got_ref, f32[1,256,256]{2,1,0:T(8,128)S(1)} %copy-done.7, bf16[2,256,256]{2,1,0:T(8,128)(2,1)S(1)} %copy-done.9, ...), custom_call_target="tpu_custom_call" | custom-call | tf_op jit(solution)/shard_map/pallas_call | solution.py:305
  (56 shorter events, 5.3 us)
Async XLA Ops:
  0.6 26.1 %copy-start.3 = (bf16[1,8,256,256]{3,2,1,0:T(8,128)(2,1)S(1)}, bf16[1,8,256,256]{3,2,1,0:T(8,128)(2,1)}, u32[]{:S(2)}) copy-start(bf16[1,8,256,256]{3,2,1,0:T(8,128)(2,1)} %param.11) | copy-start | bytes 3145732
  0.6 26.1 %collective-permute-start.4 = (bf16[8,256,256]{2,1,0:T(8,128)(2,1)}, bf16[8,256,256]{2,1,0:T(8,128)(2,1)S(1)}, u32[]{:S(2)}, u32[]{:S(2)}) collective-permute-start(bf16[8,256,256]{2,1,0:T(8,128)(2,1)} %bitcast.21), channel_id=1, source_target_pairs={{0,1},{1,0},{2,3},{3,2},{4,5},{5,4},{6,7},{7,6},{8,9},{9,8},{10,11... | collective-permute-start | bytes 3145736 | tf_op jit(solution)/shard_map/ppermute | solution.py:278
  1.2 2.7 %collective-permute-start.5 = (bf16[256,256]{1,0:T(8,128)(2,1)}, bf16[256,256]{1,0:T(8,128)(2,1)S(1)}, u32[]{:S(2)}, u32[]{:S(2)}) collective-permute-start(bf16[256,256]{1,0:T(8,128)(2,1)} %bitcast.25), channel_id=1, source_target_pairs={{0,1},{1,0},{2,3},{3,2},{4,5},{5,4},{6,7},{7,6},{8,9},{9,8},{10,11... | collective-permute-start | bytes 393224 | tf_op jit(solution)/shard_map/ppermute | solution.py:278
  2.2 2.5 %collective-permute-start.9 = (bf16[256,256]{1,0:T(8,128)(2,1)S(1)}, bf16[256,256]{1,0:T(8,128)(2,1)S(1)}, u32[]{:S(2)}, u32[]{:S(2)}) collective-permute-start(bf16[256,256]{1,0:T(8,128)(2,1)S(1)} %get-tuple-element.83), channel_id=1, source_target_pairs={{0,1},{1,0},{2,3},{3,2},{4,5},{5,4},{6,7},{7,6},{8,9},{9,8},{10,11... | collective-permute-start | bytes 393224 | tf_op jit(solution)/shard_map/ppermute | solution.py:278
  4.8 22.0 %copy-start.6 = (f32[1,256,256]{2,1,0:T(8,128)S(1)}, f32[1,256,256]{2,1,0:T(8,128)}, u32[]{:S(2)}) copy-start(f32[1,256,256]{2,1,0:T(8,128)} %d_ref.1) | copy-start | bytes 786436
  4.8 22.0 %copy-start.8 = (bf16[2,256,256]{2,1,0:T(8,128)(2,1)S(1)}, bf16[2,256,256]{2,1,0:T(8,128)(2,1)}, u32[]{:S(2)}) copy-start(bf16[2,256,256]{2,1,0:T(8,128)(2,1)} %pp_ref.1) | copy-start | bytes 786436
  4.8 21.9 %collective-permute-start.10 = (bf16[2,256,256]{2,1,0:T(8,128)(2,1)S(1)}, bf16[2,256,256]{2,1,0:T(8,128)(2,1)S(1)}, u32[]{:S(2)}, u32[]{:S(2)}) collective-permute-start(bf16[2,256,256]{2,1,0:T(8,128)(2,1)S(1)} %shard_map.128.refs_0_), channel_id=1, source_target_pairs={{0,2},{1,3},{2,0},{3,1},{4,6},{5,7},{6,4},{7,5},{8,10},{9,11},{10,... | collective-permute-start | bytes 786440 | tf_op jit(solution)/shard_map/ppermute | solution.py:281
  7.8 12.2 %collective-permute-start.6 = (bf16[2,256,128]{2,1,0:T(8,128)(2,1)S(1)}, bf16[2,256,128]{2,1,0:T(8,128)(2,1)S(1)}, u32[]{:S(2)}, u32[]{:S(2)}) collective-permute-start(bf16[2,256,128]{2,1,0:T(8,128)(2,1)S(1)} %fusion.1.refs_2_), channel_id=1, source_target_pairs={{0,2},{1,3},{2,0},{3,1},{4,6},{5,7},{6,4},{7,5},{8,10},{9,11},{10,... | collective-permute-start | bytes 393224 | tf_op jit(solution)/shard_map/ppermute | solution.py:281
  7.9 12.2 %collective-permute-start.7 = (bf16[2,256,128]{2,1,0:T(8,128)(2,1)S(1)}, bf16[2,256,128]{2,1,0:T(8,128)(2,1)S(1)}, u32[]{:S(2)}, u32[]{:S(2)}) collective-permute-start(bf16[2,256,128]{2,1,0:T(8,128)(2,1)S(1)} %fusion.1.refs_2_), channel_id=1, source_target_pairs={{0,4},{1,5},{2,6},{3,7},{4,0},{5,1},{6,2},{7,3},{8,12},{9,13},{10,... | collective-permute-start | bytes 393224 | tf_op jit(solution)/shard_map/ppermute | solution.py:281
  10.9 14.2 %collective-permute-start.8 = (bf16[2,256,128]{2,1,0:T(8,128)(2,1)S(1)}, bf16[2,256,128]{2,1,0:T(8,128)(2,1)S(1)}, u32[]{:S(2)}, u32[]{:S(2)}) collective-permute-start(bf16[2,256,128]{2,1,0:T(8,128)(2,1)S(1)} %fusion.1.refs_2_), channel_id=1, source_target_pairs={{0,6},{1,7},{2,4},{3,5},{4,2},{5,3},{6,0},{7,1},{8,14},{9,15},{10,... | collective-permute-start | bytes 393224 | tf_op jit(solution)/shard_map/ppermute | solution.py:281
  12.9 13.8 %copy-start.11 = (s32[4,8]{1,0:T(4,128)S(1)}, s32[4,8]{1,0:T(4,128)}, u32[]{:S(2)}) copy-start(s32[4,8]{1,0:T(4,128)} %us_ref.1) | copy-start | bytes 388
  12.9 13.8 %copy-start.13 = (s32[2,8]{1,0:T(2,128)S(1)}, s32[2,8]{1,0:T(2,128)}, u32[]{:S(2)}) copy-start(s32[2,8]{1,0:T(2,128)} %ck_ref.1) | copy-start | bytes 196
  25.1 21.3 %collective-permute-start.12 = (bf16[2,256,256]{2,1,0:T(8,128)(2,1)S(1)}, bf16[2,256,256]{2,1,0:T(8,128)(2,1)S(1)}, u32[]{:S(2)}, u32[]{:S(2)}) collective-permute-start(bf16[2,256,256]{2,1,0:T(8,128)(2,1)S(1)} %shard_map.128.refs_0_), channel_id=1, source_target_pairs={{0,4},{1,5},{2,6},{3,7},{4,0},{5,1},{6,2},{7,3},{8,12},{9,13},{10,... | collective-permute-start | bytes 786440 | tf_op jit(solution)/shard_map/ppermute | solution.py:281
  25.1 21.3 %collective-permute-start.13 = (bf16[2,256,256]{2,1,0:T(8,128)(2,1)S(1)}, bf16[2,256,256]{2,1,0:T(8,128)(2,1)S(1)}, u32[]{:S(2)}, u32[]{:S(2)}) collective-permute-start(bf16[2,256,256]{2,1,0:T(8,128)(2,1)S(1)} %shard_map.128.refs_0_), channel_id=1, source_target_pairs={{0,6},{1,7},{2,4},{3,5},{4,2},{5,3},{6,0},{7,1},{8,14},{9,15},{10,... | collective-permute-start | bytes 786440 | tf_op jit(solution)/shard_map/ppermute | solution.py:281
  29.2 7.7 %collective-permute-start = (bf16[3,256,128]{2,1,0:T(8,128)(2,1)S(1)}, bf16[3,256,128]{2,1,0:T(8,128)(2,1)S(1)}, u32[]{:S(2)}, u32[]{:S(2)}) collective-permute-start(bf16[3,256,128]{2,1,0:T(8,128)(2,1)S(1)} %get-tuple-element.43.refs_0_), channel_id=1, source_target_pairs={{0,8},{8,0},{16,24},{24,16},{1,9},{9,1},{17,25},{25,17},{2,10},{10... | collective-permute-start | bytes 589832 | tf_op jit(solution)/shard_map/cond/branch_1_fun/ppermute | solution.py:284
  30.8 9.7 %collective-permute-start.1 = (bf16[3,256,128]{2,1,0:T(8,128)(2,1)S(1)}, bf16[3,256,128]{2,1,0:T(8,128)(2,1)S(1)}, u32[]{:S(2)}, u32[]{:S(2)}) collective-permute-start(bf16[3,256,128]{2,1,0:T(8,128)(2,1)S(1)} %get-tuple-element.43.refs_0_), channel_id=1, source_target_pairs={{0,16},{8,24},{16,0},{24,8},{1,17},{9,25},{17,1},{25,9},{2,18},{10... | collective-permute-start | bytes 589832 | tf_op jit(solution)/shard_map/cond/branch_1_fun/ppermute | solution.py:284
  32.3 8.2 %collective-permute-start.2 = (bf16[3,256,128]{2,1,0:T(8,128)(2,1)S(1)}, bf16[3,256,128]{2,1,0:T(8,128)(2,1)S(1)}, u32[]{:S(2)}, u32[]{:S(2)}) collective-permute-start(bf16[3,256,128]{2,1,0:T(8,128)(2,1)S(1)} %get-tuple-element.43.refs_0_), channel_id=1, source_target_pairs={{0,24},{8,16},{16,8},{24,0},{1,25},{9,17},{17,9},{25,1},{2,26},{10... | collective-permute-start | bytes 589832 | tf_op jit(solution)/shard_map/cond/branch_1_fun/ppermute | solution.py:284
  41.1 1.5 %collective-permute-start.3 = (bf16[3,256,128]{2,1,0:T(8,128)(2,1)S(1)}, bf16[3,256,128]{2,1,0:T(8,128)(2,1)S(1)}, u32[]{:S(2)}, u32[]{:S(2)}) collective-permute-start(bf16[3,256,128]{2,1,0:T(8,128)(2,1)S(1)} %get-tuple-element.47), channel_id=1, source_target_pairs={{0,1},{1,0},{2,3},{3,2},{4,5},{5,4},{6,7},{7,6},{8,9},{9,8},{10,11... | collective-permute-start | bytes 589832 | tf_op jit(solution)/shard_map/cond/branch_1_fun/ppermute | solution.py:278
  44.3 2.0 %copy-start.5 = (bf16[2,256,256]{2,1,0:T(8,128)(2,1)S(1)}, bf16[2,256,256]{2,1,0:T(8,128)(2,1)}, u32[]{:S(2)}) copy-start(bf16[2,256,256]{2,1,0:T(8,128)(2,1)} %copy-done.4) | copy-start | bytes 786436
  44.3 2.0 %copy-start.10 = (bf16[4,64,384]{2,1,0:T(8,128)(2,1)S(1)}, bf16[4,64,384]{2,1,0:T(8,128)(2,1)}, u32[]{:S(2)}) copy-start(bf16[4,64,384]{2,1,0:T(8,128)(2,1)} %get-tuple-element.71.rs1_ref) | copy-start | bytes 589828
  44.4 1.3 %collective-permute-start.11 = (bf16[256,128]{1,0:T(8,128)(2,1)S(1)}, bf16[256,128]{1,0:T(8,128)(2,1)S(1)}, u32[]{:S(2)}, u32[]{:S(2)}) collective-permute-start(bf16[256,128]{1,0:T(8,128)(2,1)S(1)} %get-tuple-element.85), channel_id=1, source_target_pairs={{0,1},{1,0},{2,3},{3,2},{4,5},{5,4},{6,7},{7,6},{8,9},{9,8},{10,11... | collective-permute-start | bytes 196616 | tf_op jit(solution)/shard_map/ppermute | solution.py:278
  49.0 6.0 %collective-permute-start.14 = (bf16[64,640]{1,0:T(8,128)(2,1)S(1)}, bf16[64,640]{1,0:T(8,128)(2,1)S(1)}, u32[]{:S(2)}, u32[]{:S(2)}) collective-permute-start(bf16[64,640]{1,0:T(8,128)(2,1)S(1)} %get-tuple-element.82), channel_id=1, source_target_pairs={{0,2},{1,3},{2,0},{3,1},{4,6},{5,7},{6,4},{7,5},{8,10},{9,11},{10,... | collective-permute-start | bytes 245768 | tf_op jit(solution)/shard_map/ppermute | solution.py:281
  52.3 9.4 %collective-permute-start.15 = (bf16[64,640]{1,0:T(8,128)(2,1)S(1)}, bf16[64,640]{1,0:T(8,128)(2,1)S(1)}, u32[]{:S(2)}, u32[]{:S(2)}) collective-permute-start(bf16[64,640]{1,0:T(8,128)(2,1)S(1)} %get-tuple-element.81), channel_id=1, source_target_pairs={{0,4},{1,5},{2,6},{3,7},{4,0},{5,1},{6,2},{7,3},{8,12},{9,13},{10,... | collective-permute-start | bytes 245768 | tf_op jit(solution)/shard_map/ppermute | solution.py:281
  53.4 8.3 %collective-permute-start.16 = (bf16[64,640]{1,0:T(8,128)(2,1)S(1)}, bf16[64,640]{1,0:T(8,128)(2,1)S(1)}, u32[]{:S(2)}, u32[]{:S(2)}) collective-permute-start(bf16[64,640]{1,0:T(8,128)(2,1)S(1)} %get-tuple-element.80), channel_id=1, source_target_pairs={{0,6},{1,7},{2,4},{3,5},{4,2},{5,3},{6,0},{7,1},{8,14},{9,15},{10,... | collective-permute-start | bytes 245768 | tf_op jit(solution)/shard_map/ppermute | solution.py:281
  54.8 11.4 %collective-permute-start.20 = (bf16[256,256]{1,0:T(8,128)(2,1)S(1)}, bf16[256,256]{1,0:T(8,128)(2,1)S(1)}, u32[]{:S(2)}, u32[]{:S(2)}) collective-permute-start(bf16[256,256]{1,0:T(8,128)(2,1)S(1)} %get-tuple-element.75), channel_id=1, source_target_pairs={{0,1},{1,0},{2,3},{3,2},{4,5},{5,4},{6,7},{7,6},{8,9},{9,8},{10,11... | collective-permute-start | bytes 393224 | tf_op jit(solution)/shard_map/ppermute | solution.py:278
  61.7 5.4 %collective-permute-start.17 = (bf16[64,640]{1,0:T(8,128)(2,1)S(1)}, bf16[64,640]{1,0:T(8,128)(2,1)S(1)}, u32[]{:S(2)}, u32[]{:S(2)}) collective-permute-start(bf16[64,640]{1,0:T(8,128)(2,1)S(1)} %shard_map.131.refs_0_), channel_id=1, source_target_pairs={{0,2},{1,3},{2,0},{3,1},{4,6},{5,7},{6,4},{7,5},{8,10},{9,11},{10,... | collective-permute-start | bytes 245768 | tf_op jit(solution)/shard_map/ppermute | solution.py:281
  63.3 8.6 %collective-permute-start.18 = (bf16[64,640]{1,0:T(8,128)(2,1)S(1)}, bf16[64,640]{1,0:T(8,128)(2,1)S(1)}, u32[]{:S(2)}, u32[]{:S(2)}) collective-permute-start(bf16[64,640]{1,0:T(8,128)(2,1)S(1)} %shard_map.131.refs_0_), channel_id=1, source_target_pairs={{0,4},{1,5},{2,6},{3,7},{4,0},{5,1},{6,2},{7,3},{8,12},{9,13},{10,... | collective-permute-start | bytes 245768 | tf_op jit(solution)/shard_map/ppermute | solution.py:281
  64.5 7.4 %collective-permute-start.19 = (bf16[64,640]{1,0:T(8,128)(2,1)S(1)}, bf16[64,640]{1,0:T(8,128)(2,1)S(1)}, u32[]{:S(2)}, u32[]{:S(2)}) collective-permute-start(bf16[64,640]{1,0:T(8,128)(2,1)S(1)} %shard_map.131.refs_0_), channel_id=1, source_target_pairs={{0,6},{1,7},{2,4},{3,5},{4,2},{5,3},{6,0},{7,1},{8,14},{9,15},{10,... | collective-permute-start | bytes 245768 | tf_op jit(solution)/shard_map/ppermute | solution.py:281
  66.2 8.4 %copy-start.2 = (f32[2,256,256]{2,1,0:T(8,128)S(1)}, f32[2,256,256]{2,1,0:T(8,128)}, u32[]{:S(2)}) copy-start(f32[2,256,256]{2,1,0:T(8,128)} %ld_ref.1) | copy-start | bytes 1572868
  72.8 1.7 %copy-start.7 = (f32[1,256,256]{2,1,0:T(8,128)S(1)}, f32[1,256,256]{2,1,0:T(8,128)}, u32[]{:S(2)}) copy-start(f32[1,256,256]{2,1,0:T(8,128)} %d_ref.1) | copy-start | bytes 786436
  72.8 1.7 %copy-start.9 = (bf16[2,256,256]{2,1,0:T(8,128)(2,1)S(1)}, bf16[2,256,256]{2,1,0:T(8,128)(2,1)}, u32[]{:S(2)}) copy-start(bf16[2,256,256]{2,1,0:T(8,128)(2,1)} %pp_ref.1) | copy-start | bytes 786436
  72.9 1.7 %collective-permute-start.21 = (bf16[256,640]{1,0:T(8,128)(2,1)S(1)}, bf16[256,640]{1,0:T(8,128)(2,1)S(1)}, u32[]{:S(2)}, u32[]{:S(2)}) collective-permute-start(bf16[256,640]{1,0:T(8,128)(2,1)S(1)} %shard_map.133.own_ref), channel_id=1, source_target_pairs={{0,1},{1,0},{2,3},{3,2},{4,5},{5,4},{6,7},{7,6},{8,9},{9,8},{10,11... | collective-permute-start | bytes 983048 | tf_op jit(solution)/shard_map/ppermute | solution.py:278
  (4 other events, 3.2 us)

commit v3 on v2

--- a/solution.py
+++ b/solution.py
@@ -101,15 +101,12 @@
     return lax.axis_index("prow"), col // CORES, col % CORES
 
 
-def upper_body(nz, us_ref, to_ref, ts_ref, us_full_ref, uo_hbm, d_hbm, *refs):
-    stacks, (rx_ref, ud_ref, xs, uo_ref, d_ref, sems) = refs[:nz], refs[-6:]
+def upper_body(nz, us_ref, to_ref, ts_ref, *refs):
+    pairs = [(refs[2 * s], refs[2 * s + 1]) for s in range(nz)]
+    d_hbm, rx_ref, ud_ref, xs, d_ref, sem = refs[2 * nz :]
     row, z, c = place()
-    copies = [
-        pltpu.make_async_copy(uo_hbm, uo_ref, sems.at[0]),
-        pltpu.make_async_copy(d_hbm, d_ref, sems.at[1]),
-    ]
-    for copy in copies:
-        copy.start()
+    copy = pltpu.make_async_copy(d_hbm, d_ref, sem)
+    copy.start()
     half = xs.shape[1]
     quarter = xs.shape[0] // nz
     acc = [None, None]
@@ -117,14 +114,14 @@
         for q in range(CORES):
             i = CORES * (z ^ s) + (c if q == 0 else 1 - c)
             flag = us_ref[row, i].astype(F32).astype(BF)
-            piece = stacks[s][q] * flag
+            panel = pairs[s][q][...]
+            piece = jnp.where(c == 0, panel[:, :half], panel[:, half:]) * flag
             for p, t_ref in enumerate((to_ref, ts_ref)):
                 prod = dot(t_ref[i], piece)
                 acc[p] = prod if acc[p] is None else acc[p] + prod
-    for copy in copies:
-        copy.wait()
+    copy.wait()
     x = None
-    for p, u_ref in enumerate((uo_ref, us_full_ref)):
+    for p, u_ref in enumerate(pairs[0]):
         j = CORES * z + (c if p == 0 else 1 - c)
         flag = us_ref[row, j].astype(F32)
         block = (-(flag * acc[p])).astype(BF)
@@ -211,18 +208,15 @@
         refs[-1][i] = ref[...]
 
 
-def halves_body(own_ref, got_ref, out_ref):
+def order_body(u_own_ref, u_got_ref, l_own_ref, l_got_ref, d_ref, ub_ref, lb_ref, d_out_ref):
     _, _, c = place()
-    half = own_ref.shape[1]
-    own, got = own_ref[...], got_ref[...]
-    out_ref[0, 0, :, :half] = jnp.where(c == 0, own, got)
-    out_ref[0, 0, :, half:] = jnp.where(c == 0, got, own)
-
-
-def order_body(own_ref, got_ref, out_ref):
-    _, _, c = place()
-    out_ref[c, 0] = own_ref[...]
-    out_ref[1 - c, 0] = got_ref[...]
+    half = u_own_ref.shape[1]
+    own, got = u_own_ref[...], u_got_ref[...]
+    ub_ref[0, 0, :, :half] = jnp.where(c == 0, own, got)
+    ub_ref[0, 0, :, half:] = jnp.where(c == 0, got, own)
+    lb_ref[c, 0] = l_own_ref[...]
+    lb_ref[1 - c, 0] = l_got_ref[...]
+    d_out_ref[...] = d_ref[...]
 
 
 def add_body(own_ref, *refs):
@@ -292,9 +286,8 @@
     l_own = jnp.where(first, l_all[0], l_all[1])
     l_sib = over_core(jnp.where(first, l_all[1], l_all[0]))
     t_sib = over_core(t_own)
-    u_both = jnp.stack([u_own, u_sib])
-    u_stack = jnp.where(first, u_both[:, :, :half], u_both[:, :, half:])
-    u_all = [u_stack] + [over_z(u_stack, s) for s in range(1, nz)]
+    u_far = [over_z(u_own, s) for s in range(1, nz)]
+    u_all = [(u_own, u_sib)] + [(u, over_core(u)) for u in u_far]
 
     vm = pl.BlockSpec(memory_space=pltpu.VMEM)
     sm = pl.BlockSpec(memory_space=pltpu.SMEM)
@@ -311,30 +304,25 @@
             compiler_params=pltpu.CompilerParams(vmem_limit_bytes=24 * 1024 * 1024),
         )(*args, *rest)
 
-    def upper(us, to, ts, usib, *refs):
-        stacks, uo, d = refs[:nz], refs[nz], refs[nz + 1]
-        upper_body(nz, us, to, ts, usib, uo, d, *stacks, *refs[-6:])
-
     l_stack = kernel(
-        functools.partial(pair_body, 2), shape((CORES, size, size), BF), (l_own, l_sib), rest=(u_stack,)
-    )
-    l_later = lax.optimization_barrier((l_stack, *u_all[1:]))[0]
-    l_stacks = [l_stack, over_z(l_stack, 1)] + [over_z(l_later, s) for s in range(2, nz)]
+        functools.partial(pair_body, 2), shape((CORES, size, size), BF), (l_own, l_sib)
+    )
+    l_later = lax.optimization_barrier((l_stack, *u_far))[0]
+    l_far = [over_z(l_later, s) for s in range(2, nz)]
     scalars = (upper_structure, child_order, child_keep)
 
     def upper_part(_):
         rx, ud_part = kernel(
-            upper,
+            functools.partial(upper_body, nz),
             (shape((CORES + 1, size, half), BF), shape((nz, quarter, half), BF)),
-            (upper_structure, t_own, t_sib, u_sib, *u_all),
+            (upper_structure, t_own, t_sib, *[u for pair in u_all for u in pair]),
             smem=1,
             scratch=[
                 pltpu.VMEM((size, half), F32),
-                pltpu.VMEM((size, size), BF),
                 pltpu.VMEM((size, size), F32),
-                pltpu.SemaphoreType.DMA((2,)),
+                pltpu.SemaphoreType.DMA,
             ],
-            rest=(u_own, d_own, l_stacks[1]),
+            rest=(d_own,),
         )
         rx_all = [rx] + [over_row(rx, s) for s in range(1, rows)]
         keep, give = kernel(
@@ -351,28 +339,36 @@
             smem=3,
             scratch=[pltpu.VMEM((size, size), F32)],
         )
-        return rx[:CORES], w, rs1
+        l_next = lax.optimization_barrier((l_stack, rx_all[1]))[0]
+        return rx[:CORES], w, rs1, over_z(l_next, 1)
 
     def no_part(_):
         return (
             jnp.zeros((CORES, size, half), BF),
             jnp.zeros((CORES, size, size), F32),
             jnp.zeros((nz, quarter, size + half), BF),
+            jnp.zeros((CORES, size, size), BF),
         )
 
-    ub, w, rs1 = lax.cond(child_order[0] >= 0, upper_part, no_part, None)
+    ub, w, rs1, l_near = lax.cond(child_order[0] >= 0, upper_part, no_part, None)
     ub_got = over_core(ub[1])
-    upper_blocks = kernel(halves_body, shape((1, 1, size, size), BF), (ub[0], ub_got))
     lb_own, lb_give, sums = kernel(
         functools.partial(lower_body, nz),
         (shape((size, size), BF), shape((size, size), BF), shape((nz, quarter, 2 * size + half), BF)),
-        (*scalars, t_own, t_sib, w, rs1, *l_stacks),
+        (*scalars, t_own, t_sib, w, rs1, l_stack, l_near, *l_far),
         smem=3,
         scratch=[pltpu.VMEM((size, size), F32)],
-        rest=(upper_blocks,),
     )
     lb_got = over_core(lb_give)
-    lower_blocks = kernel(order_body, shape((CORES, 1, size, size), BF), (lb_own, lb_got))
+    upper_blocks, lower_blocks, diag = kernel(
+        order_body,
+        (
+            shape((1, 1, size, size), BF),
+            shape((CORES, 1, size, size), BF),
+            shape((CORES, size, size), F32),
+        ),
+        (ub[0], ub_got, lb_own, lb_got, lower_diag_inverse),
+    )
     got_sums = [over_z(sums[s], s) for s in range(1, nz)]
     part = kernel(add_body, shape(sums.shape[1:], BF), (sums, *got_sums))
     every = [part] + [over_z(part, s) for s in range(1, nz)]
@@ -380,7 +376,7 @@
         functools.partial(join_body, nz),
         shape((size, part.shape[1]), BF),
         tuple(every),
-        rest=(lower_blocks,),
+        rest=(diag,),
     )
     upper_diag, lower_parent, lower_diag = kernel(
         out_body,
@@ -389,7 +385,7 @@
             shape((CORES, size, size), BF),
             shape((CORES, size, size), F32),
         ),
-        (total, over_core(total), upper_diag_inverse, parent_panels, lower_diag_inverse),
+        (total, over_core(total), upper_diag_inverse, parent_panels, diag),
     )
     return upper_blocks, upper_diag, lower_blocks, lower_parent, lower_diag
 

time: 76 us -> 69.4 us (0.913)
  waiting for transfers between devices: 37 us -> 33.6 us
  local copies, waits for them, and re-layouts: 3.25 us -> 1.1 us
  other arithmetic: 1.9 us -> 0.99 us
    ppermute x12, waiting for transfers between devices: 24 us -> 20.2 us  [over_z(): return lax.ppermute(x, 'pcol', [(i, i ^ CORES * s) for i in range(cols)])]
    unnamed x28 -> x14, local copies, waits for them, and re-layouts: 3.2 us -> 1.05 us
    ppermute x3, waiting for transfers between devices: 7.7 us -> 8.79 us  [over_row(): return lax.ppermute(x, 'prow', [(i, i ^ s) for i in range(rows)])]
    select_n x1 -> x0, other arithmetic: 0.91 us -> none  [near_shards(): u_stack = jnp.where(first, u_both[:, :, :half], u_both[:, :, half:])]
    ppermute x7 -> x10, waiting for transfers between devices: 5.27 us -> 4.58 us  [over_core(): return lax.ppermute(x, 'pcol', [(i, i ^ 1) for i in range(cols)])]
    pallas_call x10 -> x9, Pallas kernels: 8.49 us -> 8.53 us  [kernel(): pl.pallas_call(body, out_shape=out, in_specs=[sm] * smem + [vm] * (len(ar...]
  transfers between devices with their start and end apart: 22 -> 25, of which waited for: 13 -> 13; matrix products, arithmetic and copies ran while one was open for 3% -> 1% of each run, Pallas kernels for 7% -> 8%
where the time goes in v3:
time: 69.4 us; the launch traced here: 69.2 us
  waiting for transfers between devices  33.6 us (48%)
  starting transfers between devices  24.1 us (35%)
  Pallas kernels  8.53 us (12%)
  local copies, waits for them, and re-layouts  1.1 us (2%)
  other arithmetic  0.99 us (1%)
  between operations  0.8 us (1%)
    ppermute x12, waiting for transfers between devices, over_z(): return lax.ppermute(x, 'pcol', [(i, i ^ CORES * s) for i in range(cols)])  20.2 us
    ppermute x12, starting transfers between devices, over_z(): return lax.ppermute(x, 'pcol', [(i, i ^ CORES * s) for i in range(cols)])  19.2 us
    ppermute x3, waiting for transfers between devices, over_row(): return lax.ppermute(x, 'prow', [(i, i ^ s) for i in range(rows)])  8.79 us
    pallas_call x9, Pallas kernels, kernel(): pl.pallas_call(body, out_shape=out, in_specs=[sm] * smem + [vm] * (len(ar...  8.53 us
    ppermute x10, waiting for transfers between devices, over_core(): return lax.ppermute(x, 'pcol', [(i, i ^ 1) for i in range(cols)])  4.58 us
    ppermute x3, starting transfers between devices, over_row(): return lax.ppermute(x, 'prow', [(i, i ^ s) for i in range(rows)])  3.55 us
    ppermute x10, starting transfers between devices, over_core(): return lax.ppermute(x, 'pcol', [(i, i ^ 1) for i in range(cols)])  1.44 us
  transfers between devices with their start and end apart: 25, of which 13 were waited for; matrix products, arithmetic and copies ran while one was open for 1% of the time, Pallas kernels for 8%

profile of v3, /device:TPU:0, one launch (start us, length us, event | category | flops | bytes accessed | tf_op | source)
XLA Modules:
  0.0 69.2 jit_solution(12720245824449252858)
XLA Ops:
  0.6 0.5 collective-permute-start.5
  1.2 1.0 %select_bitcast_fusion = (bf16[256,256]{1,0:T(8,128)(2,1)S(1)}, bf16[256,256]{1,0:T(8,128)(2,1)S(1)}) fusion(pred[]{:T(512)S(6)} %eq.5, bf16[2,1,256,256]{3,2,1,0:T(8,128)(2,1)} %param.17), kind=kLoop, calls=%fused_computation | loop fusion | flops 131072 | bytes 524289 | tf_op jit(solution)/shard_map/jit(_where)/select_n | solution.py:287
  2.3 4.0 %collective-permute-start.9 = (bf16[256,256]{1,0:T(8,128)(2,1)}, bf16[256,256]{1,0:T(8,128)(2,1)S(1)}, u32[]{:S(2)}, u32[]{:S(2)}) collective-permute-start(bf16[256,256]{1,0:T(8,128)(2,1)} %bitcast.23), channel_id=1, source_target_pairs={{0,4},{1,5},{2,6},{3,7},{4,0},{5,1},{6,2},{7,3},{8,12},{9,13},{10,... | collective-permute-start | bytes 393224 | tf_op jit(solution)/shard_map/ppermute | solution.py:275
  6.3 1.3 %collective-permute-start.11 = (bf16[256,256]{1,0:T(8,128)(2,1)}, bf16[256,256]{1,0:T(8,128)(2,1)S(1)}, u32[]{:S(2)}, u32[]{:S(2)}) collective-permute-start(bf16[256,256]{1,0:T(8,128)(2,1)} %bitcast.24), channel_id=1, source_target_pairs={{0,6},{1,7},{2,4},{3,5},{4,2},{5,3},{6,0},{7,1},{8,14},{9,15},{10,... | collective-permute-start | bytes 393224 | tf_op jit(solution)/shard_map/ppermute | solution.py:275
  7.9 8.6 %collective-permute-done.9 = bf16[256,256]{1,0:T(8,128)(2,1)S(1)} collective-permute-done((bf16[256,256]{1,0:T(8,128)(2,1)}, bf16[256,256]{1,0:T(8,128)(2,1)S(1)}, u32[]{:S(2)}, u32[]{:S(2)}) %collective-permute-start.9) | collective-permute-done | bytes 131104 | tf_op jit(solution)/shard_map/ppermute | solution.py:275
  16.5 0.8 %collective-permute-done.7 = bf16[256,256]{1,0:T(8,128)(2,1)S(1)} collective-permute-done((bf16[256,256]{1,0:T(8,128)(2,1)}, bf16[256,256]{1,0:T(8,128)(2,1)S(1)}, u32[]{:S(2)}, u32[]{:S(2)}) %collective-permute-start.7) | collective-permute-done | bytes 131104 | tf_op jit(solution)/shard_map/ppermute | solution.py:275
  17.3 4.1 %collective-permute-start.15 = (bf16[2,256,256]{2,1,0:T(8,128)(2,1)S(1)}, bf16[2,256,256]{2,1,0:T(8,128)(2,1)S(1)}, u32[]{:S(2)}, u32[]{:S(2)}) collective-permute-start(bf16[2,256,256]{2,1,0:T(8,128)(2,1)S(1)} %shard_map.128.refs_0_), channel_id=1, source_target_pairs={{0,4},{1,5},{2,6},{3,7},{4,0},{5,1},{6,2},{7,3},{8,12},{9,13},{10,... | collective-permute-start | bytes 786440 | tf_op jit(solution)/shard_map/ppermute | solution.py:275
  21.4 0.5 collective-permute-start.16
  22.5 0.7 copy-done.6
  23.9 21.0 %conditional.1 = (bf16[2,256,128]{2,1,0:T(8,128)(2,1)S(1)}, f32[2,256,256]{2,1,0:T(8,128)S(1)}, bf16[4,64,384]{2,1,0:T(8,128)(2,1)S(1)}, bf16[2,256,256]{2,1,0:T(8,128)(2,1)}) conditional(s32[]{:T(128)} %bitcast.1, () %tuple.18, (s32[4,8]{1,0:T(4,128)S(1)}, bf16[8,256,256]{2,1,0:T(8,128)(2,1)S(1)}, bf16[8,256,256]{2,1,0:T(8,128)(2,1)S(1)}, ...), branch_computations={%region_0.1_spmd, %region_1.2_spmd} | conditional | bytes 5505284 | solution.py:353
  23.9 2.7 %branch_1_fun.3 = (bf16[3,256,128]{2,1,0:T(8,128)(2,1)S(1)}, bf16[4,64,128]{2,1,0:T(8,128)(2,1)S(1)}) custom-call(s32[4,8]{1,0:T(4,128)S(1)} %get-tuple-element.36.us_ref, bf16[8,256,256]{2,1,0:T(8,128)(2,1)S(1)} %get-tuple-element.37.to_ref, bf16[8,256,256]{2,1,0:T(8,128)(2,1)S(1)} %get-tuple-element.38.ts_ref, bf16[256,256]{1,0:T(8,128)(2,1)} %get-tuple-element.39.refs_0_, ...), custom_call_target="tpu_custom_call" | custom-call | tf_op jit(solution)/shard_map/cond/branch_1_fun/pallas_call | solution.py:298
  26.6 1.6 %collective-permute-start = (bf16[3,256,128]{2,1,0:T(8,128)(2,1)S(1)}, bf16[3,256,128]{2,1,0:T(8,128)(2,1)S(1)}, u32[]{:S(2)}, u32[]{:S(2)}) collective-permute-start(bf16[3,256,128]{2,1,0:T(8,128)(2,1)S(1)} %get-tuple-element.48.refs_0_), channel_id=1, source_target_pairs={{0,8},{8,0},{16,24},{24,16},{1,9},{9,1},{17,25},{25,17},{2,10},{10... | collective-permute-start | bytes 589832 | tf_op jit(solution)/shard_map/cond/branch_1_fun/ppermute | solution.py:278
  28.1 1.5 %collective-permute-start.1 = (bf16[3,256,128]{2,1,0:T(8,128)(2,1)S(1)}, bf16[3,256,128]{2,1,0:T(8,128)(2,1)S(1)}, u32[]{:S(2)}, u32[]{:S(2)}) collective-permute-start(bf16[3,256,128]{2,1,0:T(8,128)(2,1)S(1)} %get-tuple-element.48.refs_0_), channel_id=1, source_target_pairs={{0,16},{8,24},{16,0},{24,8},{1,17},{9,25},{17,1},{25,9},{2,18},{10... | collective-permute-start | bytes 589832 | tf_op jit(solution)/shard_map/cond/branch_1_fun/ppermute | solution.py:278
  30.1 4.3 %collective-permute-done.refs_1_ = bf16[3,256,128]{2,1,0:T(8,128)(2,1)S(1)} collective-permute-done((bf16[3,256,128]{2,1,0:T(8,128)(2,1)S(1)}, bf16[3,256,128]{2,1,0:T(8,128)(2,1)S(1)}, u32[]{:S(2)}, u32[]{:S(2)}) %collective-permute-start) | collective-permute-done | bytes 196640 | tf_op jit(solution)/shard_map/cond/branch_1_fun/ppermute | solution.py:278
  34.4 4.5 %collective-permute-done.1.refs_2_ = bf16[3,256,128]{2,1,0:T(8,128)(2,1)S(1)} collective-permute-done((bf16[3,256,128]{2,1,0:T(8,128)(2,1)S(1)}, bf16[3,256,128]{2,1,0:T(8,128)(2,1)S(1)}, u32[]{:S(2)}, u32[]{:S(2)}) %collective-permute-start.1) | collective-permute-done | bytes 196640 | tf_op jit(solution)/shard_map/cond/branch_1_fun/ppermute | solution.py:278
  38.9 0.6 branch_1_fun.4
  39.7 1.4 %collective-permute-done.3.got_ref = bf16[3,256,128]{2,1,0:T(8,128)(2,1)S(1)} collective-permute-done((bf16[3,256,128]{2,1,0:T(8,128)(2,1)S(1)}, bf16[3,256,128]{2,1,0:T(8,128)(2,1)S(1)}, u32[]{:S(2)}, u32[]{:S(2)}) %collective-permute-start.3) | collective-permute-done | bytes 196640 | tf_op jit(solution)/shard_map/cond/branch_1_fun/ppermute | solution.py:272
  41.1 1.0 %branch_1_fun.5 = (f32[2,256,256]{2,1,0:T(8,128)S(1)}, bf16[4,64,384]{2,1,0:T(8,128)(2,1)S(1)}) custom-call(s32[4,8]{1,0:T(4,128)S(1)} %get-tuple-element.36.us_ref, s32[8]{0:T(128)S(1)} %get-tuple-element.49.co_ref, s32[2,8]{1,0:T(2,128)S(1)} %get-tuple-element.50.ck_ref, bf16[3,256,128]{2,1,0:T(8,128)(2,1)S(1)} %get-tuple-element.51.keep_ref, ...), custom_call_target="tpu_custom_call" | custom-call | tf_op jit(solution)/shard_map/cond/branch_1_fun/pallas_call | solution.py:298
  42.2 2.7 %collective-permute-done.4 = bf16[2,256,256]{2,1,0:T(8,128)(2,1)} collective-permute-done((bf16[2,256,256]{2,1,0:T(8,128)(2,1)S(1)}, bf16[2,256,256]{2,1,0:T(8,128)(2,1)}, u32[]{:S(2)}, u32[]{:S(2)}) %collective-permute-start.4) | collective-permute-done | bytes 262176 | tf_op jit(solution)/shard_map/cond/branch_1_fun/ppermute | solution.py:275
  44.9 2.0 %shard_map.129 = (bf16[256,256]{1,0:T(8,128)(2,1)S(1)}, bf16[256,256]{1,0:T(8,128)(2,1)S(1)}, bf16[4,64,640]{2,1,0:T(8,128)(2,1)S(1)}) custom-call(s32[4,8]{1,0:T(4,128)S(1)} %copy-done.5, s32[8]{0:T(128)S(1)} %copy-done.6, s32[2,8]{1,0:T(2,128)S(1)} %copy-done.7, bf16[8,256,256]{2,1,0:T(8,128)(2,1)S(1)} %bitcast.21, ...), custom_call_target="tpu_custom_call" | custom-call | tf_op jit(solution)/shard_map/pallas_call | solution.py:298
  47.0 0.6 collective-permute-start.18
  47.5 1.5 %collective-permute-start.19 = (bf16[64,640]{1,0:T(8,128)(2,1)S(1)}, bf16[64,640]{1,0:T(8,128)(2,1)S(1)}, u32[]{:S(2)}, u32[]{:S(2)}) collective-permute-start(bf16[64,640]{1,0:T(8,128)(2,1)S(1)} %get-tuple-element.96), channel_id=1, source_target_pairs={{0,4},{1,5},{2,6},{3,7},{4,0},{5,1},{6,2},{7,3},{8,12},{9,13},{10,... | collective-permute-start | bytes 245768 | tf_op jit(solution)/shard_map/ppermute | solution.py:275
  49.0 2.4 %collective-permute-start.20 = (bf16[64,640]{1,0:T(8,128)(2,1)S(1)}, bf16[64,640]{1,0:T(8,128)(2,1)S(1)}, u32[]{:S(2)}, u32[]{:S(2)}) collective-permute-start(bf16[64,640]{1,0:T(8,128)(2,1)S(1)} %get-tuple-element.95), channel_id=1, source_target_pairs={{0,6},{1,7},{2,4},{3,5},{4,2},{5,3},{6,0},{7,1},{8,14},{9,15},{10,... | collective-permute-start | bytes 245768 | tf_op jit(solution)/shard_map/ppermute | solution.py:275
  51.4 0.9 %collective-permute-done.18.refs_0_ = bf16[64,640]{1,0:T(8,128)(2,1)S(1)} collective-permute-done((bf16[64,640]{1,0:T(8,128)(2,1)S(1)}, bf16[64,640]{1,0:T(8,128)(2,1)S(1)}, u32[]{:S(2)}, u32[]{:S(2)}) %collective-permute-start.18) | collective-permute-done | bytes 81952 | tf_op jit(solution)/shard_map/ppermute | solution.py:275
  52.3 4.4 %collective-permute-done.19.refs_1_ = bf16[64,640]{1,0:T(8,128)(2,1)S(1)} collective-permute-done((bf16[64,640]{1,0:T(8,128)(2,1)S(1)}, bf16[64,640]{1,0:T(8,128)(2,1)S(1)}, u32[]{:S(2)}, u32[]{:S(2)}) %collective-permute-start.19) | collective-permute-done | bytes 81952 | tf_op jit(solution)/shard_map/ppermute | solution.py:275
  56.8 1.5 %collective-permute-start.21 = (bf16[64,640]{1,0:T(8,128)(2,1)S(1)}, bf16[64,640]{1,0:T(8,128)(2,1)S(1)}, u32[]{:S(2)}, u32[]{:S(2)}) collective-permute-start(bf16[64,640]{1,0:T(8,128)(2,1)S(1)} %shard_map.131.refs_0_), channel_id=1, source_target_pairs={{0,2},{1,3},{2,0},{3,1},{4,6},{5,7},{6,4},{7,5},{8,10},{9,11},{10,... | collective-permute-start | bytes 245768 | tf_op jit(solution)/shard_map/ppermute | solution.py:275
  58.8 2.5 %collective-permute-start.23 = (bf16[64,640]{1,0:T(8,128)(2,1)S(1)}, bf16[64,640]{1,0:T(8,128)(2,1)S(1)}, u32[]{:S(2)}, u32[]{:S(2)}) collective-permute-start(bf16[64,640]{1,0:T(8,128)(2,1)S(1)} %shard_map.131.refs_0_), channel_id=1, source_target_pairs={{0,6},{1,7},{2,4},{3,5},{4,2},{5,3},{6,0},{7,1},{8,14},{9,15},{10,... | collective-permute-start | bytes 245768 | tf_op jit(solution)/shard_map/ppermute | solution.py:275
  61.4 1.2 %collective-permute-done.14.u_got_ref = bf16[256,128]{1,0:T(8,128)(2,1)S(1)} collective-permute-done((bf16[256,128]{1,0:T(8,128)(2,1)S(1)}, bf16[256,128]{1,0:T(8,128)(2,1)S(1)}, u32[]{:S(2)}, u32[]{:S(2)}) %collective-permute-start.14) | collective-permute-done | bytes 65568 | tf_op jit(solution)/shard_map/ppermute | solution.py:272
  62.6 0.8 %shard_map.130 = (bf16[1,1,256,256]{3,2,1,0:T(8,128)(2,1)}, bf16[2,1,256,256]{3,2,1,0:T(8,128)(2,1)}, f32[2,256,256]{2,1,0:T(8,128)S(1)}) custom-call(bf16[256,128]{1,0:T(8,128)(2,1)S(1)} %get-tuple-element.101.u_own_ref, bf16[256,128]{1,0:T(8,128)(2,1)S(1)} %collective-permute-done.14.u_got_ref, bf16[256,256]{1,0:T(8,128)(2,1)S(1)} %get-tuple-element.85.l_own_ref, ...), custom_call_target="tpu_custom_call" | custom-call | tf_op jit(solution)/shard_map/pallas_call | solution.py:298
  63.4 2.8 %collective-permute-done.22.refs_2_ = bf16[64,640]{1,0:T(8,128)(2,1)S(1)} collective-permute-done((bf16[64,640]{1,0:T(8,128)(2,1)S(1)}, bf16[64,640]{1,0:T(8,128)(2,1)S(1)}, u32[]{:S(2)}, u32[]{:S(2)}) %collective-permute-start.22) | collective-permute-done | bytes 81952 | tf_op jit(solution)/shard_map/ppermute | solution.py:275
  66.4 1.6 %collective-permute-done.24.got_ref = bf16[256,640]{1,0:T(8,128)(2,1)S(1)} collective-permute-done((bf16[256,640]{1,0:T(8,128)(2,1)S(1)}, bf16[256,640]{1,0:T(8,128)(2,1)S(1)}, u32[]{:S(2)}, u32[]{:S(2)}) %collective-permute-start.24) | collective-permute-done | bytes 327712 | tf_op jit(solution)/shard_map/ppermute | solution.py:272
  68.0 1.2 %shard_map.133 = (f32[1,256,256]{2,1,0:T(8,128)}, bf16[2,256,256]{2,1,0:T(8,128)(2,1)}, f32[2,256,256]{2,1,0:T(8,128)}) custom-call(bf16[256,640]{1,0:T(8,128)(2,1)S(1)} %shard_map.132.own_ref, bf16[256,640]{1,0:T(8,128)(2,1)S(1)} %collective-permute-done.24.got_ref, f32[1,256,256]{2,1,0:T(8,128)S(1)} %copy-done.2, bf16[2,256,256]{2,1,0:T(8,128)(2,1)S(1)} %copy-done.3, ...), custom_call_target="tpu_custom_call" | custom-call | tf_op jit(solution)/shard_map/pallas_call | solution.py:298
  (48 shorter events, 3.0 us)
Async XLA Ops:
  0.6 22.9 %copy-start.1 = (bf16[1,8,256,256]{3,2,1,0:T(8,128)(2,1)S(1)}, bf16[1,8,256,256]{3,2,1,0:T(8,128)(2,1)}, u32[]{:S(2)}) copy-start(bf16[1,8,256,256]{3,2,1,0:T(8,128)(2,1)} %param.11) | copy-start | bytes 3145732
  0.6 22.8 %collective-permute-start.5 = (bf16[8,256,256]{2,1,0:T(8,128)(2,1)}, bf16[8,256,256]{2,1,0:T(8,128)(2,1)S(1)}, u32[]{:S(2)}, u32[]{:S(2)}) collective-permute-start(bf16[8,256,256]{2,1,0:T(8,128)(2,1)} %bitcast.19), channel_id=1, source_target_pairs={{0,1},{1,0},{2,3},{3,2},{4,5},{5,4},{6,7},{7,6},{8,9},{9,8},{10,11... | collective-permute-start | bytes 3145736 | tf_op jit(solution)/shard_map/ppermute | solution.py:272
  2.2 5.7 %collective-permute-start.13 = (bf16[256,256]{1,0:T(8,128)(2,1)S(1)}, bf16[256,256]{1,0:T(8,128)(2,1)S(1)}, u32[]{:S(2)}, u32[]{:S(2)}) collective-permute-start(bf16[256,256]{1,0:T(8,128)(2,1)S(1)} %get-tuple-element.98), channel_id=1, source_target_pairs={{0,1},{1,0},{2,3},{3,2},{4,5},{5,4},{6,7},{7,6},{8,9},{9,8},{10,11... | collective-permute-start | bytes 393224 | tf_op jit(solution)/shard_map/ppermute | solution.py:272
  2.3 14.1 %collective-permute-start.9 = (bf16[256,256]{1,0:T(8,128)(2,1)}, bf16[256,256]{1,0:T(8,128)(2,1)S(1)}, u32[]{:S(2)}, u32[]{:S(2)}) collective-permute-start(bf16[256,256]{1,0:T(8,128)(2,1)} %bitcast.23), channel_id=1, source_target_pairs={{0,4},{1,5},{2,6},{3,7},{4,0},{5,1},{6,2},{7,3},{8,12},{9,13},{10,... | collective-permute-start | bytes 393224 | tf_op jit(solution)/shard_map/ppermute | solution.py:275
  6.3 10.2 %collective-permute-start.11 = (bf16[256,256]{1,0:T(8,128)(2,1)}, bf16[256,256]{1,0:T(8,128)(2,1)S(1)}, u32[]{:S(2)}, u32[]{:S(2)}) collective-permute-start(bf16[256,256]{1,0:T(8,128)(2,1)} %bitcast.24), channel_id=1, source_target_pairs={{0,6},{1,7},{2,4},{3,5},{4,2},{5,3},{6,0},{7,1},{8,14},{9,15},{10,... | collective-permute-start | bytes 393224 | tf_op jit(solution)/shard_map/ppermute | solution.py:275
  7.7 9.6 %collective-permute-start.7 = (bf16[256,256]{1,0:T(8,128)(2,1)}, bf16[256,256]{1,0:T(8,128)(2,1)S(1)}, u32[]{:S(2)}, u32[]{:S(2)}) collective-permute-start(bf16[256,256]{1,0:T(8,128)(2,1)} %bitcast.25), channel_id=1, source_target_pairs={{0,2},{1,3},{2,0},{3,1},{4,6},{5,7},{6,4},{7,5},{8,10},{9,11},{10,... | collective-permute-start | bytes 393224 | tf_op jit(solution)/shard_map/ppermute | solution.py:275
  7.9 14.1 %collective-permute-start.6 = (bf16[256,256]{1,0:T(8,128)(2,1)}, bf16[256,256]{1,0:T(8,128)(2,1)S(1)}, u32[]{:S(2)}, u32[]{:S(2)}) collective-permute-start(bf16[256,256]{1,0:T(8,128)(2,1)} %bitcast.26), channel_id=1, source_target_pairs={{0,1},{1,0},{2,3},{3,2},{4,5},{5,4},{6,7},{7,6},{8,9},{9,8},{10,11... | collective-permute-start | bytes 393224 | tf_op jit(solution)/shard_map/ppermute | solution.py:272
  16.5 5.5 %collective-permute-start.10 = (bf16[256,256]{1,0:T(8,128)(2,1)S(1)}, bf16[256,256]{1,0:T(8,128)(2,1)S(1)}, u32[]{:S(2)}, u32[]{:S(2)}) collective-permute-start(bf16[256,256]{1,0:T(8,128)(2,1)S(1)} %collective-permute-done.9), channel_id=1, source_target_pairs={{0,1},{1,0},{2,3},{3,2},{4,5},{5,4},{6,7},{7,6},{8,9},{9,8},{10,11... | collective-permute-start | bytes 393224 | tf_op jit(solution)/shard_map/ppermute | solution.py:272
  17.3 27.6 %collective-permute-start.15 = (bf16[2,256,256]{2,1,0:T(8,128)(2,1)S(1)}, bf16[2,256,256]{2,1,0:T(8,128)(2,1)S(1)}, u32[]{:S(2)}, u32[]{:S(2)}) collective-permute-start(bf16[2,256,256]{2,1,0:T(8,128)(2,1)S(1)} %shard_map.128.refs_0_), channel_id=1, source_target_pairs={{0,4},{1,5},{2,6},{3,7},{4,0},{5,1},{6,2},{7,3},{8,12},{9,13},{10,... | collective-permute-start | bytes 786440 | tf_op jit(solution)/shard_map/ppermute | solution.py:275
  21.4 23.5 %collective-permute-start.16 = (bf16[2,256,256]{2,1,0:T(8,128)(2,1)S(1)}, bf16[2,256,256]{2,1,0:T(8,128)(2,1)S(1)}, u32[]{:S(2)}, u32[]{:S(2)}) collective-permute-start(bf16[2,256,256]{2,1,0:T(8,128)(2,1)S(1)} %shard_map.128.refs_0_), channel_id=1, source_target_pairs={{0,6},{1,7},{2,4},{3,5},{4,2},{5,3},{6,0},{7,1},{8,14},{9,15},{10,... | collective-permute-start | bytes 786440 | tf_op jit(solution)/shard_map/ppermute | solution.py:275
  21.9 1.3 %collective-permute-start.12 = (bf16[256,256]{1,0:T(8,128)(2,1)S(1)}, bf16[256,256]{1,0:T(8,128)(2,1)S(1)}, u32[]{:S(2)}, u32[]{:S(2)}) collective-permute-start(bf16[256,256]{1,0:T(8,128)(2,1)S(1)} %collective-permute-done.11), channel_id=1, source_target_pairs={{0,1},{1,0},{2,3},{3,2},{4,5},{5,4},{6,7},{7,6},{8,9},{9,8},{10,11... | collective-permute-start | bytes 393224 | tf_op jit(solution)/shard_map/ppermute | solution.py:272
  22.0 1.5 %collective-permute-start.8 = (bf16[256,256]{1,0:T(8,128)(2,1)S(1)}, bf16[256,256]{1,0:T(8,128)(2,1)S(1)}, u32[]{:S(2)}, u32[]{:S(2)}) collective-permute-start(bf16[256,256]{1,0:T(8,128)(2,1)S(1)} %collective-permute-done.7), channel_id=1, source_target_pairs={{0,1},{1,0},{2,3},{3,2},{4,5},{5,4},{6,7},{7,6},{8,9},{9,8},{10,11... | collective-permute-start | bytes 393224 | tf_op jit(solution)/shard_map/ppermute | solution.py:272
  23.2 0.7 copy-start.5
  23.2 0.7 copy-start.7
  26.6 7.8 %collective-permute-start = (bf16[3,256,128]{2,1,0:T(8,128)(2,1)S(1)}, bf16[3,256,128]{2,1,0:T(8,128)(2,1)S(1)}, u32[]{:S(2)}, u32[]{:S(2)}) collective-permute-start(bf16[3,256,128]{2,1,0:T(8,128)(2,1)S(1)} %get-tuple-element.48.refs_0_), channel_id=1, source_target_pairs={{0,8},{8,0},{16,24},{24,16},{1,9},{9,1},{17,25},{25,17},{2,10},{10... | collective-permute-start | bytes 589832 | tf_op jit(solution)/shard_map/cond/branch_1_fun/ppermute | solution.py:278
  28.1 10.8 %collective-permute-start.1 = (bf16[3,256,128]{2,1,0:T(8,128)(2,1)S(1)}, bf16[3,256,128]{2,1,0:T(8,128)(2,1)S(1)}, u32[]{:S(2)}, u32[]{:S(2)}) collective-permute-start(bf16[3,256,128]{2,1,0:T(8,128)(2,1)S(1)} %get-tuple-element.48.refs_0_), channel_id=1, source_target_pairs={{0,16},{8,24},{16,0},{24,8},{1,17},{9,25},{17,1},{25,9},{2,18},{10... | collective-permute-start | bytes 589832 | tf_op jit(solution)/shard_map/cond/branch_1_fun/ppermute | solution.py:278
  29.7 9.3 %collective-permute-start.2 = (bf16[3,256,128]{2,1,0:T(8,128)(2,1)S(1)}, bf16[3,256,128]{2,1,0:T(8,128)(2,1)S(1)}, u32[]{:S(2)}, u32[]{:S(2)}) collective-permute-start(bf16[3,256,128]{2,1,0:T(8,128)(2,1)S(1)} %get-tuple-element.48.refs_0_), channel_id=1, source_target_pairs={{0,24},{8,16},{16,8},{24,0},{1,25},{9,17},{17,9},{25,1},{2,26},{10... | collective-permute-start | bytes 589832 | tf_op jit(solution)/shard_map/cond/branch_1_fun/ppermute | solution.py:278
  34.4 10.5 %collective-permute-start.4 = (bf16[2,256,256]{2,1,0:T(8,128)(2,1)S(1)}, bf16[2,256,256]{2,1,0:T(8,128)(2,1)}, u32[]{:S(2)}, u32[]{:S(2)}) collective-permute-start(bf16[2,256,256]{2,1,0:T(8,128)(2,1)S(1)} %get-tuple-element.60), channel_id=1, source_target_pairs={{0,2},{1,3},{2,0},{3,1},{4,6},{5,7},{6,4},{7,5},{8,10},{9,11},{10,... | collective-permute-start | bytes 786440 | tf_op jit(solution)/shard_map/cond/branch_1_fun/ppermute | solution.py:275
  39.6 1.5 %copy-start.4 = (bf16[2,256,256]{2,1,0:T(8,128)(2,1)S(1)}, bf16[2,256,256]{2,1,0:T(8,128)(2,1)}, u32[]{:S(2)}) copy-start(bf16[2,256,256]{2,1,0:T(8,128)(2,1)} %get-tuple-element.53.pp_ref) | copy-start | bytes 786436 | tf_op jit(solution)/shard_map/cond
  39.6 1.5 %collective-permute-start.3 = (bf16[3,256,128]{2,1,0:T(8,128)(2,1)S(1)}, bf16[3,256,128]{2,1,0:T(8,128)(2,1)S(1)}, u32[]{:S(2)}, u32[]{:S(2)}) collective-permute-start(bf16[3,256,128]{2,1,0:T(8,128)(2,1)S(1)} %get-tuple-element.52), channel_id=1, source_target_pairs={{0,1},{1,0},{2,3},{3,2},{4,5},{5,4},{6,7},{7,6},{8,9},{9,8},{10,11... | collective-permute-start | bytes 589832 | tf_op jit(solution)/shard_map/cond/branch_1_fun/ppermute | solution.py:272
  46.9 15.7 %copy-start = (f32[2,256,256]{2,1,0:T(8,128)S(1)}, f32[2,256,256]{2,1,0:T(8,128)}, u32[]{:S(2)}) copy-start(f32[2,256,256]{2,1,0:T(8,128)} %d_ref.2) | copy-start | bytes 1572868
  47.0 5.4 %collective-permute-start.18 = (bf16[64,640]{1,0:T(8,128)(2,1)S(1)}, bf16[64,640]{1,0:T(8,128)(2,1)S(1)}, u32[]{:S(2)}, u32[]{:S(2)}) collective-permute-start(bf16[64,640]{1,0:T(8,128)(2,1)S(1)} %get-tuple-element.97), channel_id=1, source_target_pairs={{0,2},{1,3},{2,0},{3,1},{4,6},{5,7},{6,4},{7,5},{8,10},{9,11},{10,... | collective-permute-start | bytes 245768 | tf_op jit(solution)/shard_map/ppermute | solution.py:275
  47.5 9.2 %collective-permute-start.19 = (bf16[64,640]{1,0:T(8,128)(2,1)S(1)}, bf16[64,640]{1,0:T(8,128)(2,1)S(1)}, u32[]{:S(2)}, u32[]{:S(2)}) collective-permute-start(bf16[64,640]{1,0:T(8,128)(2,1)S(1)} %get-tuple-element.96), channel_id=1, source_target_pairs={{0,4},{1,5},{2,6},{3,7},{4,0},{5,1},{6,2},{7,3},{8,12},{9,13},{10,... | collective-permute-start | bytes 245768 | tf_op jit(solution)/shard_map/ppermute | solution.py:275
  49.0 7.8 %collective-permute-start.20 = (bf16[64,640]{1,0:T(8,128)(2,1)S(1)}, bf16[64,640]{1,0:T(8,128)(2,1)S(1)}, u32[]{:S(2)}, u32[]{:S(2)}) collective-permute-start(bf16[64,640]{1,0:T(8,128)(2,1)S(1)} %get-tuple-element.95), channel_id=1, source_target_pairs={{0,6},{1,7},{2,4},{3,5},{4,2},{5,3},{6,0},{7,1},{8,14},{9,15},{10,... | collective-permute-start | bytes 245768 | tf_op jit(solution)/shard_map/ppermute | solution.py:275
  51.4 11.2 %collective-permute-start.17 = (bf16[256,256]{1,0:T(8,128)(2,1)S(1)}, bf16[256,256]{1,0:T(8,128)(2,1)S(1)}, u32[]{:S(2)}, u32[]{:S(2)}) collective-permute-start(bf16[256,256]{1,0:T(8,128)(2,1)S(1)} %get-tuple-element.86), channel_id=1, source_target_pairs={{0,1},{1,0},{2,3},{3,2},{4,5},{5,4},{6,7},{7,6},{8,9},{9,8},{10,11... | collective-permute-start | bytes 393224 | tf_op jit(solution)/shard_map/ppermute | solution.py:272
  56.8 6.6 %collective-permute-start.21 = (bf16[64,640]{1,0:T(8,128)(2,1)S(1)}, bf16[64,640]{1,0:T(8,128)(2,1)S(1)}, u32[]{:S(2)}, u32[]{:S(2)}) collective-permute-start(bf16[64,640]{1,0:T(8,128)(2,1)S(1)} %shard_map.131.refs_0_), channel_id=1, source_target_pairs={{0,2},{1,3},{2,0},{3,1},{4,6},{5,7},{6,4},{7,5},{8,10},{9,11},{10,... | collective-permute-start | bytes 245768 | tf_op jit(solution)/shard_map/ppermute | solution.py:275
  58.3 7.9 %collective-permute-start.22 = (bf16[64,640]{1,0:T(8,128)(2,1)S(1)}, bf16[64,640]{1,0:T(8,128)(2,1)S(1)}, u32[]{:S(2)}, u32[]{:S(2)}) collective-permute-start(bf16[64,640]{1,0:T(8,128)(2,1)S(1)} %shard_map.131.refs_0_), channel_id=1, source_target_pairs={{0,4},{1,5},{2,6},{3,7},{4,0},{5,1},{6,2},{7,3},{8,12},{9,13},{10,... | collective-permute-start | bytes 245768 | tf_op jit(solution)/shard_map/ppermute | solution.py:275
  58.8 7.4 %collective-permute-start.23 = (bf16[64,640]{1,0:T(8,128)(2,1)S(1)}, bf16[64,640]{1,0:T(8,128)(2,1)S(1)}, u32[]{:S(2)}, u32[]{:S(2)}) collective-permute-start(bf16[64,640]{1,0:T(8,128)(2,1)S(1)} %shard_map.131.refs_0_), channel_id=1, source_target_pairs={{0,6},{1,7},{2,4},{3,5},{4,2},{5,3},{6,0},{7,1},{8,14},{9,15},{10,... | collective-permute-start | bytes 245768 | tf_op jit(solution)/shard_map/ppermute | solution.py:275
  61.3 1.3 %collective-permute-start.14 = (bf16[256,128]{1,0:T(8,128)(2,1)S(1)}, bf16[256,128]{1,0:T(8,128)(2,1)S(1)}, u32[]{:S(2)}, u32[]{:S(2)}) collective-permute-start(bf16[256,128]{1,0:T(8,128)(2,1)S(1)} %get-tuple-element.100), channel_id=1, source_target_pairs={{0,1},{1,0},{2,3},{3,2},{4,5},{5,4},{6,7},{7,6},{8,9},{9,8},{10,11... | collective-permute-start | bytes 196616 | tf_op jit(solution)/shard_map/ppermute | solution.py:272
  66.2 1.7 %copy-start.2 = (f32[1,256,256]{2,1,0:T(8,128)S(1)}, f32[1,256,256]{2,1,0:T(8,128)}, u32[]{:S(2)}) copy-start(f32[1,256,256]{2,1,0:T(8,128)} %d_ref.3) | copy-start | bytes 786436
  66.2 1.7 %copy-start.3 = (bf16[2,256,256]{2,1,0:T(8,128)(2,1)S(1)}, bf16[2,256,256]{2,1,0:T(8,128)(2,1)}, u32[]{:S(2)}) copy-start(bf16[2,256,256]{2,1,0:T(8,128)(2,1)} %pp_ref.1) | copy-start | bytes 786436
  66.3 1.7 %collective-permute-start.24 = (bf16[256,640]{1,0:T(8,128)(2,1)S(1)}, bf16[256,640]{1,0:T(8,128)(2,1)S(1)}, u32[]{:S(2)}, u32[]{:S(2)}) collective-permute-start(bf16[256,640]{1,0:T(8,128)(2,1)S(1)} %shard_map.132.own_ref), channel_id=1, source_target_pairs={{0,1},{1,0},{2,3},{3,2},{4,5},{5,4},{6,7},{7,6},{8,9},{9,8},{10,11... | collective-permute-start | bytes 983048 | tf_op jit(solution)/shard_map/ppermute | solution.py:272
  (1 other events, 0.7 us)

commit v4 on v3

--- a/solution.py
+++ b/solution.py
@@ -149,7 +149,7 @@
                 out_ref[...] = block[...]
 
 
-def parent_body(nz, us_ref, co_ref, ck_ref, keep_ref, got_ref, pp_ref, lm_ref, lg_ref, ud_ref,
+def parent_body(nz, us_ref, co_ref, ck_ref, keep_ref, got_ref, pp_ref, l_ref, ud_ref,
                 w_ref, rs_ref, a_ref):
     row, z, c = place()
     half = keep_ref.shape[2]
@@ -160,12 +160,12 @@
     parent = co_ref[CORES * row + c] // CH
     p_mine, p_other = pp_ref[c, mine, :], pp_ref[c, other, :]
     a_ref[...] = dot(keep_ref[CORES], p_mine) + dot(got_ref[CORES], p_other)
-    for p, l_ref in enumerate((lm_ref, lg_ref)):
+    for p in range(CORES):
         j = CORES * z + (c if p == 0 else 1 - c)
         flag = (us_ref[parent, j] * ck_ref[c, j]).astype(F32).astype(BF)
         k_half, g_half = keep_ref[p], got_ref[1 - p]
         w_ref[p] = dot(k_half, p_mine) + dot(g_half, p_other)
-        masked = l_ref[...] * flag
+        masked = l_ref[p] * flag
         a_ref[mine, :] = a_ref[mine, :] + dot_t(k_half, masked)
         a_ref[other, :] = a_ref[other, :] + dot_t(g_half, masked)
     for s in range(nz):
@@ -203,9 +203,10 @@
         rs_ref[s, :, size:] = rs1_ref[s]
 
 
-def pair_body(count, *refs):
-    for i, ref in enumerate(refs[:count]):
-        refs[-1][i] = ref[...]
+def pair_body(own_ref, got_ref, out_ref):
+    _, _, c = place()
+    out_ref[0] = own_ref[c]
+    out_ref[1] = got_ref[c]
 
 
 def order_body(u_own_ref, u_got_ref, l_own_ref, l_got_ref, d_ref, ub_ref, lb_ref, d_out_ref):
@@ -266,7 +267,6 @@
     size = upper_panels.shape[-1]
     half, quarter = size // CORES, size // nz
     row, z, c = place()
-    first = c == 0
 
     def over_core(x):
         return lax.ppermute(x, "pcol", [(i, i ^ 1) for i in range(cols)])
@@ -283,8 +283,7 @@
     l_all = lower_panels[:, 0]
     d_own = upper_diag_inverse[0]
     u_sib = over_core(u_own)
-    l_own = jnp.where(first, l_all[0], l_all[1])
-    l_sib = over_core(jnp.where(first, l_all[1], l_all[0]))
+    l_got = over_core(l_all)
     t_sib = over_core(t_own)
     u_far = [over_z(u_own, s) for s in range(1, nz)]
     u_all = [(u_own, u_sib)] + [(u, over_core(u)) for u in u_far]
@@ -304,11 +303,9 @@
             compiler_params=pltpu.CompilerParams(vmem_limit_bytes=24 * 1024 * 1024),
         )(*args, *rest)
 
-    l_stack = kernel(
-        functools.partial(pair_body, 2), shape((CORES, size, size), BF), (l_own, l_sib)
-    )
+    l_stack = kernel(pair_body, shape((CORES, size, size), BF), (l_all, l_got))
     l_later = lax.optimization_barrier((l_stack, *u_far))[0]
-    l_far = [over_z(l_later, s) for s in range(2, nz)]
+    l_far = [over_z(l_later, s) for s in range(1, nz)]
     scalars = (upper_structure, child_order, child_keep)
 
     def upper_part(_):
@@ -324,7 +321,9 @@
             ],
             rest=(d_own,),
         )
-        rx_all = [rx] + [over_row(rx, s) for s in range(1, rows)]
+        rx_all = [rx]
+        for s in range(1, rows):
+            rx_all.append(over_row(rx_all[s & (s - 1)], s & -s))
         keep, give = kernel(
             functools.partial(pick_body, rows),
             (shape(rx.shape, BF), shape(rx.shape, BF)),
@@ -335,27 +334,25 @@
         w, rs1 = kernel(
             functools.partial(parent_body, nz),
             (shape((CORES, size, size), F32), shape((nz, quarter, size + half), BF)),
-            (*scalars, keep, got, parent_panels, l_own, l_sib, ud_part),
+            (*scalars, keep, got, parent_panels, l_stack, ud_part),
             smem=3,
             scratch=[pltpu.VMEM((size, size), F32)],
         )
-        l_next = lax.optimization_barrier((l_stack, rx_all[1]))[0]
-        return rx[:CORES], w, rs1, over_z(l_next, 1)
+        return rx[:CORES], w, rs1
 
     def no_part(_):
         return (
             jnp.zeros((CORES, size, half), BF),
             jnp.zeros((CORES, size, size), F32),
             jnp.zeros((nz, quarter, size + half), BF),
-            jnp.zeros((CORES, size, size), BF),
         )
 
-    ub, w, rs1, l_near = lax.cond(child_order[0] >= 0, upper_part, no_part, None)
+    ub, w, rs1 = lax.cond(row >= 0, upper_part, no_part, None)
     ub_got = over_core(ub[1])
     lb_own, lb_give, sums = kernel(
         functools.partial(lower_body, nz),
         (shape((size, size), BF), shape((size, size), BF), shape((nz, quarter, 2 * size + half), BF)),
-        (*scalars, t_own, t_sib, w, rs1, l_stack, l_near, *l_far),
+        (*scalars, t_own, t_sib, w, rs1, l_stack, *l_far),
         smem=3,
         scratch=[pltpu.VMEM((size, size), F32)],
     )

time: 69.4 us -> 67.8 us (0.977)
  waiting for transfers between devices: 33.6 us -> 31.7 us
  other arithmetic: 0.99 us -> 0 us
  starting transfers between devices: 24.1 us -> 24.8 us
    ppermute x12, waiting for transfers between devices: 20.2 us -> 18.1 us  [over_z(): return lax.ppermute(x, 'pcol', [(i, i ^ CORES * s) for i in range(cols)])]
    ppermute x3, starting transfers between devices: 3.55 us -> 4.57 us  [over_row(): return lax.ppermute(x, 'prow', [(i, i ^ s) for i in range(rows)])]
    select_n x1 -> x0, other arithmetic: 0.99 us -> none  [near_shards(): l_sib = over_core(jnp.where(first, l_all[1], l_all[0]))]
    unnamed x14 -> x20, local copies, waits for them, and re-layouts: 1.05 us -> 1.56 us
  transfers between devices with their start and end apart: 25 -> 25, of which waited for: 13 -> 12; matrix products, arithmetic and copies ran while one was open for 1% -> 0% of each run, Pallas kernels for 8% -> 7%
where the time goes in v4:
time: 67.8 us; the launch traced here: 67.6 us
  waiting for transfers between devices  31.7 us (47%)
  starting transfers between devices  24.8 us (37%)
  Pallas kernels  8.59 us (13%)
  local copies, waits for them, and re-layouts  1.61 us (2%)
  between operations  0.79 us (1%)
    ppermute x12, starting transfers between devices, over_z(): return lax.ppermute(x, 'pcol', [(i, i ^ CORES * s) for i in range(cols)])  18.9 us
    ppermute x12, waiting for transfers between devices, over_z(): return lax.ppermute(x, 'pcol', [(i, i ^ CORES * s) for i in range(cols)])  18.1 us
    pallas_call x9, Pallas kernels, kernel(): pl.pallas_call(body, out_shape=out, in_specs=[sm] * smem + [vm] * (len(ar...  8.59 us
    ppermute x3, waiting for transfers between devices, over_row(): return lax.ppermute(x, 'prow', [(i, i ^ s) for i in range(rows)])  8.55 us
    ppermute x10, waiting for transfers between devices, over_core(): return lax.ppermute(x, 'pcol', [(i, i ^ 1) for i in range(cols)])  5.03 us
    ppermute x3, starting transfers between devices, over_row(): return lax.ppermute(x, 'prow', [(i, i ^ s) for i in range(rows)])  4.57 us
    unnamed x20, local copies, waits for them, and re-layouts  1.56 us
    ppermute x10, starting transfers between devices, over_core(): return lax.ppermute(x, 'pcol', [(i, i ^ 1) for i in range(cols)])  1.39 us
  transfers between devices with their start and end apart: 25, of which 12 were waited for; matrix products, arithmetic and copies ran while one was open for 0% of the time, Pallas kernels for 7%

profile of v4, /device:TPU:0, one launch (start us, length us, event | category | flops | bytes accessed | tf_op | source)
XLA Modules:
  0.0 67.6 jit_solution(4554483789338988155)
XLA Ops:
  1.2 5.0 %collective-permute-start.10 = (bf16[256,256]{1,0:T(8,128)(2,1)}, bf16[256,256]{1,0:T(8,128)(2,1)S(1)}, u32[]{:S(2)}, u32[]{:S(2)}) collective-permute-start(bf16[256,256]{1,0:T(8,128)(2,1)} %bitcast.20), channel_id=1, source_target_pairs={{0,6},{1,7},{2,4},{3,5},{4,2},{5,3},{6,0},{7,1},{8,14},{9,15},{10,... | collective-permute-start | bytes 393224 | tf_op jit(solution)/shard_map/ppermute | solution.py:275
  6.8 4.0 %collective-permute-done.10 = bf16[256,256]{1,0:T(8,128)(2,1)S(1)} collective-permute-done((bf16[256,256]{1,0:T(8,128)(2,1)}, bf16[256,256]{1,0:T(8,128)(2,1)S(1)}, u32[]{:S(2)}, u32[]{:S(2)}) %collective-permute-start.10) | collective-permute-done | bytes 131104 | tf_op jit(solution)/shard_map/ppermute | solution.py:275
  10.8 3.3 %collective-permute-done.6 = bf16[256,256]{1,0:T(8,128)(2,1)S(1)} collective-permute-done((bf16[256,256]{1,0:T(8,128)(2,1)}, bf16[256,256]{1,0:T(8,128)(2,1)S(1)}, u32[]{:S(2)}, u32[]{:S(2)}) %collective-permute-start.6) | collective-permute-done | bytes 131104 | tf_op jit(solution)/shard_map/ppermute | solution.py:275
  14.6 0.9 %copy-done.1 = bf16[2,1,256,256]{3,2,1,0:T(8,128)(2,1)S(1)} copy-done((bf16[2,1,256,256]{3,2,1,0:T(8,128)(2,1)S(1)}, bf16[2,1,256,256]{3,2,1,0:T(8,128)(2,1)}, u32[]{:S(2)}) %copy-start.1) | copy-done | bytes 262168
  15.6 2.2 %collective-permute-done.8 = bf16[256,256]{1,0:T(8,128)(2,1)S(1)} collective-permute-done((bf16[256,256]{1,0:T(8,128)(2,1)}, bf16[256,256]{1,0:T(8,128)(2,1)S(1)}, u32[]{:S(2)}, u32[]{:S(2)}) %collective-permute-start.8) | collective-permute-done | bytes 131104 | tf_op jit(solution)/shard_map/ppermute | solution.py:275
  17.8 3.0 %collective-permute-start.15 = (bf16[2,256,256]{2,1,0:T(8,128)(2,1)S(1)}, bf16[2,256,256]{2,1,0:T(8,128)(2,1)S(1)}, u32[]{:S(2)}, u32[]{:S(2)}) collective-permute-start(bf16[2,256,256]{2,1,0:T(8,128)(2,1)S(1)} %shard_map.128.refs_0_), channel_id=1, source_target_pairs={{0,4},{1,5},{2,6},{3,7},{4,0},{5,1},{6,2},{7,3},{8,12},{9,13},{10,... | collective-permute-start | bytes 786440 | tf_op jit(solution)/shard_map/ppermute | solution.py:275
  20.8 1.3 %collective-permute-start.16 = (bf16[2,256,256]{2,1,0:T(8,128)(2,1)S(1)}, bf16[2,256,256]{2,1,0:T(8,128)(2,1)S(1)}, u32[]{:S(2)}, u32[]{:S(2)}) collective-permute-start(bf16[2,256,256]{2,1,0:T(8,128)(2,1)S(1)} %shard_map.128.refs_0_), channel_id=1, source_target_pairs={{0,6},{1,7},{2,4},{3,5},{4,2},{5,3},{6,0},{7,1},{8,14},{9,15},{10,... | collective-permute-start | bytes 786440 | tf_op jit(solution)/shard_map/ppermute | solution.py:275
  22.9 0.7 %collective-permute-done.9 = bf16[256,256]{1,0:T(8,128)(2,1)S(1)} collective-permute-done((bf16[256,256]{1,0:T(8,128)(2,1)S(1)}, bf16[256,256]{1,0:T(8,128)(2,1)S(1)}, u32[]{:S(2)}, u32[]{:S(2)}) %collective-permute-start.9) | collective-permute-done | bytes 131104 | tf_op jit(solution)/shard_map/ppermute | solution.py:272
  23.6 18.8 %conditional.1 = (bf16[2,256,128]{2,1,0:T(8,128)(2,1)S(1)}, f32[2,256,256]{2,1,0:T(8,128)S(1)}, bf16[4,64,384]{2,1,0:T(8,128)(2,1)S(1)}) conditional(s32[]{:T(128)} %convert_element_type.3, () %tuple.17, (s32[4,8]{1,0:T(4,128)S(1)}, bf16[8,256,256]{2,1,0:T(8,128)(2,1)}, bf16[8,256,256]{2,1,0:T(8,128)(2,1)S(1)}, bf16[256,256]{1,0:T(8,128)(2,1)}, ...), branch_computations={%region_0.0_spmd, %region_1.0_spmd} | conditional | bytes 3408056 | solution.py:350
  23.7 2.5 %branch_1_fun.3 = (bf16[3,256,128]{2,1,0:T(8,128)(2,1)S(1)}, bf16[4,64,128]{2,1,0:T(8,128)(2,1)S(1)}) custom-call(s32[4,8]{1,0:T(4,128)S(1)} %get-tuple-element.32.us_ref, bf16[8,256,256]{2,1,0:T(8,128)(2,1)} %get-tuple-element.33.to_ref, bf16[8,256,256]{2,1,0:T(8,128)(2,1)S(1)} %get-tuple-element.34.ts_ref, bf16[256,256]{1,0:T(8,128)(2,1)} %get-tuple-element.35.refs_0_, ...), custom_call_target="tpu_custom_call" | custom-call | tf_op jit(solution)/shard_map/cond/branch_1_fun/pallas_call | solution.py:297
  26.2 1.6 %collective-permute-start.1 = (bf16[3,256,128]{2,1,0:T(8,128)(2,1)S(1)}, bf16[3,256,128]{2,1,0:T(8,128)(2,1)S(1)}, u32[]{:S(2)}, u32[]{:S(2)}) collective-permute-start(bf16[3,256,128]{2,1,0:T(8,128)(2,1)S(1)} %get-tuple-element.44.refs_0_), channel_id=1, source_target_pairs={{0,16},{8,24},{16,0},{24,8},{1,17},{9,25},{17,1},{25,9},{2,18},{10... | collective-permute-start | bytes 589832 | tf_op jit(solution)/shard_map/cond/branch_1_fun/ppermute | solution.py:278
  27.7 1.5 %collective-permute-start = (bf16[3,256,128]{2,1,0:T(8,128)(2,1)S(1)}, bf16[3,256,128]{2,1,0:T(8,128)(2,1)S(1)}, u32[]{:S(2)}, u32[]{:S(2)}) collective-permute-start(bf16[3,256,128]{2,1,0:T(8,128)(2,1)S(1)} %get-tuple-element.44.refs_0_), channel_id=1, source_target_pairs={{0,8},{8,0},{16,24},{24,16},{1,9},{9,1},{17,25},{25,17},{2,10},{10... | collective-permute-start | bytes 589832 | tf_op jit(solution)/shard_map/cond/branch_1_fun/ppermute | solution.py:278
  29.2 3.9 %collective-permute-done.1.refs_2_ = bf16[3,256,128]{2,1,0:T(8,128)(2,1)S(1)} collective-permute-done((bf16[3,256,128]{2,1,0:T(8,128)(2,1)S(1)}, bf16[3,256,128]{2,1,0:T(8,128)(2,1)S(1)}, u32[]{:S(2)}, u32[]{:S(2)}) %collective-permute-start.1) | collective-permute-done | bytes 196640 | tf_op jit(solution)/shard_map/cond/branch_1_fun/ppermute | solution.py:278
  33.2 1.5 %collective-permute-start.2 = (bf16[3,256,128]{2,1,0:T(8,128)(2,1)S(1)}, bf16[3,256,128]{2,1,0:T(8,128)(2,1)S(1)}, u32[]{:S(2)}, u32[]{:S(2)}) collective-permute-start(bf16[3,256,128]{2,1,0:T(8,128)(2,1)S(1)} %collective-permute-done.1.refs_2_), channel_id=1, source_target_pairs={{0,8},{8,0},{16,24},{24,16},{1,9},{9,1},{17,25},{25,17},{2,10},{10... | collective-permute-start | bytes 589832 | tf_op jit(solution)/shard_map/cond/branch_1_fun/ppermute | solution.py:278
  34.7 4.6 %collective-permute-done.2.refs_3_ = bf16[3,256,128]{2,1,0:T(8,128)(2,1)S(1)} collective-permute-done((bf16[3,256,128]{2,1,0:T(8,128)(2,1)S(1)}, bf16[3,256,128]{2,1,0:T(8,128)(2,1)S(1)}, u32[]{:S(2)}, u32[]{:S(2)}) %collective-permute-start.2) | collective-permute-done | bytes 196640 | tf_op jit(solution)/shard_map/cond/branch_1_fun/ppermute | solution.py:278
  39.3 0.6 branch_1_fun.4
  40.0 1.4 %collective-permute-done.3.got_ref = bf16[3,256,128]{2,1,0:T(8,128)(2,1)S(1)} collective-permute-done((bf16[3,256,128]{2,1,0:T(8,128)(2,1)S(1)}, bf16[3,256,128]{2,1,0:T(8,128)(2,1)S(1)}, u32[]{:S(2)}, u32[]{:S(2)}) %collective-permute-start.3) | collective-permute-done | bytes 196640 | tf_op jit(solution)/shard_map/cond/branch_1_fun/ppermute | solution.py:272
  41.4 1.0 %branch_1_fun.5 = (f32[2,256,256]{2,1,0:T(8,128)S(1)}, bf16[4,64,384]{2,1,0:T(8,128)(2,1)S(1)}) custom-call(s32[4,8]{1,0:T(4,128)S(1)} %get-tuple-element.32.us_ref, s32[8]{0:T(128)S(1)} %get-tuple-element.45.co_ref, s32[2,8]{1,0:T(2,128)S(1)} %get-tuple-element.46.ck_ref, bf16[3,256,128]{2,1,0:T(8,128)(2,1)S(1)} %get-tuple-element.47.keep_ref, ...), custom_call_target="tpu_custom_call" | custom-call | tf_op jit(solution)/shard_map/cond/branch_1_fun/pallas_call | solution.py:297
  42.5 2.3 %shard_map.129 = (bf16[256,256]{1,0:T(8,128)(2,1)S(1)}, bf16[256,256]{1,0:T(8,128)(2,1)S(1)}, bf16[4,64,640]{2,1,0:T(8,128)(2,1)S(1)}) custom-call(s32[4,8]{1,0:T(4,128)S(1)} %copy-done.7, s32[8]{0:T(128)S(1)} %copy-done.8, s32[2,8]{1,0:T(2,128)S(1)} %copy-done.9, bf16[8,256,256]{2,1,0:T(8,128)(2,1)} %bitcast.18, ...), custom_call_target="tpu_custom_call" | custom-call | tf_op jit(solution)/shard_map/pallas_call | solution.py:297
  44.9 1.2 %collective-permute-start.18 = (bf16[64,640]{1,0:T(8,128)(2,1)S(1)}, bf16[64,640]{1,0:T(8,128)(2,1)S(1)}, u32[]{:S(2)}, u32[]{:S(2)}) collective-permute-start(bf16[64,640]{1,0:T(8,128)(2,1)S(1)} %get-tuple-element.88), channel_id=1, source_target_pairs={{0,2},{1,3},{2,0},{3,1},{4,6},{5,7},{6,4},{7,5},{8,10},{9,11},{10,... | collective-permute-start | bytes 245768 | tf_op jit(solution)/shard_map/ppermute | solution.py:275
  46.1 1.9 %collective-permute-start.19 = (bf16[64,640]{1,0:T(8,128)(2,1)S(1)}, bf16[64,640]{1,0:T(8,128)(2,1)S(1)}, u32[]{:S(2)}, u32[]{:S(2)}) collective-permute-start(bf16[64,640]{1,0:T(8,128)(2,1)S(1)} %get-tuple-element.87), channel_id=1, source_target_pairs={{0,4},{1,5},{2,6},{3,7},{4,0},{5,1},{6,2},{7,3},{8,12},{9,13},{10,... | collective-permute-start | bytes 245768 | tf_op jit(solution)/shard_map/ppermute | solution.py:275
  48.0 1.3 %collective-permute-start.20 = (bf16[64,640]{1,0:T(8,128)(2,1)S(1)}, bf16[64,640]{1,0:T(8,128)(2,1)S(1)}, u32[]{:S(2)}, u32[]{:S(2)}) collective-permute-start(bf16[64,640]{1,0:T(8,128)(2,1)S(1)} %get-tuple-element.86), channel_id=1, source_target_pairs={{0,6},{1,7},{2,4},{3,5},{4,2},{5,3},{6,0},{7,1},{8,14},{9,15},{10,... | collective-permute-start | bytes 245768 | tf_op jit(solution)/shard_map/ppermute | solution.py:275
  49.3 1.0 %collective-permute-done.18.refs_0_ = bf16[64,640]{1,0:T(8,128)(2,1)S(1)} collective-permute-done((bf16[64,640]{1,0:T(8,128)(2,1)S(1)}, bf16[64,640]{1,0:T(8,128)(2,1)S(1)}, u32[]{:S(2)}, u32[]{:S(2)}) %collective-permute-start.18) | collective-permute-done | bytes 81952 | tf_op jit(solution)/shard_map/ppermute | solution.py:275
  50.3 4.8 %collective-permute-done.19.refs_1_ = bf16[64,640]{1,0:T(8,128)(2,1)S(1)} collective-permute-done((bf16[64,640]{1,0:T(8,128)(2,1)S(1)}, bf16[64,640]{1,0:T(8,128)(2,1)S(1)}, u32[]{:S(2)}, u32[]{:S(2)}) %collective-permute-start.19) | collective-permute-done | bytes 81952 | tf_op jit(solution)/shard_map/ppermute | solution.py:275
  55.2 1.5 %collective-permute-start.21 = (bf16[64,640]{1,0:T(8,128)(2,1)S(1)}, bf16[64,640]{1,0:T(8,128)(2,1)S(1)}, u32[]{:S(2)}, u32[]{:S(2)}) collective-permute-start(bf16[64,640]{1,0:T(8,128)(2,1)S(1)} %shard_map.131.refs_0_), channel_id=1, source_target_pairs={{0,2},{1,3},{2,0},{3,1},{4,6},{5,7},{6,4},{7,5},{8,10},{9,11},{10,... | collective-permute-start | bytes 245768 | tf_op jit(solution)/shard_map/ppermute | solution.py:275
  56.7 1.3 %collective-permute-start.22 = (bf16[64,640]{1,0:T(8,128)(2,1)S(1)}, bf16[64,640]{1,0:T(8,128)(2,1)S(1)}, u32[]{:S(2)}, u32[]{:S(2)}) collective-permute-start(bf16[64,640]{1,0:T(8,128)(2,1)S(1)} %shard_map.131.refs_0_), channel_id=1, source_target_pairs={{0,4},{1,5},{2,6},{3,7},{4,0},{5,1},{6,2},{7,3},{8,12},{9,13},{10,... | collective-permute-start | bytes 245768 | tf_op jit(solution)/shard_map/ppermute | solution.py:275
  58.0 1.7 %collective-permute-start.23 = (bf16[64,640]{1,0:T(8,128)(2,1)S(1)}, bf16[64,640]{1,0:T(8,128)(2,1)S(1)}, u32[]{:S(2)}, u32[]{:S(2)}) collective-permute-start(bf16[64,640]{1,0:T(8,128)(2,1)S(1)} %shard_map.131.refs_0_), channel_id=1, source_target_pairs={{0,6},{1,7},{2,4},{3,5},{4,2},{5,3},{6,0},{7,1},{8,14},{9,15},{10,... | collective-permute-start | bytes 245768 | tf_op jit(solution)/shard_map/ppermute | solution.py:275
  59.7 1.2 %collective-permute-done.13.u_got_ref = bf16[256,128]{1,0:T(8,128)(2,1)S(1)} collective-permute-done((bf16[256,128]{1,0:T(8,128)(2,1)S(1)}, bf16[256,128]{1,0:T(8,128)(2,1)S(1)}, u32[]{:S(2)}, u32[]{:S(2)}) %collective-permute-start.13) | collective-permute-done | bytes 65568 | tf_op jit(solution)/shard_map/ppermute | solution.py:272
  61.0 0.8 %shard_map.130 = (bf16[1,1,256,256]{3,2,1,0:T(8,128)(2,1)}, bf16[2,1,256,256]{3,2,1,0:T(8,128)(2,1)}, f32[2,256,256]{2,1,0:T(8,128)S(1)}) custom-call(bf16[256,128]{1,0:T(8,128)(2,1)S(1)} %get-tuple-element.90.u_own_ref, bf16[256,128]{1,0:T(8,128)(2,1)S(1)} %collective-permute-done.13.u_got_ref, bf16[256,256]{1,0:T(8,128)(2,1)S(1)} %get-tuple-element.76.l_own_ref, ...), custom_call_target="tpu_custom_call" | custom-call | tf_op jit(solution)/shard_map/pallas_call | solution.py:297
  61.8 2.9 %collective-permute-done.22.refs_2_ = bf16[64,640]{1,0:T(8,128)(2,1)S(1)} collective-permute-done((bf16[64,640]{1,0:T(8,128)(2,1)S(1)}, bf16[64,640]{1,0:T(8,128)(2,1)S(1)}, u32[]{:S(2)}, u32[]{:S(2)}) %collective-permute-start.22) | collective-permute-done | bytes 81952 | tf_op jit(solution)/shard_map/ppermute | solution.py:275
  64.8 1.6 %collective-permute-done.24.got_ref = bf16[256,640]{1,0:T(8,128)(2,1)S(1)} collective-permute-done((bf16[256,640]{1,0:T(8,128)(2,1)S(1)}, bf16[256,640]{1,0:T(8,128)(2,1)S(1)}, u32[]{:S(2)}, u32[]{:S(2)}) %collective-permute-start.24) | collective-permute-done | bytes 327712 | tf_op jit(solution)/shard_map/ppermute | solution.py:272
  66.4 1.2 %shard_map.133 = (f32[1,256,256]{2,1,0:T(8,128)}, bf16[2,256,256]{2,1,0:T(8,128)(2,1)}, f32[2,256,256]{2,1,0:T(8,128)}) custom-call(bf16[256,640]{1,0:T(8,128)(2,1)S(1)} %shard_map.132.own_ref, bf16[256,640]{1,0:T(8,128)(2,1)S(1)} %collective-permute-done.24.got_ref, f32[1,256,256]{2,1,0:T(8,128)S(1)} %copy-done.2, bf16[2,256,256]{2,1,0:T(8,128)(2,1)S(1)} %copy-done.3, ...), custom_call_target="tpu_custom_call" | custom-call | tf_op jit(solution)/shard_map/pallas_call | solution.py:297
  (51 shorter events, 2.8 us)
Async XLA Ops:
  0.6 23.0 %collective-permute-start.4 = (bf16[8,256,256]{2,1,0:T(8,128)(2,1)}, bf16[8,256,256]{2,1,0:T(8,128)(2,1)S(1)}, u32[]{:S(2)}, u32[]{:S(2)}) collective-permute-start(bf16[8,256,256]{2,1,0:T(8,128)(2,1)} %bitcast.16), channel_id=1, source_target_pairs={{0,1},{1,0},{2,3},{3,2},{4,5},{5,4},{6,7},{7,6},{8,9},{9,8},{10,11... | collective-permute-start | bytes 3145736 | tf_op jit(solution)/shard_map/ppermute | solution.py:272
  1.1 13.0 %collective-permute-start.12 = (bf16[2,256,256]{2,1,0:T(8,128)(2,1)}, bf16[2,256,256]{2,1,0:T(8,128)(2,1)S(1)}, u32[]{:S(2)}, u32[]{:S(2)}) collective-permute-start(bf16[2,256,256]{2,1,0:T(8,128)(2,1)} %bitcast.14), channel_id=1, source_target_pairs={{0,1},{1,0},{2,3},{3,2},{4,5},{5,4},{6,7},{7,6},{8,9},{9,8},{10,11... | collective-permute-start | bytes 786440 | tf_op jit(solution)/shard_map/ppermute | solution.py:272
  1.2 9.6 %collective-permute-start.10 = (bf16[256,256]{1,0:T(8,128)(2,1)}, bf16[256,256]{1,0:T(8,128)(2,1)S(1)}, u32[]{:S(2)}, u32[]{:S(2)}) collective-permute-start(bf16[256,256]{1,0:T(8,128)(2,1)} %bitcast.20), channel_id=1, source_target_pairs={{0,6},{1,7},{2,4},{3,5},{4,2},{5,3},{6,0},{7,1},{8,14},{9,15},{10,... | collective-permute-start | bytes 393224 | tf_op jit(solution)/shard_map/ppermute | solution.py:275
  6.3 7.9 %collective-permute-start.6 = (bf16[256,256]{1,0:T(8,128)(2,1)}, bf16[256,256]{1,0:T(8,128)(2,1)S(1)}, u32[]{:S(2)}, u32[]{:S(2)}) collective-permute-start(bf16[256,256]{1,0:T(8,128)(2,1)} %bitcast.21), channel_id=1, source_target_pairs={{0,2},{1,3},{2,0},{3,1},{4,6},{5,7},{6,4},{7,5},{8,10},{9,11},{10,... | collective-permute-start | bytes 393224 | tf_op jit(solution)/shard_map/ppermute | solution.py:275
  6.3 11.5 %collective-permute-start.8 = (bf16[256,256]{1,0:T(8,128)(2,1)}, bf16[256,256]{1,0:T(8,128)(2,1)S(1)}, u32[]{:S(2)}, u32[]{:S(2)}) collective-permute-start(bf16[256,256]{1,0:T(8,128)(2,1)} %bitcast.22), channel_id=1, source_target_pairs={{0,4},{1,5},{2,6},{3,7},{4,0},{5,1},{6,2},{7,3},{8,12},{9,13},{10,... | collective-permute-start | bytes 393224 | tf_op jit(solution)/shard_map/ppermute | solution.py:275
  10.8 7.0 %collective-permute-start.5 = (bf16[256,256]{1,0:T(8,128)(2,1)}, bf16[256,256]{1,0:T(8,128)(2,1)}, u32[]{:S(2)}, u32[]{:S(2)}) collective-permute-start(bf16[256,256]{1,0:T(8,128)(2,1)} %bitcast.23), channel_id=1, source_target_pairs={{0,1},{1,0},{2,3},{3,2},{4,5},{5,4},{6,7},{7,6},{8,9},{9,8},{10,11... | collective-permute-start | bytes 393224 | tf_op jit(solution)/shard_map/ppermute | solution.py:272
  14.1 1.5 %copy-start.4 = (bf16[256,256]{1,0:T(8,128)(2,1)}, bf16[256,256]{1,0:T(8,128)(2,1)S(1)}, u32[]{:S(2)}) copy-start(bf16[256,256]{1,0:T(8,128)(2,1)S(1)} %collective-permute-done.6) | copy-start | bytes 393220
  14.1 6.7 %collective-permute-start.11 = (bf16[256,256]{1,0:T(8,128)(2,1)S(1)}, bf16[256,256]{1,0:T(8,128)(2,1)S(1)}, u32[]{:S(2)}, u32[]{:S(2)}) collective-permute-start(bf16[256,256]{1,0:T(8,128)(2,1)S(1)} %collective-permute-done.10), channel_id=1, source_target_pairs={{0,1},{1,0},{2,3},{3,2},{4,5},{5,4},{6,7},{7,6},{8,9},{9,8},{10,11... | collective-permute-start | bytes 393224 | tf_op jit(solution)/shard_map/ppermute | solution.py:272
  14.1 8.1 %collective-permute-start.7 = (bf16[256,256]{1,0:T(8,128)(2,1)S(1)}, bf16[256,256]{1,0:T(8,128)(2,1)S(1)}, u32[]{:S(2)}, u32[]{:S(2)}) collective-permute-start(bf16[256,256]{1,0:T(8,128)(2,1)S(1)} %collective-permute-done.6), channel_id=1, source_target_pairs={{0,1},{1,0},{2,3},{3,2},{4,5},{5,4},{6,7},{7,6},{8,9},{9,8},{10,11... | collective-permute-start | bytes 393224 | tf_op jit(solution)/shard_map/ppermute | solution.py:272
  14.6 0.9 %copy-start.1 = (bf16[2,1,256,256]{3,2,1,0:T(8,128)(2,1)S(1)}, bf16[2,1,256,256]{3,2,1,0:T(8,128)(2,1)}, u32[]{:S(2)}) copy-start(bf16[2,1,256,256]{3,2,1,0:T(8,128)(2,1)} %param.17) | copy-start | bytes 786436
  15.6 8.0 %copy-start.2 = (f32[1,256,256]{2,1,0:T(8,128)S(1)}, f32[1,256,256]{2,1,0:T(8,128)}, u32[]{:S(2)}) copy-start(f32[1,256,256]{2,1,0:T(8,128)} %d_ref.3) | copy-start | bytes 786436
  15.6 8.0 %copy-start.3 = (bf16[2,256,256]{2,1,0:T(8,128)(2,1)S(1)}, bf16[2,256,256]{2,1,0:T(8,128)(2,1)}, u32[]{:S(2)}) copy-start(bf16[2,256,256]{2,1,0:T(8,128)(2,1)} %pp_ref.1) | copy-start | bytes 786436
  17.8 24.7 %collective-permute-start.14 = (bf16[2,256,256]{2,1,0:T(8,128)(2,1)S(1)}, bf16[2,256,256]{2,1,0:T(8,128)(2,1)S(1)}, u32[]{:S(2)}, u32[]{:S(2)}) collective-permute-start(bf16[2,256,256]{2,1,0:T(8,128)(2,1)S(1)} %shard_map.128.refs_0_), channel_id=1, source_target_pairs={{0,2},{1,3},{2,0},{3,1},{4,6},{5,7},{6,4},{7,5},{8,10},{9,11},{10,... | collective-permute-start | bytes 786440 | tf_op jit(solution)/shard_map/ppermute | solution.py:275
  17.8 24.7 %collective-permute-start.15 = (bf16[2,256,256]{2,1,0:T(8,128)(2,1)S(1)}, bf16[2,256,256]{2,1,0:T(8,128)(2,1)S(1)}, u32[]{:S(2)}, u32[]{:S(2)}) collective-permute-start(bf16[2,256,256]{2,1,0:T(8,128)(2,1)S(1)} %shard_map.128.refs_0_), channel_id=1, source_target_pairs={{0,4},{1,5},{2,6},{3,7},{4,0},{5,1},{6,2},{7,3},{8,12},{9,13},{10,... | collective-permute-start | bytes 786440 | tf_op jit(solution)/shard_map/ppermute | solution.py:275
  20.8 1.4 %copy-start.5 = (bf16[256,256]{1,0:T(8,128)(2,1)}, bf16[256,256]{1,0:T(8,128)(2,1)S(1)}, u32[]{:S(2)}) copy-start(bf16[256,256]{1,0:T(8,128)(2,1)S(1)} %collective-permute-done.11) | copy-start | bytes 393220
  20.8 21.7 %collective-permute-start.16 = (bf16[2,256,256]{2,1,0:T(8,128)(2,1)S(1)}, bf16[2,256,256]{2,1,0:T(8,128)(2,1)S(1)}, u32[]{:S(2)}, u32[]{:S(2)}) collective-permute-start(bf16[2,256,256]{2,1,0:T(8,128)(2,1)S(1)} %shard_map.128.refs_0_), channel_id=1, source_target_pairs={{0,6},{1,7},{2,4},{3,5},{4,2},{5,3},{6,0},{7,1},{8,14},{9,15},{10,... | collective-permute-start | bytes 786440 | tf_op jit(solution)/shard_map/ppermute | solution.py:275
  22.2 1.4 %collective-permute-start.9 = (bf16[256,256]{1,0:T(8,128)(2,1)S(1)}, bf16[256,256]{1,0:T(8,128)(2,1)S(1)}, u32[]{:S(2)}, u32[]{:S(2)}) collective-permute-start(bf16[256,256]{1,0:T(8,128)(2,1)S(1)} %collective-permute-done.8), channel_id=1, source_target_pairs={{0,1},{1,0},{2,3},{3,2},{4,5},{5,4},{6,7},{7,6},{8,9},{9,8},{10,11... | collective-permute-start | bytes 393224 | tf_op jit(solution)/shard_map/ppermute | solution.py:272
  22.9 0.8 %copy-start.9 = (s32[2,8]{1,0:T(2,128)S(1)}, s32[2,8]{1,0:T(2,128)}, u32[]{:S(2)}) copy-start(s32[2,8]{1,0:T(2,128)} %ck_ref.1) | copy-start | bytes 196
  26.2 7.0 %collective-permute-start.1 = (bf16[3,256,128]{2,1,0:T(8,128)(2,1)S(1)}, bf16[3,256,128]{2,1,0:T(8,128)(2,1)S(1)}, u32[]{:S(2)}, u32[]{:S(2)}) collective-permute-start(bf16[3,256,128]{2,1,0:T(8,128)(2,1)S(1)} %get-tuple-element.44.refs_0_), channel_id=1, source_target_pairs={{0,16},{8,24},{16,0},{24,8},{1,17},{9,25},{17,1},{25,9},{2,18},{10... | collective-permute-start | bytes 589832 | tf_op jit(solution)/shard_map/cond/branch_1_fun/ppermute | solution.py:278
  27.7 6.9 %collective-permute-start = (bf16[3,256,128]{2,1,0:T(8,128)(2,1)S(1)}, bf16[3,256,128]{2,1,0:T(8,128)(2,1)S(1)}, u32[]{:S(2)}, u32[]{:S(2)}) collective-permute-start(bf16[3,256,128]{2,1,0:T(8,128)(2,1)S(1)} %get-tuple-element.44.refs_0_), channel_id=1, source_target_pairs={{0,8},{8,0},{16,24},{24,16},{1,9},{9,1},{17,25},{25,17},{2,10},{10... | collective-permute-start | bytes 589832 | tf_op jit(solution)/shard_map/cond/branch_1_fun/ppermute | solution.py:278
  33.2 6.1 %collective-permute-start.2 = (bf16[3,256,128]{2,1,0:T(8,128)(2,1)S(1)}, bf16[3,256,128]{2,1,0:T(8,128)(2,1)S(1)}, u32[]{:S(2)}, u32[]{:S(2)}) collective-permute-start(bf16[3,256,128]{2,1,0:T(8,128)(2,1)S(1)} %collective-permute-done.1.refs_2_), channel_id=1, source_target_pairs={{0,8},{8,0},{16,24},{24,16},{1,9},{9,1},{17,25},{25,17},{2,10},{10... | collective-permute-start | bytes 589832 | tf_op jit(solution)/shard_map/cond/branch_1_fun/ppermute | solution.py:278
  39.9 1.5 %collective-permute-start.3 = (bf16[3,256,128]{2,1,0:T(8,128)(2,1)S(1)}, bf16[3,256,128]{2,1,0:T(8,128)(2,1)S(1)}, u32[]{:S(2)}, u32[]{:S(2)}) collective-permute-start(bf16[3,256,128]{2,1,0:T(8,128)(2,1)S(1)} %get-tuple-element.48), channel_id=1, source_target_pairs={{0,1},{1,0},{2,3},{3,2},{4,5},{5,4},{6,7},{7,6},{8,9},{9,8},{10,11... | collective-permute-start | bytes 589832 | tf_op jit(solution)/shard_map/cond/branch_1_fun/ppermute | solution.py:272
  44.9 16.1 %copy-start = (f32[2,256,256]{2,1,0:T(8,128)S(1)}, f32[2,256,256]{2,1,0:T(8,128)}, u32[]{:S(2)}) copy-start(f32[2,256,256]{2,1,0:T(8,128)} %d_ref.2) | copy-start | bytes 1572868
  44.9 5.4 %collective-permute-start.18 = (bf16[64,640]{1,0:T(8,128)(2,1)S(1)}, bf16[64,640]{1,0:T(8,128)(2,1)S(1)}, u32[]{:S(2)}, u32[]{:S(2)}) collective-permute-start(bf16[64,640]{1,0:T(8,128)(2,1)S(1)} %get-tuple-element.88), channel_id=1, source_target_pairs={{0,2},{1,3},{2,0},{3,1},{4,6},{5,7},{6,4},{7,5},{8,10},{9,11},{10,... | collective-permute-start | bytes 245768 | tf_op jit(solution)/shard_map/ppermute | solution.py:275
  46.1 9.1 %collective-permute-start.19 = (bf16[64,640]{1,0:T(8,128)(2,1)S(1)}, bf16[64,640]{1,0:T(8,128)(2,1)S(1)}, u32[]{:S(2)}, u32[]{:S(2)}) collective-permute-start(bf16[64,640]{1,0:T(8,128)(2,1)S(1)} %get-tuple-element.87), channel_id=1, source_target_pairs={{0,4},{1,5},{2,6},{3,7},{4,0},{5,1},{6,2},{7,3},{8,12},{9,13},{10,... | collective-permute-start | bytes 245768 | tf_op jit(solution)/shard_map/ppermute | solution.py:275
  48.0 7.1 %collective-permute-start.20 = (bf16[64,640]{1,0:T(8,128)(2,1)S(1)}, bf16[64,640]{1,0:T(8,128)(2,1)S(1)}, u32[]{:S(2)}, u32[]{:S(2)}) collective-permute-start(bf16[64,640]{1,0:T(8,128)(2,1)S(1)} %get-tuple-element.86), channel_id=1, source_target_pairs={{0,6},{1,7},{2,4},{3,5},{4,2},{5,3},{6,0},{7,1},{8,14},{9,15},{10,... | collective-permute-start | bytes 245768 | tf_op jit(solution)/shard_map/ppermute | solution.py:275
  49.3 11.6 %collective-permute-start.17 = (bf16[256,256]{1,0:T(8,128)(2,1)S(1)}, bf16[256,256]{1,0:T(8,128)(2,1)S(1)}, u32[]{:S(2)}, u32[]{:S(2)}) collective-permute-start(bf16[256,256]{1,0:T(8,128)(2,1)S(1)} %get-tuple-element.77), channel_id=1, source_target_pairs={{0,1},{1,0},{2,3},{3,2},{4,5},{5,4},{6,7},{7,6},{8,9},{9,8},{10,11... | collective-permute-start | bytes 393224 | tf_op jit(solution)/shard_map/ppermute | solution.py:272
  55.2 6.6 %collective-permute-start.21 = (bf16[64,640]{1,0:T(8,128)(2,1)S(1)}, bf16[64,640]{1,0:T(8,128)(2,1)S(1)}, u32[]{:S(2)}, u32[]{:S(2)}) collective-permute-start(bf16[64,640]{1,0:T(8,128)(2,1)S(1)} %shard_map.131.refs_0_), channel_id=1, source_target_pairs={{0,2},{1,3},{2,0},{3,1},{4,6},{5,7},{6,4},{7,5},{8,10},{9,11},{10,... | collective-permute-start | bytes 245768 | tf_op jit(solution)/shard_map/ppermute | solution.py:275
  56.7 8.0 %collective-permute-start.22 = (bf16[64,640]{1,0:T(8,128)(2,1)S(1)}, bf16[64,640]{1,0:T(8,128)(2,1)S(1)}, u32[]{:S(2)}, u32[]{:S(2)}) collective-permute-start(bf16[64,640]{1,0:T(8,128)(2,1)S(1)} %shard_map.131.refs_0_), channel_id=1, source_target_pairs={{0,4},{1,5},{2,6},{3,7},{4,0},{5,1},{6,2},{7,3},{8,12},{9,13},{10,... | collective-permute-start | bytes 245768 | tf_op jit(solution)/shard_map/ppermute | solution.py:275
  58.0 6.7 %collective-permute-start.23 = (bf16[64,640]{1,0:T(8,128)(2,1)S(1)}, bf16[64,640]{1,0:T(8,128)(2,1)S(1)}, u32[]{:S(2)}, u32[]{:S(2)}) collective-permute-start(bf16[64,640]{1,0:T(8,128)(2,1)S(1)} %shard_map.131.refs_0_), channel_id=1, source_target_pairs={{0,6},{1,7},{2,4},{3,5},{4,2},{5,3},{6,0},{7,1},{8,14},{9,15},{10,... | collective-permute-start | bytes 245768 | tf_op jit(solution)/shard_map/ppermute | solution.py:275
  59.6 1.3 %collective-permute-start.13 = (bf16[256,128]{1,0:T(8,128)(2,1)S(1)}, bf16[256,128]{1,0:T(8,128)(2,1)S(1)}, u32[]{:S(2)}, u32[]{:S(2)}) collective-permute-start(bf16[256,128]{1,0:T(8,128)(2,1)S(1)} %get-tuple-element.89), channel_id=1, source_target_pairs={{0,1},{1,0},{2,3},{3,2},{4,5},{5,4},{6,7},{7,6},{8,9},{9,8},{10,11... | collective-permute-start | bytes 196616 | tf_op jit(solution)/shard_map/ppermute | solution.py:272
  64.7 1.7 %collective-permute-start.24 = (bf16[256,640]{1,0:T(8,128)(2,1)S(1)}, bf16[256,640]{1,0:T(8,128)(2,1)S(1)}, u32[]{:S(2)}, u32[]{:S(2)}) collective-permute-start(bf16[256,640]{1,0:T(8,128)(2,1)S(1)} %shard_map.132.own_ref), channel_id=1, source_target_pairs={{0,1},{1,0},{2,3},{3,2},{4,5},{5,4},{6,7},{7,6},{8,9},{9,8},{10,11... | collective-permute-start | bytes 983048 | tf_op jit(solution)/shard_map/ppermute | solution.py:272
  (3 other events, 2.2 us)

commit v5 on v4

--- a/solution.py
+++ b/solution.py
@@ -101,7 +101,7 @@
     return lax.axis_index("prow"), col // CORES, col % CORES
 
 
-def upper_body(nz, us_ref, to_ref, ts_ref, *refs):
+def upper_body(nz, flags_ref, to_ref, ts_ref, *refs):
     pairs = [(refs[2 * s], refs[2 * s + 1]) for s in range(nz)]
     d_hbm, rx_ref, ud_ref, xs, d_ref, sem = refs[2 * nz :]
     row, z, c = place()
@@ -113,7 +113,7 @@
     for s in range(nz):
         for q in range(CORES):
             i = CORES * (z ^ s) + (c if q == 0 else 1 - c)
-            flag = us_ref[row, i].astype(F32).astype(BF)
+            flag = flags_ref[pl.ds(CORES * s + q, 1), :half].astype(BF)
             panel = pairs[s][q][...]
             piece = jnp.where(c == 0, panel[:, :half], panel[:, half:]) * flag
             for p, t_ref in enumerate((to_ref, ts_ref)):
@@ -122,8 +122,7 @@
     copy.wait()
     x = None
     for p, u_ref in enumerate(pairs[0]):
-        j = CORES * z + (c if p == 0 else 1 - c)
-        flag = us_ref[row, j].astype(F32)
+        flag = flags_ref[pl.ds(p, 1), :half]
         block = (-(flag * acc[p])).astype(BF)
         rx_ref[p] = block
         prod = dot_t(u_ref[...], block)
@@ -137,32 +136,30 @@
     rx_ref[CORES] = xs[...].astype(BF)
 
 
-def pick_body(rows, co_ref, *refs):
-    blocks, (keep_ref, give_ref) = refs[:rows], refs[-2:]
-    row, _, c = place()
-    for k, out_ref in ((c, keep_ref), (1 - c, give_ref)):
-        index = (co_ref[CORES * row + k] // CH) ^ row
+def pick_body(nz, rows, flags_ref, *refs):
+    blocks, outs = refs[:rows], refs[-2:]
+    half = outs[0].shape[2]
+    for k, out_ref in enumerate(outs):
+        total = None
         for s, block in enumerate(blocks):
-
-            @pl.when(index == s)
-            def _(out_ref=out_ref, block=block):
-                out_ref[...] = block[...]
-
-
-def parent_body(nz, us_ref, co_ref, ck_ref, keep_ref, got_ref, pp_ref, l_ref, ud_ref,
+            flag = flags_ref[pl.ds(2 * CORES * nz + rows * k + s, 1), :half].astype(BF)
+            part = block[...] * flag
+            total = part if total is None else total + part
+        out_ref[...] = total
+
+
+def parent_body(nz, flags_ref, keep_ref, got_ref, pp_ref, l_ref, ud_ref,
                 w_ref, rs_ref, a_ref):
-    row, z, c = place()
+    _, z, c = place()
     half = keep_ref.shape[2]
     size = pp_ref.shape[1]
     quarter = size // nz
     mine = pl.ds(pl.multiple_of(c * half, half), half)
     other = pl.ds(pl.multiple_of((1 - c) * half, half), half)
-    parent = co_ref[CORES * row + c] // CH
     p_mine, p_other = pp_ref[c, mine, :], pp_ref[c, other, :]
     a_ref[...] = dot(keep_ref[CORES], p_mine) + dot(got_ref[CORES], p_other)
     for p in range(CORES):
-        j = CORES * z + (c if p == 0 else 1 - c)
-        flag = (us_ref[parent, j] * ck_ref[c, j]).astype(F32).astype(BF)
+        flag = flags_ref[pl.ds(CORES * nz + p, 1), :].astype(BF)
         k_half, g_half = keep_ref[p], got_ref[1 - p]
         w_ref[p] = dot(k_half, p_mine) + dot(g_half, p_other)
         masked = l_ref[p] * flag
@@ -174,23 +171,21 @@
         rs_ref[s, :, size:] = ud_ref[s]
 
 
-def lower_body(nz, us_ref, co_ref, ck_ref, to_ref, ts_ref, w_ref, rs1_ref, *refs):
+def lower_body(nz, flags_ref, to_ref, ts_ref, w_ref, rs1_ref, *refs):
     stacks, (lo_ref, lg_ref, rs_ref, r_ref) = refs[:nz], refs[-4:]
-    row, z, c = place()
+    _, z, c = place()
     quarter = r_ref.shape[0] // nz
-    parent = co_ref[CORES * row + c] // CH
     acc = [w_ref[0], w_ref[1]]
     for s in range(nz):
         for q in range(CORES):
             i = CORES * (z ^ s) + (c if q == 0 else 1 - c)
-            flag = (us_ref[parent, i] * ck_ref[c, i]).astype(F32).astype(BF)
+            flag = flags_ref[pl.ds(CORES * nz + CORES * s + q, 1), :].astype(BF)
             piece = stacks[s][q] * flag
             for p, t_ref in enumerate((to_ref, ts_ref)):
                 acc[p] = acc[p] + dot(t_ref[i], piece)
     total = None
     for p, o_ref in enumerate((lo_ref, lg_ref)):
-        j = CORES * z + (c if p == 0 else 1 - c)
-        flag = (us_ref[parent, j] * ck_ref[c, j]).astype(F32)
+        flag = flags_ref[pl.ds(CORES * nz + p, 1), :]
         block = (-(flag * acc[p])).astype(BF)
         o_ref[...] = block
         prod = dot_t(stacks[0][p], block)
@@ -203,10 +198,22 @@
         rs_ref[s, :, size:] = rs1_ref[s]
 
 
-def pair_body(own_ref, got_ref, out_ref):
-    _, _, c = place()
+def pair_body(own_ref, got_ref, _, out_ref):
+    c = place()[2]
     out_ref[0] = own_ref[c]
     out_ref[1] = got_ref[c]
+
+
+def flags_body(nz, rows, us_ref, co_ref, ck_ref, flags_ref):
+    row, z, c = place()
+    parents = [co_ref[CORES * row + k] // CH for k in (c, 1 - c)]
+    places = [CORES * (z ^ s) + (c if q == 0 else 1 - c) for s in range(nz) for q in range(CORES)]
+    flags = [us_ref[row, i] for i in places]
+    flags += [us_ref[parents[0], i] * ck_ref[c, i] for i in places]
+    for parent in parents:
+        flags += [jnp.where((parent ^ row) == s, 1, 0) for s in range(rows)]
+    for n, flag in enumerate(flags):
+        flags_ref[pl.ds(n, 1), :] = jnp.full((1, flags_ref.shape[1]), flag, jnp.int32).astype(F32)
 
 
 def order_body(u_own_ref, u_got_ref, l_own_ref, l_got_ref, d_ref, ub_ref, lb_ref, d_out_ref):
@@ -303,17 +310,24 @@
             compiler_params=pltpu.CompilerParams(vmem_limit_bytes=24 * 1024 * 1024),
         )(*args, *rest)
 
-    l_stack = kernel(pair_body, shape((CORES, size, size), BF), (l_all, l_got))
+    scalars = (upper_structure, child_order, child_keep)
+    flags = kernel(
+        functools.partial(flags_body, nz, rows),
+        shape((2 * CORES * nz + CORES * rows, size), F32),
+        scalars,
+        smem=3,
+    )
+    l_stack = kernel(
+        pair_body, shape((CORES, size, size), BF), (l_all, l_got), rest=(flags,)
+    )
     l_later = lax.optimization_barrier((l_stack, *u_far))[0]
     l_far = [over_z(l_later, s) for s in range(1, nz)]
-    scalars = (upper_structure, child_order, child_keep)
 
     def upper_part(_):
         rx, ud_part = kernel(
             functools.partial(upper_body, nz),
             (shape((CORES + 1, size, half), BF), shape((nz, quarter, half), BF)),
-            (upper_structure, t_own, t_sib, *[u for pair in u_all for u in pair]),
-            smem=1,
+            (flags, t_own, t_sib, *[u for pair in u_all for u in pair]),
             scratch=[
                 pltpu.VMEM((size, half), F32),
                 pltpu.VMEM((size, size), F32),
@@ -325,17 +339,15 @@
         for s in range(1, rows):
             rx_all.append(over_row(rx_all[s & (s - 1)], s & -s))
         keep, give = kernel(
-            functools.partial(pick_body, rows),
+            functools.partial(pick_body, nz, rows),
             (shape(rx.shape, BF), shape(rx.shape, BF)),
-            (child_order, *rx_all),
-            smem=1,
+            (flags, *rx_all),
         )
         got = over_core(give)
         w, rs1 = kernel(
             functools.partial(parent_body, nz),
             (shape((CORES, size, size), F32), shape((nz, quarter, size + half), BF)),
-            (*scalars, keep, got, parent_panels, l_stack, ud_part),
-            smem=3,
+            (flags, keep, got, parent_panels, l_stack, ud_part),
             scratch=[pltpu.VMEM((size, size), F32)],
         )
         return rx[:CORES], w, rs1
@@ -352,8 +364,7 @@
     lb_own, lb_give, sums = kernel(
         functools.partial(lower_body, nz),
         (shape((size, size), BF), shape((size, size), BF), shape((nz, quarter, 2 * size + half), BF)),
-        (*scalars, t_own, t_sib, w, rs1, l_stack, *l_far),
-        smem=3,
+        (flags, t_own, t_sib, w, rs1, l_stack, *l_far),
         scratch=[pltpu.VMEM((size, size), F32)],
     )
     lb_got = over_core(lb_give)

time: 67.8 us -> 67.5 us (level)
    ppermute x12, waiting for transfers between devices: 18.1 us -> 17.2 us  [over_z(): return lax.ppermute(x, 'pcol', [(i, i ^ CORES * s) for i in range(cols)])]
    pallas_call x9 -> x10, Pallas kernels: 8.59 us -> 8.23 us  [kernel(): pl.pallas_call(body, out_shape=out, in_specs=[sm] * smem + [vm] * (len(ar...]
    unnamed x20 -> x18, local copies, waits for them, and re-layouts: 1.56 us -> 1.63 us
where the time goes in v5:
time: 67.5 us; the launch traced here: 67.3 us
  waiting for transfers between devices  31.4 us (47%)
  starting transfers between devices  25.2 us (37%)
  Pallas kernels  8.23 us (12%)
  local copies, waits for them, and re-layouts  1.68 us (2%)
  between operations  0.78 us (1%)
    ppermute x12, starting transfers between devices, over_z(): return lax.ppermute(x, 'pcol', [(i, i ^ CORES * s) for i in range(cols)])  19.2 us
    ppermute x12, waiting for transfers between devices, over_z(): return lax.ppermute(x, 'pcol', [(i, i ^ CORES * s) for i in range(cols)])  17.2 us
    ppermute x3, waiting for transfers between devices, over_row(): return lax.ppermute(x, 'prow', [(i, i ^ s) for i in range(rows)])  8.55 us
    pallas_call x10, Pallas kernels, kernel(): pl.pallas_call(body, out_shape=out, in_specs=[sm] * smem + [vm] * (len(ar...  8.23 us
    ppermute x10, waiting for transfers between devices, over_core(): return lax.ppermute(x, 'pcol', [(i, i ^ 1) for i in range(cols)])  5.63 us
    ppermute x3, starting transfers between devices, over_row(): return lax.ppermute(x, 'prow', [(i, i ^ s) for i in range(rows)])  4.57 us
    unnamed x18, local copies, waits for them, and re-layouts  1.63 us
    ppermute x10, starting transfers between devices, over_core(): return lax.ppermute(x, 'pcol', [(i, i ^ 1) for i in range(cols)])  1.41 us
  transfers between devices with their start and end apart: 25, of which 12 were waited for; matrix products, arithmetic and copies ran while one was open for 0% of the time, Pallas kernels for 7%

profile of v5, /device:TPU:0, one launch (start us, length us, event | category | flops | bytes accessed | tf_op | source)
XLA Modules:
  0.0 67.3 jit_solution(5629214802773002230)
XLA Ops:
  1.3 5.0 %collective-permute-start.10 = (bf16[256,256]{1,0:T(8,128)(2,1)}, bf16[256,256]{1,0:T(8,128)(2,1)S(1)}, u32[]{:S(2)}, u32[]{:S(2)}) collective-permute-start(bf16[256,256]{1,0:T(8,128)(2,1)} %bitcast.20), channel_id=1, source_target_pairs={{0,6},{1,7},{2,4},{3,5},{4,2},{5,3},{6,0},{7,1},{8,14},{9,15},{10,... | collective-permute-start | bytes 393224 | tf_op jit(solution)/shard_map/ppermute | solution.py:282
  6.3 0.6 collective-permute-start.8
  6.8 4.0 %collective-permute-done.10 = bf16[256,256]{1,0:T(8,128)(2,1)S(1)} collective-permute-done((bf16[256,256]{1,0:T(8,128)(2,1)}, bf16[256,256]{1,0:T(8,128)(2,1)S(1)}, u32[]{:S(2)}, u32[]{:S(2)}) %collective-permute-start.10) | collective-permute-done | bytes 131104 | tf_op jit(solution)/shard_map/ppermute | solution.py:282
  10.8 3.3 %collective-permute-done.6 = bf16[256,256]{1,0:T(8,128)(2,1)S(1)} collective-permute-done((bf16[256,256]{1,0:T(8,128)(2,1)}, bf16[256,256]{1,0:T(8,128)(2,1)S(1)}, u32[]{:S(2)}, u32[]{:S(2)}) %collective-permute-start.6) | collective-permute-done | bytes 131104 | tf_op jit(solution)/shard_map/ppermute | solution.py:282
  14.2 0.7 shard_map.128._.flags_ref
  15.4 0.9 %copy-done.1 = bf16[2,1,256,256]{3,2,1,0:T(8,128)(2,1)S(1)} copy-done((bf16[2,1,256,256]{3,2,1,0:T(8,128)(2,1)S(1)}, bf16[2,1,256,256]{3,2,1,0:T(8,128)(2,1)}, u32[]{:S(2)}) %copy-start.1) | copy-done | bytes 262168
  16.4 1.4 %collective-permute-done.8 = bf16[256,256]{1,0:T(8,128)(2,1)S(1)} collective-permute-done((bf16[256,256]{1,0:T(8,128)(2,1)}, bf16[256,256]{1,0:T(8,128)(2,1)S(1)}, u32[]{:S(2)}, u32[]{:S(2)}) %collective-permute-start.8) | collective-permute-done | bytes 131104 | tf_op jit(solution)/shard_map/ppermute | solution.py:282
  18.0 2.8 %collective-permute-start.15 = (bf16[2,256,256]{2,1,0:T(8,128)(2,1)S(1)}, bf16[2,256,256]{2,1,0:T(8,128)(2,1)S(1)}, u32[]{:S(2)}, u32[]{:S(2)}) collective-permute-start(bf16[2,256,256]{2,1,0:T(8,128)(2,1)S(1)} %shard_map.129.refs_0_), channel_id=1, source_target_pairs={{0,4},{1,5},{2,6},{3,7},{4,0},{5,1},{6,2},{7,3},{8,12},{9,13},{10,... | collective-permute-start | bytes 786440 | tf_op jit(solution)/shard_map/ppermute | solution.py:282
  20.9 1.3 %collective-permute-start.16 = (bf16[2,256,256]{2,1,0:T(8,128)(2,1)S(1)}, bf16[2,256,256]{2,1,0:T(8,128)(2,1)S(1)}, u32[]{:S(2)}, u32[]{:S(2)}) collective-permute-start(bf16[2,256,256]{2,1,0:T(8,128)(2,1)S(1)} %shard_map.129.refs_0_), channel_id=1, source_target_pairs={{0,6},{1,7},{2,4},{3,5},{4,2},{5,3},{6,0},{7,1},{8,14},{9,15},{10,... | collective-permute-start | bytes 786440 | tf_op jit(solution)/shard_map/ppermute | solution.py:282
  22.2 0.7 copy-done.8
  22.9 1.3 %collective-permute-done.9 = bf16[256,256]{1,0:T(8,128)(2,1)S(1)} collective-permute-done((bf16[256,256]{1,0:T(8,128)(2,1)S(1)}, bf16[256,256]{1,0:T(8,128)(2,1)S(1)}, u32[]{:S(2)}, u32[]{:S(2)}) %collective-permute-start.9) | collective-permute-done | bytes 131104 | tf_op jit(solution)/shard_map/ppermute | solution.py:279
  24.2 17.8 %conditional.1 = (bf16[2,256,128]{2,1,0:T(8,128)(2,1)S(1)}, f32[2,256,256]{2,1,0:T(8,128)S(1)}, bf16[4,64,384]{2,1,0:T(8,128)(2,1)S(1)}) conditional(s32[]{:T(128)} %convert_element_type.3, () %tuple.17, (f32[1,256,256]{2,1,0:T(8,128)S(1)}, f32[24,256]{1,0:T(8,128)S(1)}, bf16[8,256,256]{2,1,0:T(8,128)(2,1)}, bf16[8,256,256]{2,1,0:T(8,128)(2,1)S(1)}, ...), branch_computations={%region_0.0_spmd, %region_1.0_spmd} | conditional | bytes 3408056 | solution.py:362
  24.2 2.5 %branch_1_fun.3 = (bf16[3,256,128]{2,1,0:T(8,128)(2,1)S(1)}, bf16[4,64,128]{2,1,0:T(8,128)(2,1)S(1)}) custom-call(f32[24,256]{1,0:T(8,128)S(1)} %get-tuple-element.29.flags_ref, bf16[8,256,256]{2,1,0:T(8,128)(2,1)} %get-tuple-element.30.to_ref, bf16[8,256,256]{2,1,0:T(8,128)(2,1)S(1)} %get-tuple-element.31.ts_ref, ...), custom_call_target="tpu_custom_call" | custom-call | tf_op jit(solution)/shard_map/cond/branch_1_fun/pallas_call | solution.py:304
  26.7 1.6 %collective-permute-start.1 = (bf16[3,256,128]{2,1,0:T(8,128)(2,1)S(1)}, bf16[3,256,128]{2,1,0:T(8,128)(2,1)S(1)}, u32[]{:S(2)}, u32[]{:S(2)}) collective-permute-start(bf16[3,256,128]{2,1,0:T(8,128)(2,1)S(1)} %get-tuple-element.41.refs_0_), channel_id=1, source_target_pairs={{0,16},{8,24},{16,0},{24,8},{1,17},{9,25},{17,1},{25,9},{2,18},{10... | collective-permute-start | bytes 589832 | tf_op jit(solution)/shard_map/cond/branch_1_fun/ppermute | solution.py:285
  28.3 1.5 %collective-permute-start = (bf16[3,256,128]{2,1,0:T(8,128)(2,1)S(1)}, bf16[3,256,128]{2,1,0:T(8,128)(2,1)S(1)}, u32[]{:S(2)}, u32[]{:S(2)}) collective-permute-start(bf16[3,256,128]{2,1,0:T(8,128)(2,1)S(1)} %get-tuple-element.41.refs_0_), channel_id=1, source_target_pairs={{0,8},{8,0},{16,24},{24,16},{1,9},{9,1},{17,25},{25,17},{2,10},{10... | collective-permute-start | bytes 589832 | tf_op jit(solution)/shard_map/cond/branch_1_fun/ppermute | solution.py:285
  29.8 3.9 %collective-permute-done.1.refs_2_ = bf16[3,256,128]{2,1,0:T(8,128)(2,1)S(1)} collective-permute-done((bf16[3,256,128]{2,1,0:T(8,128)(2,1)S(1)}, bf16[3,256,128]{2,1,0:T(8,128)(2,1)S(1)}, u32[]{:S(2)}, u32[]{:S(2)}) %collective-permute-start.1) | collective-permute-done | bytes 196640 | tf_op jit(solution)/shard_map/cond/branch_1_fun/ppermute | solution.py:285
  33.7 1.5 %collective-permute-start.2 = (bf16[3,256,128]{2,1,0:T(8,128)(2,1)S(1)}, bf16[3,256,128]{2,1,0:T(8,128)(2,1)S(1)}, u32[]{:S(2)}, u32[]{:S(2)}) collective-permute-start(bf16[3,256,128]{2,1,0:T(8,128)(2,1)S(1)} %collective-permute-done.1.refs_2_), channel_id=1, source_target_pairs={{0,8},{8,0},{16,24},{24,16},{1,9},{9,1},{17,25},{25,17},{2,10},{10... | collective-permute-start | bytes 589832 | tf_op jit(solution)/shard_map/cond/branch_1_fun/ppermute | solution.py:285
  35.2 4.6 %collective-permute-done.2.refs_3_ = bf16[3,256,128]{2,1,0:T(8,128)(2,1)S(1)} collective-permute-done((bf16[3,256,128]{2,1,0:T(8,128)(2,1)S(1)}, bf16[3,256,128]{2,1,0:T(8,128)(2,1)S(1)}, u32[]{:S(2)}, u32[]{:S(2)}) %collective-permute-start.2) | collective-permute-done | bytes 196640 | tf_op jit(solution)/shard_map/cond/branch_1_fun/ppermute | solution.py:285
  40.2 1.4 %collective-permute-done.3.got_ref = bf16[3,256,128]{2,1,0:T(8,128)(2,1)S(1)} collective-permute-done((bf16[3,256,128]{2,1,0:T(8,128)(2,1)S(1)}, bf16[3,256,128]{2,1,0:T(8,128)(2,1)S(1)}, u32[]{:S(2)}, u32[]{:S(2)}) %collective-permute-start.3) | collective-permute-done | bytes 196640 | tf_op jit(solution)/shard_map/cond/branch_1_fun/ppermute | solution.py:279
  42.1 2.3 %shard_map.130 = (bf16[256,256]{1,0:T(8,128)(2,1)S(1)}, bf16[256,256]{1,0:T(8,128)(2,1)S(1)}, bf16[4,64,640]{2,1,0:T(8,128)(2,1)S(1)}) custom-call(f32[24,256]{1,0:T(8,128)S(1)} %shard_map.128._.flags_ref, bf16[8,256,256]{2,1,0:T(8,128)(2,1)} %bitcast.18, bf16[8,256,256]{2,1,0:T(8,128)(2,1)S(1)} %collective-permute-done.4.ts_ref, ...), custom_call_target="tpu_custom_call" | custom-call | tf_op jit(solution)/shard_map/pallas_call | solution.py:304
  44.4 2.3 %collective-permute-start.18 = (bf16[64,640]{1,0:T(8,128)(2,1)S(1)}, bf16[64,640]{1,0:T(8,128)(2,1)S(1)}, u32[]{:S(2)}, u32[]{:S(2)}) collective-permute-start(bf16[64,640]{1,0:T(8,128)(2,1)S(1)} %get-tuple-element.82), channel_id=1, source_target_pairs={{0,2},{1,3},{2,0},{3,1},{4,6},{5,7},{6,4},{7,5},{8,10},{9,11},{10,... | collective-permute-start | bytes 245768 | tf_op jit(solution)/shard_map/ppermute | solution.py:282
  46.8 0.8 %collective-permute-start.19 = (bf16[64,640]{1,0:T(8,128)(2,1)S(1)}, bf16[64,640]{1,0:T(8,128)(2,1)S(1)}, u32[]{:S(2)}, u32[]{:S(2)}) collective-permute-start(bf16[64,640]{1,0:T(8,128)(2,1)S(1)} %get-tuple-element.81), channel_id=1, source_target_pairs={{0,4},{1,5},{2,6},{3,7},{4,0},{5,1},{6,2},{7,3},{8,12},{9,13},{10,... | collective-permute-start | bytes 245768 | tf_op jit(solution)/shard_map/ppermute | solution.py:282
  47.6 1.7 %collective-permute-start.20 = (bf16[64,640]{1,0:T(8,128)(2,1)S(1)}, bf16[64,640]{1,0:T(8,128)(2,1)S(1)}, u32[]{:S(2)}, u32[]{:S(2)}) collective-permute-start(bf16[64,640]{1,0:T(8,128)(2,1)S(1)} %get-tuple-element.80), channel_id=1, source_target_pairs={{0,6},{1,7},{2,4},{3,5},{4,2},{5,3},{6,0},{7,1},{8,14},{9,15},{10,... | collective-permute-start | bytes 245768 | tf_op jit(solution)/shard_map/ppermute | solution.py:282
  49.7 5.3 %collective-permute-done.19.refs_1_ = bf16[64,640]{1,0:T(8,128)(2,1)S(1)} collective-permute-done((bf16[64,640]{1,0:T(8,128)(2,1)S(1)}, bf16[64,640]{1,0:T(8,128)(2,1)S(1)}, u32[]{:S(2)}, u32[]{:S(2)}) %collective-permute-start.19) | collective-permute-done | bytes 81952 | tf_op jit(solution)/shard_map/ppermute | solution.py:282
  55.1 1.5 %collective-permute-start.21 = (bf16[64,640]{1,0:T(8,128)(2,1)S(1)}, bf16[64,640]{1,0:T(8,128)(2,1)S(1)}, u32[]{:S(2)}, u32[]{:S(2)}) collective-permute-start(bf16[64,640]{1,0:T(8,128)(2,1)S(1)} %shard_map.132.refs_0_), channel_id=1, source_target_pairs={{0,2},{1,3},{2,0},{3,1},{4,6},{5,7},{6,4},{7,5},{8,10},{9,11},{10,... | collective-permute-start | bytes 245768 | tf_op jit(solution)/shard_map/ppermute | solution.py:282
  56.6 0.9 %collective-permute-start.22 = (bf16[64,640]{1,0:T(8,128)(2,1)S(1)}, bf16[64,640]{1,0:T(8,128)(2,1)S(1)}, u32[]{:S(2)}, u32[]{:S(2)}) collective-permute-start(bf16[64,640]{1,0:T(8,128)(2,1)S(1)} %shard_map.132.refs_0_), channel_id=1, source_target_pairs={{0,4},{1,5},{2,6},{3,7},{4,0},{5,1},{6,2},{7,3},{8,12},{9,13},{10,... | collective-permute-start | bytes 245768 | tf_op jit(solution)/shard_map/ppermute | solution.py:282
  57.5 2.0 %collective-permute-start.23 = (bf16[64,640]{1,0:T(8,128)(2,1)S(1)}, bf16[64,640]{1,0:T(8,128)(2,1)S(1)}, u32[]{:S(2)}, u32[]{:S(2)}) collective-permute-start(bf16[64,640]{1,0:T(8,128)(2,1)S(1)} %shard_map.132.refs_0_), channel_id=1, source_target_pairs={{0,6},{1,7},{2,4},{3,5},{4,2},{5,3},{6,0},{7,1},{8,14},{9,15},{10,... | collective-permute-start | bytes 245768 | tf_op jit(solution)/shard_map/ppermute | solution.py:282
  59.6 1.2 %collective-permute-done.13.u_got_ref = bf16[256,128]{1,0:T(8,128)(2,1)S(1)} collective-permute-done((bf16[256,128]{1,0:T(8,128)(2,1)S(1)}, bf16[256,128]{1,0:T(8,128)(2,1)S(1)}, u32[]{:S(2)}, u32[]{:S(2)}) %collective-permute-start.13) | collective-permute-done | bytes 65568 | tf_op jit(solution)/shard_map/ppermute | solution.py:279
  60.9 0.8 %shard_map.131 = (bf16[1,1,256,256]{3,2,1,0:T(8,128)(2,1)}, bf16[2,1,256,256]{3,2,1,0:T(8,128)(2,1)}, f32[2,256,256]{2,1,0:T(8,128)S(1)}) custom-call(bf16[256,128]{1,0:T(8,128)(2,1)S(1)} %get-tuple-element.84.u_own_ref, bf16[256,128]{1,0:T(8,128)(2,1)S(1)} %collective-permute-done.13.u_got_ref, bf16[256,256]{1,0:T(8,128)(2,1)S(1)} %get-tuple-element.71.l_own_ref, ...), custom_call_target="tpu_custom_call" | custom-call | tf_op jit(solution)/shard_map/pallas_call | solution.py:304
  61.7 2.7 %collective-permute-done.22.refs_2_ = bf16[64,640]{1,0:T(8,128)(2,1)S(1)} collective-permute-done((bf16[64,640]{1,0:T(8,128)(2,1)S(1)}, bf16[64,640]{1,0:T(8,128)(2,1)S(1)}, u32[]{:S(2)}, u32[]{:S(2)}) %collective-permute-start.22) | collective-permute-done | bytes 81952 | tf_op jit(solution)/shard_map/ppermute | solution.py:282
  64.5 1.6 %collective-permute-done.24.got_ref = bf16[256,640]{1,0:T(8,128)(2,1)S(1)} collective-permute-done((bf16[256,640]{1,0:T(8,128)(2,1)S(1)}, bf16[256,640]{1,0:T(8,128)(2,1)S(1)}, u32[]{:S(2)}, u32[]{:S(2)}) %collective-permute-start.24) | collective-permute-done | bytes 327712 | tf_op jit(solution)/shard_map/ppermute | solution.py:279
  66.1 1.2 %shard_map.134 = (f32[1,256,256]{2,1,0:T(8,128)}, bf16[2,256,256]{2,1,0:T(8,128)(2,1)}, f32[2,256,256]{2,1,0:T(8,128)}) custom-call(bf16[256,640]{1,0:T(8,128)(2,1)S(1)} %shard_map.133.own_ref, bf16[256,640]{1,0:T(8,128)(2,1)S(1)} %collective-permute-done.24.got_ref, f32[1,256,256]{2,1,0:T(8,128)S(1)} %copy-done.6, bf16[2,256,256]{2,1,0:T(8,128)(2,1)S(1)} %copy-done.5, ...), custom_call_target="tpu_custom_call" | custom-call | tf_op jit(solution)/shard_map/pallas_call | solution.py:304
  (50 shorter events, 3.0 us)
Async XLA Ops:
  0.6 13.5 %copy-start.2 = (s32[4,8]{1,0:T(4,128)S(1)}, s32[4,8]{1,0:T(4,128)}, u32[]{:S(2)}) copy-start(s32[4,8]{1,0:T(4,128)} %us_ref.1) | copy-start | bytes 388
  0.6 23.6 %collective-permute-start.4 = (bf16[8,256,256]{2,1,0:T(8,128)(2,1)}, bf16[8,256,256]{2,1,0:T(8,128)(2,1)S(1)}, u32[]{:S(2)}, u32[]{:S(2)}) collective-permute-start(bf16[8,256,256]{2,1,0:T(8,128)(2,1)} %bitcast.16), channel_id=1, source_target_pairs={{0,1},{1,0},{2,3},{3,2},{4,5},{5,4},{6,7},{7,6},{8,9},{9,8},{10,11... | collective-permute-start | bytes 3145736 | tf_op jit(solution)/shard_map/ppermute | solution.py:279
  1.2 13.0 %copy-start.3 = (s32[2,8]{1,0:T(2,128)S(1)}, s32[2,8]{1,0:T(2,128)}, u32[]{:S(2)}) copy-start(s32[2,8]{1,0:T(2,128)} %ck_ref.1) | copy-start | bytes 196
  1.2 13.0 %copy-start.4 = (s32[8]{0:T(128)S(1)}, s32[8]{0:T(128)}, u32[]{:S(2)}) copy-start(s32[8]{0:T(128)} %co_ref.1) | copy-start | bytes 100
  1.2 13.7 %collective-permute-start.12 = (bf16[2,256,256]{2,1,0:T(8,128)(2,1)}, bf16[2,256,256]{2,1,0:T(8,128)(2,1)S(1)}, u32[]{:S(2)}, u32[]{:S(2)}) collective-permute-start(bf16[2,256,256]{2,1,0:T(8,128)(2,1)} %bitcast.14), channel_id=1, source_target_pairs={{0,1},{1,0},{2,3},{3,2},{4,5},{5,4},{6,7},{7,6},{8,9},{9,8},{10,11... | collective-permute-start | bytes 786440 | tf_op jit(solution)/shard_map/ppermute | solution.py:279
  1.3 9.6 %collective-permute-start.10 = (bf16[256,256]{1,0:T(8,128)(2,1)}, bf16[256,256]{1,0:T(8,128)(2,1)S(1)}, u32[]{:S(2)}, u32[]{:S(2)}) collective-permute-start(bf16[256,256]{1,0:T(8,128)(2,1)} %bitcast.20), channel_id=1, source_target_pairs={{0,6},{1,7},{2,4},{3,5},{4,2},{5,3},{6,0},{7,1},{8,14},{9,15},{10,... | collective-permute-start | bytes 393224 | tf_op jit(solution)/shard_map/ppermute | solution.py:282
  6.3 7.9 %collective-permute-start.6 = (bf16[256,256]{1,0:T(8,128)(2,1)}, bf16[256,256]{1,0:T(8,128)(2,1)S(1)}, u32[]{:S(2)}, u32[]{:S(2)}) collective-permute-start(bf16[256,256]{1,0:T(8,128)(2,1)} %bitcast.21), channel_id=1, source_target_pairs={{0,2},{1,3},{2,0},{3,1},{4,6},{5,7},{6,4},{7,5},{8,10},{9,11},{10,... | collective-permute-start | bytes 393224 | tf_op jit(solution)/shard_map/ppermute | solution.py:282
  6.3 11.5 %collective-permute-start.8 = (bf16[256,256]{1,0:T(8,128)(2,1)}, bf16[256,256]{1,0:T(8,128)(2,1)S(1)}, u32[]{:S(2)}, u32[]{:S(2)}) collective-permute-start(bf16[256,256]{1,0:T(8,128)(2,1)} %bitcast.22), channel_id=1, source_target_pairs={{0,4},{1,5},{2,6},{3,7},{4,0},{5,1},{6,2},{7,3},{8,12},{9,13},{10,... | collective-permute-start | bytes 393224 | tf_op jit(solution)/shard_map/ppermute | solution.py:282
  10.8 5.6 %copy-start.7 = (bf16[256,256]{1,0:T(8,128)(2,1)}, bf16[256,256]{1,0:T(8,128)(2,1)S(1)}, u32[]{:S(2)}) copy-start(bf16[256,256]{1,0:T(8,128)(2,1)S(1)} %collective-permute-done.10) | copy-start | bytes 393220
  10.8 7.2 %collective-permute-start.5 = (bf16[256,256]{1,0:T(8,128)(2,1)}, bf16[256,256]{1,0:T(8,128)(2,1)}, u32[]{:S(2)}, u32[]{:S(2)}) collective-permute-start(bf16[256,256]{1,0:T(8,128)(2,1)} %bitcast.23), channel_id=1, source_target_pairs={{0,1},{1,0},{2,3},{3,2},{4,5},{5,4},{6,7},{7,6},{8,9},{9,8},{10,11... | collective-permute-start | bytes 393224 | tf_op jit(solution)/shard_map/ppermute | solution.py:279
  14.1 6.7 %collective-permute-start.11 = (bf16[256,256]{1,0:T(8,128)(2,1)S(1)}, bf16[256,256]{1,0:T(8,128)(2,1)}, u32[]{:S(2)}, u32[]{:S(2)}) collective-permute-start(bf16[256,256]{1,0:T(8,128)(2,1)S(1)} %collective-permute-done.10), channel_id=1, source_target_pairs={{0,1},{1,0},{2,3},{3,2},{4,5},{5,4},{6,7},{7,6},{8,9},{9,8},{10,11... | collective-permute-start | bytes 393224 | tf_op jit(solution)/shard_map/ppermute | solution.py:279
  14.8 7.4 %collective-permute-start.7 = (bf16[256,256]{1,0:T(8,128)(2,1)S(1)}, bf16[256,256]{1,0:T(8,128)(2,1)S(1)}, u32[]{:S(2)}, u32[]{:S(2)}) collective-permute-start(bf16[256,256]{1,0:T(8,128)(2,1)S(1)} %collective-permute-done.6), channel_id=1, source_target_pairs={{0,1},{1,0},{2,3},{3,2},{4,5},{5,4},{6,7},{7,6},{8,9},{9,8},{10,11... | collective-permute-start | bytes 393224 | tf_op jit(solution)/shard_map/ppermute | solution.py:279
  16.4 7.9 %copy-start.5 = (bf16[2,256,256]{2,1,0:T(8,128)(2,1)S(1)}, bf16[2,256,256]{2,1,0:T(8,128)(2,1)}, u32[]{:S(2)}) copy-start(bf16[2,256,256]{2,1,0:T(8,128)(2,1)} %pp_ref.1) | copy-start | bytes 786436
  16.4 7.9 %copy-start.6 = (f32[1,256,256]{2,1,0:T(8,128)S(1)}, f32[1,256,256]{2,1,0:T(8,128)}, u32[]{:S(2)}) copy-start(f32[1,256,256]{2,1,0:T(8,128)} %d_ref.3) | copy-start | bytes 786436
  17.8 24.2 %collective-permute-start.14 = (bf16[2,256,256]{2,1,0:T(8,128)(2,1)S(1)}, bf16[2,256,256]{2,1,0:T(8,128)(2,1)S(1)}, u32[]{:S(2)}, u32[]{:S(2)}) collective-permute-start(bf16[2,256,256]{2,1,0:T(8,128)(2,1)S(1)} %shard_map.129.refs_0_), channel_id=1, source_target_pairs={{0,2},{1,3},{2,0},{3,1},{4,6},{5,7},{6,4},{7,5},{8,10},{9,11},{10,... | collective-permute-start | bytes 786440 | tf_op jit(solution)/shard_map/ppermute | solution.py:282
  18.0 24.0 %collective-permute-start.15 = (bf16[2,256,256]{2,1,0:T(8,128)(2,1)S(1)}, bf16[2,256,256]{2,1,0:T(8,128)(2,1)S(1)}, u32[]{:S(2)}, u32[]{:S(2)}) collective-permute-start(bf16[2,256,256]{2,1,0:T(8,128)(2,1)S(1)} %shard_map.129.refs_0_), channel_id=1, source_target_pairs={{0,4},{1,5},{2,6},{3,7},{4,0},{5,1},{6,2},{7,3},{8,12},{9,13},{10,... | collective-permute-start | bytes 786440 | tf_op jit(solution)/shard_map/ppermute | solution.py:282
  20.9 21.2 %collective-permute-start.16 = (bf16[2,256,256]{2,1,0:T(8,128)(2,1)S(1)}, bf16[2,256,256]{2,1,0:T(8,128)(2,1)S(1)}, u32[]{:S(2)}, u32[]{:S(2)}) collective-permute-start(bf16[2,256,256]{2,1,0:T(8,128)(2,1)S(1)} %shard_map.129.refs_0_), channel_id=1, source_target_pairs={{0,6},{1,7},{2,4},{3,5},{4,2},{5,3},{6,0},{7,1},{8,14},{9,15},{10,... | collective-permute-start | bytes 786440 | tf_op jit(solution)/shard_map/ppermute | solution.py:282
  22.9 1.3 %collective-permute-start.9 = (bf16[256,256]{1,0:T(8,128)(2,1)S(1)}, bf16[256,256]{1,0:T(8,128)(2,1)S(1)}, u32[]{:S(2)}, u32[]{:S(2)}) collective-permute-start(bf16[256,256]{1,0:T(8,128)(2,1)S(1)} %collective-permute-done.8), channel_id=1, source_target_pairs={{0,1},{1,0},{2,3},{3,2},{4,5},{5,4},{6,7},{7,6},{8,9},{9,8},{10,11... | collective-permute-start | bytes 393224 | tf_op jit(solution)/shard_map/ppermute | solution.py:279
  26.7 7.0 %collective-permute-start.1 = (bf16[3,256,128]{2,1,0:T(8,128)(2,1)S(1)}, bf16[3,256,128]{2,1,0:T(8,128)(2,1)S(1)}, u32[]{:S(2)}, u32[]{:S(2)}) collective-permute-start(bf16[3,256,128]{2,1,0:T(8,128)(2,1)S(1)} %get-tuple-element.41.refs_0_), channel_id=1, source_target_pairs={{0,16},{8,24},{16,0},{24,8},{1,17},{9,25},{17,1},{25,9},{2,18},{10... | collective-permute-start | bytes 589832 | tf_op jit(solution)/shard_map/cond/branch_1_fun/ppermute | solution.py:285
  28.3 6.9 %collective-permute-start = (bf16[3,256,128]{2,1,0:T(8,128)(2,1)S(1)}, bf16[3,256,128]{2,1,0:T(8,128)(2,1)S(1)}, u32[]{:S(2)}, u32[]{:S(2)}) collective-permute-start(bf16[3,256,128]{2,1,0:T(8,128)(2,1)S(1)} %get-tuple-element.41.refs_0_), channel_id=1, source_target_pairs={{0,8},{8,0},{16,24},{24,16},{1,9},{9,1},{17,25},{25,17},{2,10},{10... | collective-permute-start | bytes 589832 | tf_op jit(solution)/shard_map/cond/branch_1_fun/ppermute | solution.py:285
  33.7 6.1 %collective-permute-start.2 = (bf16[3,256,128]{2,1,0:T(8,128)(2,1)S(1)}, bf16[3,256,128]{2,1,0:T(8,128)(2,1)S(1)}, u32[]{:S(2)}, u32[]{:S(2)}) collective-permute-start(bf16[3,256,128]{2,1,0:T(8,128)(2,1)S(1)} %collective-permute-done.1.refs_2_), channel_id=1, source_target_pairs={{0,8},{8,0},{16,24},{24,16},{1,9},{9,1},{17,25},{25,17},{2,10},{10... | collective-permute-start | bytes 589832 | tf_op jit(solution)/shard_map/cond/branch_1_fun/ppermute | solution.py:285
  40.1 1.5 %collective-permute-start.3 = (bf16[3,256,128]{2,1,0:T(8,128)(2,1)S(1)}, bf16[3,256,128]{2,1,0:T(8,128)(2,1)S(1)}, u32[]{:S(2)}, u32[]{:S(2)}) collective-permute-start(bf16[3,256,128]{2,1,0:T(8,128)(2,1)S(1)} %get-tuple-element.43), channel_id=1, source_target_pairs={{0,1},{1,0},{2,3},{3,2},{4,5},{5,4},{6,7},{7,6},{8,9},{9,8},{10,11... | collective-permute-start | bytes 589832 | tf_op jit(solution)/shard_map/cond/branch_1_fun/ppermute | solution.py:279
  44.4 16.4 %copy-start = (f32[2,256,256]{2,1,0:T(8,128)S(1)}, f32[2,256,256]{2,1,0:T(8,128)}, u32[]{:S(2)}) copy-start(f32[2,256,256]{2,1,0:T(8,128)} %d_ref.2) | copy-start | bytes 1572868
  44.4 5.3 %collective-permute-start.18 = (bf16[64,640]{1,0:T(8,128)(2,1)S(1)}, bf16[64,640]{1,0:T(8,128)(2,1)S(1)}, u32[]{:S(2)}, u32[]{:S(2)}) collective-permute-start(bf16[64,640]{1,0:T(8,128)(2,1)S(1)} %get-tuple-element.82), channel_id=1, source_target_pairs={{0,2},{1,3},{2,0},{3,1},{4,6},{5,7},{6,4},{7,5},{8,10},{9,11},{10,... | collective-permute-start | bytes 245768 | tf_op jit(solution)/shard_map/ppermute | solution.py:282
  46.8 8.3 %collective-permute-start.19 = (bf16[64,640]{1,0:T(8,128)(2,1)S(1)}, bf16[64,640]{1,0:T(8,128)(2,1)S(1)}, u32[]{:S(2)}, u32[]{:S(2)}) collective-permute-start(bf16[64,640]{1,0:T(8,128)(2,1)S(1)} %get-tuple-element.81), channel_id=1, source_target_pairs={{0,4},{1,5},{2,6},{3,7},{4,0},{5,1},{6,2},{7,3},{8,12},{9,13},{10,... | collective-permute-start | bytes 245768 | tf_op jit(solution)/shard_map/ppermute | solution.py:282
  47.6 7.5 %collective-permute-start.20 = (bf16[64,640]{1,0:T(8,128)(2,1)S(1)}, bf16[64,640]{1,0:T(8,128)(2,1)S(1)}, u32[]{:S(2)}, u32[]{:S(2)}) collective-permute-start(bf16[64,640]{1,0:T(8,128)(2,1)S(1)} %get-tuple-element.80), channel_id=1, source_target_pairs={{0,6},{1,7},{2,4},{3,5},{4,2},{5,3},{6,0},{7,1},{8,14},{9,15},{10,... | collective-permute-start | bytes 245768 | tf_op jit(solution)/shard_map/ppermute | solution.py:282
  49.2 11.7 %collective-permute-start.17 = (bf16[256,256]{1,0:T(8,128)(2,1)S(1)}, bf16[256,256]{1,0:T(8,128)(2,1)S(1)}, u32[]{:S(2)}, u32[]{:S(2)}) collective-permute-start(bf16[256,256]{1,0:T(8,128)(2,1)S(1)} %get-tuple-element.72), channel_id=1, source_target_pairs={{0,1},{1,0},{2,3},{3,2},{4,5},{5,4},{6,7},{7,6},{8,9},{9,8},{10,11... | collective-permute-start | bytes 393224 | tf_op jit(solution)/shard_map/ppermute | solution.py:279
  55.1 6.6 %collective-permute-start.21 = (bf16[64,640]{1,0:T(8,128)(2,1)S(1)}, bf16[64,640]{1,0:T(8,128)(2,1)S(1)}, u32[]{:S(2)}, u32[]{:S(2)}) collective-permute-start(bf16[64,640]{1,0:T(8,128)(2,1)S(1)} %shard_map.132.refs_0_), channel_id=1, source_target_pairs={{0,2},{1,3},{2,0},{3,1},{4,6},{5,7},{6,4},{7,5},{8,10},{9,11},{10,... | collective-permute-start | bytes 245768 | tf_op jit(solution)/shard_map/ppermute | solution.py:282
  56.6 7.8 %collective-permute-start.22 = (bf16[64,640]{1,0:T(8,128)(2,1)S(1)}, bf16[64,640]{1,0:T(8,128)(2,1)S(1)}, u32[]{:S(2)}, u32[]{:S(2)}) collective-permute-start(bf16[64,640]{1,0:T(8,128)(2,1)S(1)} %shard_map.132.refs_0_), channel_id=1, source_target_pairs={{0,4},{1,5},{2,6},{3,7},{4,0},{5,1},{6,2},{7,3},{8,12},{9,13},{10,... | collective-permute-start | bytes 245768 | tf_op jit(solution)/shard_map/ppermute | solution.py:282
  57.5 6.9 %collective-permute-start.23 = (bf16[64,640]{1,0:T(8,128)(2,1)S(1)}, bf16[64,640]{1,0:T(8,128)(2,1)S(1)}, u32[]{:S(2)}, u32[]{:S(2)}) collective-permute-start(bf16[64,640]{1,0:T(8,128)(2,1)S(1)} %shard_map.132.refs_0_), channel_id=1, source_target_pairs={{0,6},{1,7},{2,4},{3,5},{4,2},{5,3},{6,0},{7,1},{8,14},{9,15},{10,... | collective-permute-start | bytes 245768 | tf_op jit(solution)/shard_map/ppermute | solution.py:282
  59.5 1.3 %collective-permute-start.13 = (bf16[256,128]{1,0:T(8,128)(2,1)S(1)}, bf16[256,128]{1,0:T(8,128)(2,1)S(1)}, u32[]{:S(2)}, u32[]{:S(2)}) collective-permute-start(bf16[256,128]{1,0:T(8,128)(2,1)S(1)} %get-tuple-element.83), channel_id=1, source_target_pairs={{0,1},{1,0},{2,3},{3,2},{4,5},{5,4},{6,7},{7,6},{8,9},{9,8},{10,11... | collective-permute-start | bytes 196616 | tf_op jit(solution)/shard_map/ppermute | solution.py:279
  64.4 1.7 %collective-permute-start.24 = (bf16[256,640]{1,0:T(8,128)(2,1)S(1)}, bf16[256,640]{1,0:T(8,128)(2,1)S(1)}, u32[]{:S(2)}, u32[]{:S(2)}) collective-permute-start(bf16[256,640]{1,0:T(8,128)(2,1)S(1)} %shard_map.133.own_ref), channel_id=1, source_target_pairs={{0,1},{1,0},{2,3},{3,2},{4,5},{5,4},{6,7},{7,6},{8,9},{9,8},{10,11... | collective-permute-start | bytes 983048 | tf_op jit(solution)/shard_map/ppermute | solution.py:279
  (2 other events, 1.6 us)
